TPU v7x, 32 devices: a whole 2x2x4 slice. The times are simulated.
32 devices in a mesh: grp: 2 (over x), layer: 16 (over z, y, core).
Axes of the slice: x: 2, y: 2, z: 4, core: 2. Of those that a mesh axis runs over, the one named last changes fastest.
Arguments:
- query_pool: bfloat16 [1024, 16, 4096], P('grp', 'layer'), parts along dimension 0, may hold values from -6 to 6
- train_store: bfloat16 [2048, 16, 4096], P('grp', 'layer'), parts along dimension 0, may hold values from -6 to 6
- query_ids: int32 [1024], P('grp'), parts along dimension 0, may hold values from 0 to 511
- train_ids: int32 [2048], P('grp'), parts along dimension 0, may hold values from 0 to 1023
- out_basis: bfloat16 [16, 64, 64], P('layer'), may hold values from -0.75 to 0.75
- in_basis: bfloat16 [16, 64, 64], P('layer'), may hold values from -0.75 to 0.75
- eigenvalues: float32 [16, 4096], P('layer'), may hold values from 0.05 to 100
Outputs:
- scores: float32 [1024, 1024], P('grp', 'layer'), parts along dimension 0
There are 2 independent parts, one for each index of `grp`. A program takes and returns all parts, laid end to end along the dimension named above; an argument that names none is the same for every part. Nothing has to cross between parts.
All inputs are finite; a program needn't handle non-finite values.
Results may differ from a plain program's by a relative error of at most 0.0042.
Values sent between devices are 32-bit elements; how exact they have to be, the bound alone decides.
No kernel may reach another device: no remote copies, remote signals or barrier semaphores. Data moves between devices by JAX's collectives and lax.ppermute only.
A program may use at most 128 MiB of HBM per device.

v0:
```python
import jax
import jax.numpy as jnp
from jax import lax
from jax.sharding import PartitionSpec as P


def rotate(feat, outer, inner):
    count = feat.shape[0]
    side = outer.shape[0]
    grads = feat.reshape(count, side, feat.shape[1] // side)
    half = jnp.einsum("roi,ij->roj", grads, inner, preferred_element_type=jnp.float32).astype(
        jnp.bfloat16
    )
    rotated = jnp.einsum("op,roj->rpj", outer, half, preferred_element_type=jnp.float32)
    return rotated.reshape(count, feat.shape[1])


def shards(query_pool, train_store, query_ids, train_ids, out_basis, in_basis, eigenvalues):
    devices = lax.axis_size("layer")
    eig_sum = lax.psum(jnp.sum(eigenvalues), "layer")
    damp = 0.1 * eig_sum / (eigenvalues.size * devices)
    queries_all = query_pool[query_ids]
    window_all = train_store[train_ids]
    total_rows = window_all.shape[0]
    module = 0
    denom = eigenvalues[module] + damp
    damped = (
        rotate(queries_all[:, module], out_basis[module], in_basis[module]) / denom[None, :]
    ).astype(jnp.bfloat16)
    rotated_train = rotate(window_all[:, module], out_basis[module], in_basis[module]).astype(
        jnp.bfloat16
    )
    wide = rotated_train.astype(jnp.float32)
    self_term = jnp.sum(wide * wide / denom[None, :], axis=1)
    damped_list = [damped]
    train_list = [rotated_train]
    columns = total_rows // devices
    module = 0
    partial_value = lax.dot_general(
        damped_list[module],
        train_list[module],
        (((1,), (1,)), ((), ())),
        preferred_element_type=jnp.float32,
    )
    total = lax.psum_scatter(partial_value, "layer", scatter_dimension=1, tiled=True)
    self_full = lax.psum(self_term, "layer")
    own_self = lax.dynamic_slice_in_dim(self_full, lax.axis_index("layer") * columns, columns, 0)
    return total * lax.rsqrt(own_self)[None, :]


def solution(mesh):
    placed = (
        P("grp", "layer", None),
        P("grp", "layer", None),
        P("grp"),
        P("grp"),
        P("layer", None, None),
        P("layer", None, None),
        P("layer", None),
    )
    return jax.shard_map(
        shards, mesh=mesh, in_specs=placed, out_specs=P("grp", "layer"), check_vma=False
    )
```

profile of v0, /device:TPU:0, one launch (start us, length us, event | category | flops | bytes accessed | tf_op | source)
XLA Modules:
  0.0 207.7 jit_solution(4005755123167166450)
XLA Ops:
  6.5 0.0 copy-start
  6.5 0.0 reduce-scatter.2.cloned.1.call-start
  6.5 1.4 reduce_sum.18
  7.9 35.5 %psum.14 = f32[]{:T(128)} all-reduce(f32[]{:T(128)} %reduce_sum.18), channel_id=1, replica_groups=mesh['grp'=2,'layer'=16] {'layer'}, use_global_device_ids=true, to_apply=%region_1.0 | all-reduce | flops 1 | bytes 8 | tf_op jit(solution)/shard_map/psum | solution.py:20
  44.1 0.8 add_reduce_fusion
  44.9 0.1 div.24
  44.9 0.1 copy.20
  45.0 0.7 fusion.29
  45.7 19.5 %gather_fusion.1 = bf16[1024,4096]{1,0:T(8,128)(2,1)} fusion(bf16[1024,4096]{1,0:T(8,128)(2,1)} %bitcast.40, s32[1024]{0:T(1024)S(1)} %fusion.29), kind=kCustom, calls=%fused_computation.1 | custom fusion | bytes 16781312 | tf_op jit(solution)/shard_map/gather | solution.py:23
  65.3 0.0 copy-start.2
  65.3 12.0 %copy.21 = bf16[1024,4096]{0,1:T(8,128)(2,1)} copy(bf16[1024,4096]{1,0:T(8,128)(2,1)} %gather_fusion.1) | data formatting | bytes 16777216 | tf_op jit(solution)/shard_map/gather | solution.py:23
  77.2 0.0 copy-done.2
  77.2 11.3 %gather_fusion = bf16[512,4096]{1,0:T(8,128)(2,1)} fusion(bf16[512,4096]{1,0:T(8,128)(2,1)} %bitcast.41, s32[1024]{0:T(1024)S(1)} %pad_clamp_fusion), kind=kCustom, calls=%fused_computation | custom fusion | bytes 8390656 | tf_op jit(solution)/shard_map/gather | solution.py:22
  88.6 6.5 %copy.16 = bf16[512,4096]{0,1:T(8,128)(2,1)} copy(bf16[512,4096]{1,0:T(8,128)(2,1)} %gather_fusion) | data formatting | bytes 8388608 | tf_op jit(solution)/shard_map/gather | solution.py:22
  95.1 0.0 copy-done
  95.1 0.0 copy-start.1
  95.1 6.3 %convolution_convert_fusion = bf16[1024,64,64]{0,2,1:T(8,128)(2,1)S(1)} fusion(bf16[1024,64,64]{0,2,1:T(8,128)(2,1)} %bitcast.42, bf16[1,64,64]{2,1,0:T(8,128)(2,1)S(1)} %copy-done), kind=kOutput, calls=%fused_computation.11 | convolution fusion | flops 541065216 | bytes 16785408 | tf_op jit(solution)/shard_map/roi,ij->roj/dot_general | solution.py:11
  101.4 0.0 copy-start.3
  101.4 0.0 copy-done.1
  101.4 3.3 %convolution_convert_fusion.1 = bf16[512,64,64]{0,2,1:T(8,128)(2,1)} fusion(bf16[512,64,64]{0,2,1:T(8,128)(2,1)S(1)} %bitcast.43, bf16[1,64,64]{2,1,0:T(8,128)(2,1)S(1)} %copy-done), kind=kOutput, calls=%fused_computation.15 | convolution fusion | flops 270532608 | bytes 8396800 | tf_op jit(solution)/shard_map/roi,ij->roj/dot_general | solution.py:11
  104.7 0.0 copy-done.3
  104.7 21.3 %fusion = (f32[1024]{0:T(1024)S(1)}, bf16[1024,64,64]{0,2,1:T(8,128)(2,1)}) fusion(f32[64,64]{0,1:T(8,128)S(1)} %copy.20, bf16[1,64,64]{2,1,0:T(8,128)(2,1)S(1)} %copy-done.3, bf16[1024,64,64]{0,2,1:T(8,128)(2,1)S(1)} %convolution_convert_fusion), kind=kOutput, calls=%fused_computation.3 | convolution fusion | flops 557841408 | bytes 16805888 | tf_op jit(solution)/shard_map/op,roj->rpj/dot_general | solution.py:14
  126.0 14.2 %fusion.17 = f32[512,1024]{0,1:T(8,128)} fusion(bf16[1024,64,64]{0,2,1:T(8,128)(2,1)} %get-tuple-element.6, f32[64,64]{0,1:T(8,128)S(1)} %copy.20, bf16[512,64,64]{0,2,1:T(8,128)(2,1)} %convolution_convert_fusion.1, bf16[1,64,64]{2,1,0:T(8,128)(2,1)S(1)} %copy-done.3), kind=kOutput, calls=%fused_computation.16 | convolution fusion | flops 4567597056 | bytes 14704640 | tf_op jit(solution)/shard_map/dot_general | solution.py:39
  140.2 0.0 reduce-scatter.2.cloned.1.call-update
  140.3 29.7 %psum.15 = f32[1024]{0:T(1024)S(1)} all-reduce(f32[1024]{0:T(1024)S(1)} %get-tuple-element.5), channel_id=1, replica_groups=mesh['grp'=2,'layer'=16] {'layer'}, use_global_device_ids=true, to_apply=%region_4.0 | all-reduce | flops 1024 | bytes 8192 | tf_op jit(solution)/shard_map/psum | solution.py:46
  170.0 0.1 dynamic-slice_rsqrt_fusion
  170.1 29.2 %reduce-scatter.2.cloned.1.call-done = f32[512,64]{0,1:T(8,128)} async-done(((f32[512,1024]{0,1:T(8,128)}), f32[512,64]{0,1:T(8,128)}) %reduce-scatter.2.cloned.1.call-update) | async-done | bytes 131088 | tf_op jit(solution)/shard_map/reduce_scatter | solution.py:45
  199.2 1.6 broadcast_multiply_fusion
  (2 shorter events, 0.0 us)
Async XLA Ops:
  6.5 88.6 %copy-start = (bf16[1,64,64]{2,1,0:T(8,128)(2,1)S(1)}, bf16[1,64,64]{2,1,0:T(8,128)(2,1)}, u32[]{:S(2)}) copy-start(bf16[1,64,64]{2,1,0:T(8,128)(2,1)} %param.12) | copy-start | bytes 24580
  6.5 192.7 %reduce-scatter.2.cloned.1.call-start = ((), (), s32[]{:S(2)}) async-start(), calls=%async_computation.1 | async-start | bytes 2228224 | tf_op jit(solution)/shard_map/reduce_scatter | solution.py:45
  65.3 12.0 %copy-start.2 = (s32[512]{0:T(512)S(1)}, s32[512]{0:T(512)}, u32[]{:S(2)}) copy-start(s32[512]{0:T(512)} %param.9) | copy-start | bytes 6148
  95.1 6.3 %copy-start.1 = (bf16[512,4096]{0,1:T(8,128)(2,1)S(1)}, bf16[512,4096]{0,1:T(8,128)(2,1)}, u32[]{:S(2)}) copy-start(bf16[512,4096]{0,1:T(8,128)(2,1)} %copy.16) | copy-start | bytes 12582916
  101.4 3.3 %copy-start.3 = (bf16[1,64,64]{2,1,0:T(8,128)(2,1)S(1)}, bf16[1,64,64]{2,1,0:T(8,128)(2,1)}, u32[]{:S(2)}) copy-start(bf16[1,64,64]{2,1,0:T(8,128)(2,1)} %param.11) | copy-start | bytes 24580
Sparse Core Ops, SparseCore 0:
  140.4 58.8 reduce-scatter.1
where the time goes:
time: 209 us; the launch traced here: 208 us
  blocking collectives  65.2 us (31%)
  local copies, waits for them, and re-layouts  49.6 us (24%)
  matrix products  45.1 us (22%)
  waiting for transfers between devices  29.2 us (14%)
  between operations  14.1 us (7%)
  other arithmetic  4.48 us (2%)
    psum x1, blocking collectives, shards(): eig_sum = lax.psum(jnp.sum(eigenvalues), 'layer')  35.5 us
    gather x2, local copies, waits for them, and re-layouts, shards(): window_all = train_store[train_ids]  31.5 us
    psum x1, blocking collectives, shards(): self_full = lax.psum(self_term, 'layer')  29.7 us
    reduce_scatter x1, waiting for transfers between devices, shards(): lax.psum_scatter(partial_value, 'layer', scatter_dimension=1, tiled=True)  29.2 us
    dot_general x1, matrix products, rotate(): jnp.einsum('op,roj->rpj', outer, half, preferred_element_type=jnp.float32)  21.3 us
    gather x2, local copies, waits for them, and re-layouts, shards(): queries_all = query_pool[query_ids]  17.8 us
    dot_general x1, matrix products, shards(): lax.dot_general(damped_list[module], train_list[module], (((1,), (1,)), (...  14.2 us
    dot_general x2, matrix products, rotate(): jnp.einsum('roi,ij->roj', grads, inner, preferred_element_type=jnp.float32)  9.56 us
  transfers between devices with their start and end apart: 1, of which 1 were waited for; matrix products, arithmetic and copies ran while one was open for 0% of the time, Pallas kernels for 0%

commit v1 on v0

v1 whole, which is shorter than its diff:
```python
import functools

import jax
import jax.numpy as jnp
from jax import lax
from jax.experimental import pallas as pl
from jax.experimental.pallas import tpu as pltpu
from jax.sharding import PartitionSpec as P

BF16 = jnp.bfloat16
F32 = jnp.float32
VMEM_LIMIT = 56 * 1024 * 1024
NN = (((1,), (0,)), ((), ()))
NT = (((1,), (1,)), ((), ()))


def dot(a, b, dims=NN):
    return lax.dot_general(a, b, dims, preferred_element_type=F32)


def iota(shape, dim):
    return lax.broadcasted_iota(jnp.int32, shape, dim)


def onehot(cond):
    return jnp.where(cond, 1.0, 0.0).astype(BF16)


def inner_weight(basis, side, pack):
    wide = side * pack
    rows = onehot(iota((wide, side), 0) // pack == iota((wide, side), 1))
    cols = onehot(iota((side, wide), 1) % side == iota((side, wide), 0))
    full = dot(dot(rows, basis, NT).astype(BF16), cols)
    keep = iota((wide, wide), 0) % pack == iota((wide, wide), 1) // side
    return jnp.where(keep, full, 0.0).astype(BF16)


def outer_weight(basis, side, pack):
    wide = side * pack
    rows = onehot(iota((wide, side), 0) % side == iota((wide, side), 1))
    k = iota((side, wide), 1)
    cols = onehot(k // (pack * pack) * pack + k % pack == iota((side, wide), 0))
    full = dot(dot(rows, basis, NT).astype(BF16), cols)
    keep = iota((wide, wide), 0) // side == iota((wide, wide), 1) // pack % pack
    return jnp.where(keep, full, 0.0).astype(BF16)


def outer_weight_t(basis, side, pack):
    wide = side * pack
    k = iota((wide, side), 0)
    rows = onehot(k // (pack * pack) * pack + k % pack == iota((wide, side), 1))
    cols = onehot(iota((side, wide), 1) % side == iota((side, wide), 0))
    full = dot(dot(rows, basis).astype(BF16), cols)
    keep = iota((wide, wide), 1) // side == iota((wide, wide), 0) // pack % pack
    return jnp.where(keep, full, 0.0).astype(BF16)


def halves(x_ref, weight, half_ref, side, pack):
    wide = side * pack
    groups = side // pack
    unit = pack * pack
    for g in range(groups):
        part = dot(weight, x_ref[:, g * wide : (g + 1) * wide], NT).astype(BF16)
        half_ref[:, g * unit : (g + 1) * unit, :] = part.reshape(groups, unit, part.shape[1])


def train_kernel(side, pack, x_ref, inner_ref, outer_ref, out_ref, half_ref, w3_ref, w4_ref):
    @pl.when(pl.program_id(0) == 0)
    def _():
        w3_ref[...] = inner_weight(inner_ref[...], side, pack)
        w4_ref[...] = outer_weight(outer_ref[...], side, pack)

    halves(x_ref, w3_ref[...], half_ref, side, pack)
    w4 = w4_ref[...]
    for g in range(side // pack):
        out_ref[g] = dot(w4, half_ref[g]).astype(BF16)


def query_kernel(side, pack, x_ref, inner_ref, out_ref, half_ref, w3_ref):
    @pl.when(pl.program_id(0) == 0)
    def _():
        w3_ref[...] = inner_weight(inner_ref[...], side, pack)

    halves(x_ref, w3_ref[...], half_ref, side, pack)
    for g in range(side // pack):
        out_ref[g] = half_ref[g].T


def rotate_train(x, inner, outer, block=256):
    rows, feat = x.shape
    side = inner.shape[0]
    pack = 256 // side
    groups, wide = side // pack, side * pack
    return pl.pallas_call(
        functools.partial(train_kernel, side, pack),
        out_shape=jax.ShapeDtypeStruct((groups, wide, rows), BF16),
        grid=(rows // block,),
        in_specs=[
            pl.BlockSpec((block, feat), lambda i: (i, 0)),
            pl.BlockSpec((side, side), lambda i: (0, 0)),
            pl.BlockSpec((side, side), lambda i: (0, 0)),
        ],
        out_specs=pl.BlockSpec((groups, wide, block), lambda i: (0, 0, i)),
        scratch_shapes=[
            pltpu.VMEM((groups, wide, block), BF16),
            pltpu.VMEM((wide, wide), BF16),
            pltpu.VMEM((wide, wide), BF16),
        ],
        compiler_params=pltpu.CompilerParams(vmem_limit_bytes=VMEM_LIMIT),
        cost_estimate=pl.CostEstimate(
            flops=4 * rows * feat * wide, bytes_accessed=4 * rows * feat, transcendentals=0
        ),
        name="rotate_train",
    )(x, inner, outer)


def rotate_query(x, inner, block=256):
    rows, feat = x.shape
    side = inner.shape[0]
    pack = 256 // side
    groups, wide = side // pack, side * pack
    return pl.pallas_call(
        functools.partial(query_kernel, side, pack),
        out_shape=jax.ShapeDtypeStruct((groups, rows, wide), BF16),
        grid=(rows // block,),
        in_specs=[
            pl.BlockSpec((block, feat), lambda i: (i, 0)),
            pl.BlockSpec((side, side), lambda i: (0, 0)),
        ],
        out_specs=pl.BlockSpec((groups, block, wide), lambda i: (0, i, 0)),
        scratch_shapes=[
            pltpu.VMEM((groups, wide, block), BF16),
            pltpu.VMEM((wide, wide), BF16),
        ],
        compiler_params=pltpu.CompilerParams(vmem_limit_bytes=VMEM_LIMIT),
        cost_estimate=pl.CostEstimate(
            flops=2 * rows * feat * wide, bytes_accessed=4 * rows * feat, transcendentals=0
        ),
        name="rotate_query",
    )(x, inner)


def row_ids_to_columns(ids_ref, start, length):
    pieces = [
        jnp.broadcast_to(ids_ref[:, start + s : start + s + 128], (128, 128)).T
        for s in range(0, length, 128)
    ]
    return pieces[0] if len(pieces) == 1 else jnp.concatenate(pieces, axis=0)


def score_kernel(
    side, pack, scale, rt_ref, hq_ref, eig_ref, sum_ref, outer_ref, ids_ref, out_ref, d_ref, p2_ref, oh_ref
):
    groups, wide, train = rt_ref.shape
    queries = hq_ref.shape[1]
    feat = groups * wide
    damp = sum_ref[0, 0] * scale
    inv = 1.0 / (eig_ref[...] + damp)
    w4t = outer_weight_t(outer_ref[...], side, pack)
    for s in range(0, train, 128):
        col = row_ids_to_columns(ids_ref, s, 128)
        for c in range(0, train, 128):
            hot = onehot(col == iota((128, 128), 1) + c)
            oh_ref[s : s + 128, c : c + 128] = hot
            oh_ref[s : s + 128, train + c : train + c + 128] = hot
    self_acc = [jnp.zeros((8, 128), F32) for _ in range(train // 128)]
    for g in range(groups):
        inv_g = inv[:, g * wide : (g + 1) * wide]
        d = dot(hq_ref[g], w4t) * inv_g
        d_ref[:, g * wide : (g + 1) * wide] = d.astype(BF16)
        col = jnp.broadcast_to(inv_g, (128, wide)).T
        for t in range(train // 128):
            r = rt_ref[g, :, t * 128 : (t + 1) * 128].astype(F32)
            self_acc[t] = self_acc[t] + (r * r * col).reshape(wide // 8, 8, 128).sum(0)
    self_row = jnp.concatenate([a.sum(0, keepdims=True) for a in self_acc], axis=1)
    rt = rt_ref[...].reshape(feat, train)
    for t in range(0, train, 256):
        p = dot(d_ref[...], rt[:, t : t + 256])
        hi = p.astype(BF16)
        p2_ref[:, t : t + 256] = hi
        p2_ref[:, train + t : train + t + 256] = (p - hi.astype(F32)).astype(BF16)
    half = train // 2
    for q in range(0, queries, 256):
        for part in range(2):
            base = part * (half + 8)
            out_ref[base : base + half, q : q + 256] = dot(
                oh_ref[part * half : (part + 1) * half, :], p2_ref[q : q + 256, :], NT
            )
    lines = train // queries
    tail = jnp.concatenate(
        [self_row[:, i * queries : (i + 1) * queries] for i in range(lines)]
        + [jnp.zeros((8 - lines, queries), F32)],
        axis=0,
    )
    for part in range(2):
        base = part * (half + 8) + half
        out_ref[base : base + 8, :] = tail


def partial_scores(rt, hq, eig, eig_sum, outer, ids, scale):
    groups, wide, train = rt.shape
    queries = hq.shape[1]
    side = outer.shape[0]
    whole = pl.BlockSpec(memory_space=pltpu.VMEM)
    return pl.pallas_call(
        functools.partial(score_kernel, side, 256 // side, scale),
        out_shape=jax.ShapeDtypeStruct((train + 16, queries), F32),
        in_specs=[whole, whole, whole, pl.BlockSpec(memory_space=pltpu.SMEM), whole, whole],
        out_specs=whole,
        scratch_shapes=[
            pltpu.VMEM((queries, groups * wide), BF16),
            pltpu.VMEM((queries, 2 * train), BF16),
            pltpu.VMEM((train, 2 * train), BF16),
        ],
        compiler_params=pltpu.CompilerParams(vmem_limit_bytes=VMEM_LIMIT),
        cost_estimate=pl.CostEstimate(
            flops=2 * queries * train * (groups * wide + 2 * train),
            bytes_accessed=2 * groups * wide * (train + queries) + 4 * train * queries,
            transcendentals=0,
        ),
        name="partial_scores",
    )(rt, hq, eig, eig_sum, outer, ids)


def split3(x):
    a = x.astype(BF16)
    rest = x - a.astype(F32)
    b = rest.astype(BF16)
    return a, b, (rest - b.astype(F32)).astype(BF16)


def final_kernel(train, mine_ref, got_ref, qids_ref, tids_ref, out_ref):
    columns, queries = out_ref.shape
    total = mine_ref[:columns, :] + got_ref[:columns, :]
    self_lines = mine_ref[columns:, :] + got_ref[columns:, :]
    lines = train // queries
    self_row = jnp.concatenate([self_lines[i : i + 1, :] for i in range(lines)], axis=1)
    ids = tids_ref[...]
    pick = jnp.where(ids == iota((columns, train), 1), self_row, 0.0)
    own = pick.sum(1, keepdims=True)
    scaled = total * lax.rsqrt(own)
    hot = onehot(iota((queries, queries), 0) == qids_ref[...])
    out_ref[...] = functools.reduce(lambda a, b: a + b, [dot(s, hot) for s in split3(scaled)])


def finish(mine, got, query_ids, train_ids, columns, train):
    queries = mine.shape[1]
    whole = pl.BlockSpec(memory_space=pltpu.VMEM)
    return pl.pallas_call(
        functools.partial(final_kernel, train),
        out_shape=jax.ShapeDtypeStruct((columns, queries), F32),
        in_specs=[whole] * 4,
        out_specs=whole,
        compiler_params=pltpu.CompilerParams(vmem_limit_bytes=VMEM_LIMIT),
        name="finish",
    )(mine, got, query_ids, train_ids)


def exchange(x, bit, devices):
    return lax.ppermute(x, "layer", [(i, i ^ bit) for i in range(devices)])


def shards(query_pool, train_store, query_ids, train_ids, out_basis, in_basis, eigenvalues):
    devices = lax.axis_size("layer")
    bits = devices.bit_length() - 1
    me = lax.axis_index("layer")
    train = train_store.shape[0]
    queries = query_pool.shape[0]
    side = out_basis.shape[1]
    columns = train // devices
    inner, outer = in_basis[0], out_basis[0]

    eig_sum = jnp.sum(eigenvalues).reshape(1, 1)
    for b in range(bits):
        eig_sum = eig_sum + exchange(eig_sum, 1 << b, devices)
    scale = 0.1 / (eigenvalues.shape[1] * devices)
    eig = eigenvalues.reshape(side, side).T.reshape(1, side * side)

    order = [sum(((k >> (bits - 1 - b)) & 1) << b for b in range(bits)) for k in range(devices)]
    blocks = train_ids.reshape(devices, columns)
    ids = jnp.stack([lax.dynamic_index_in_dim(blocks, me ^ k, 0, False) for k in order]).reshape(1, train)

    rt = rotate_train(train_store.reshape(train, -1), inner, outer)
    hq = rotate_query(query_pool.reshape(queries, -1), inner)
    both = partial_scores(rt, hq, eig, eig_sum, outer, ids, scale)

    rows = train // 2
    mine, sent = both[: rows + 8], both[rows + 8 :]
    for b in range(bits):
        got = exchange(sent, 1 << b, devices)
        if b < bits - 1:
            summed = mine + got
            rows //= 2
            mine, sent = jnp.concatenate([summed[:rows], summed[2 * rows :]]), summed[rows:]
    own_ids = lax.dynamic_index_in_dim(blocks, me, 0, False).reshape(columns, 1)
    out = finish(mine, got, query_ids.reshape(1, queries), own_ids, columns, train)
    return out.T


def solution(mesh):
    placed = (
        P("grp", "layer", None),
        P("grp", "layer", None),
        P("grp"),
        P("grp"),
        P("layer", None, None),
        P("layer", None, None),
        P("layer", None),
    )
    return jax.shard_map(
        shards, mesh=mesh, in_specs=placed, out_specs=P("grp", "layer"), check_vma=False
    )
```

time: 209 us -> 91.5 us (0.44)
  blocking collectives: 65.2 us -> 0 us
  matrix products: 45.1 us -> 0 us
  local copies, waits for them, and re-layouts: 49.6 us -> 5.85 us
  Pallas kernels: 0 us -> 33.9 us
  starting transfers between devices: 0.01 us -> 18.7 us
  between operations: 14.1 us -> 3.48 us
  waiting for transfers between devices: 29.2 us -> 26.1 us
    psum x2 -> x0, blocking collectives: 65.2 us -> none  [the longest x1 35.5 us: shards(): eig_sum = lax.psum(jnp.sum(eigenvalues), 'layer')]
    gather x4 -> x0, local copies, waits for them, and re-layouts: 49.4 us -> none  [the longest x2 31.5 us: shards(): window_all = train_store[train_ids]]
    dot_general x4 -> x0, matrix products: 45.1 us -> none  [the longest x1 21.3 us: rotate(): jnp.einsum('op,roj->rpj', outer, half, preferred_element_type=jnp.float32)]
    pallas_call x0 -> x4, Pallas kernels: none -> 33.9 us  [the longest x1 16.2 us: partial_scores(): pl.pallas_call(functools.partial(score_kernel, side, 256 // side, scale),...]
    reduce_scatter x1 -> x0, waiting for transfers between devices: 29.2 us -> none  [shards(): lax.psum_scatter(partial_value, 'layer', scatter_dimension=1, tiled=True)]
    ppermute x0 -> x8, waiting for transfers between devices: none -> 26.1 us  [exchange(): return lax.ppermute(x, 'layer', [(i, i ^ bit) for i in range(devices)])]
    ppermute x0 -> x8, starting transfers between devices: none -> 18.7 us  [exchange(): return lax.ppermute(x, 'layer', [(i, i ^ bit) for i in range(devices)])]
    reshape x0 -> x6, local copies, waits for them, and re-layouts: none -> 2.99 us  [the longest x3 0.85 us: shards(): eig = eigenvalues.reshape(side, side).T.reshape(1, side * side)]
  transfers between devices with their start and end apart: 1 -> 8, of which waited for: 1 -> 7; matrix products, arithmetic and copies ran while one was open for 0% -> 4% of each run, Pallas kernels for 0% -> 17%
where the time goes in v1:
time: 91.5 us; the launch traced here: 91.2 us
  Pallas kernels  33.9 us (37%)
  waiting for transfers between devices  26.1 us (29%)
  starting transfers between devices  18.7 us (20%)
  local copies, waits for them, and re-layouts  5.85 us (6%)
  between operations  3.48 us (4%)
  other arithmetic  3.08 us (3%)
    ppermute x8, waiting for transfers between devices, exchange(): return lax.ppermute(x, 'layer', [(i, i ^ bit) for i in range(devices)])  26.1 us
    ppermute x8, starting transfers between devices, exchange(): return lax.ppermute(x, 'layer', [(i, i ^ bit) for i in range(devices)])  18.7 us
    pallas_call x1, Pallas kernels, partial_scores(): pl.pallas_call(functools.partial(score_kernel, side, 256 // side, scale),...  16.2 us
    pallas_call x1, Pallas kernels, rotate_train(): pl.pallas_call(functools.partial(train_kernel, side, pack), out_shape=jax...  10.2 us
    pallas_call x1, Pallas kernels, rotate_query(): pl.pallas_call(functools.partial(query_kernel, side, pack), out_shape=jax...  5.31 us
    pallas_call x1, Pallas kernels, finish(): pl.pallas_call(functools.partial(final_kernel, train), out_shape=jax.Shap...  2.22 us
    reduce_sum x1, other arithmetic, shards(): eig_sum = jnp.sum(eigenvalues).reshape(1, 1)  2.08 us
  transfers between devices with their start and end apart: 8, of which 7 were waited for; matrix products, arithmetic and copies ran while one was open for 4% of the time, Pallas kernels for 17%

profile of v1, /device:TPU:0, one launch (start us, length us, event | category | flops | bytes accessed | tf_op | source)
XLA Modules:
  0.0 91.2 jit_solution(10852339558327758941)
XLA Ops:
  0.0 0.5 broadcast.3
  0.5 2.1 %fusion = (f32[]{:T(128)}, f32[4096]{0:T(1024)S(1)}) fusion(f32[1,4096]{1,0:T(1,128)} %param.13, f32[]{:T(128)} %broadcast.3), kind=kLoop, calls=%fused_computation.20 | loop fusion | flops 4095 | bytes 32776 | tf_op jit(solution)/shard_map/reduce_sum | solution.py:273
  2.6 0.5 collective-permute-start
  3.0 0.8 reshape.33
  3.8 0.1 stack.2
  3.9 0.7 reshape.34.ids_ref
  4.6 0.1 reshape.30
  4.6 0.1 copy.8
  4.7 0.7 reshape.31.eig_ref
  5.4 5.3 %rotate_query.1.hq_ref = bf16[16,512,256]{2,1,0:T(8,128)(2,1)} custom-call(bf16[512,4096]{1,0:T(8,128)(2,1)} %bitcast.10, bf16[64,64]{1,0:T(8,128)(2,1)} %bitcast.12), custom_call_target="tpu_custom_call" | custom-call | flops 1073741824 | bytes 8388608 | tf_op jit(solution)/shard_map/rotate_query/pallas_call | solution.py:122
  10.7 10.2 %rotate_train.1.rt_ref = bf16[16,256,1024]{2,1,0:T(8,128)(2,1)} custom-call(bf16[1024,4096]{1,0:T(8,128)(2,1)} %bitcast.9, bf16[64,64]{1,0:T(8,128)(2,1)} %bitcast.13, bf16[64,64]{1,0:T(8,128)(2,1)} %bitcast.14), custom_call_target="tpu_custom_call" | custom-call | flops 4294967296 | bytes 16777216 | tf_op jit(solution)/shard_map/rotate_train/pallas_call | solution.py:94
  20.9 0.0 collective-permute-done
  22.2 3.9 %collective-permute-start.1 = (f32[1,1]{1,0:T(1,128)}, f32[1,1]{1,0:T(1,128)}, u32[]{:S(2)}, u32[]{:S(2)}) collective-permute-start(f32[1,1]{1,0:T(1,128)} %add.71), channel_id=1, source_target_pairs={{0,2},{1,3},{2,0},{3,1},{4,6},{5,7},{6,4},{7,5},{8,10},{9,11},{10,... | collective-permute-start | bytes 20 | tf_op jit(solution)/shard_map/ppermute | solution.py:260
  26.1 0.2 collective-permute-done.1
  27.0 3.4 %collective-permute-start.2 = (f32[1,1]{1,0:T(1,128)}, f32[1,1]{1,0:T(1,128)}, u32[]{:S(2)}, u32[]{:S(2)}) collective-permute-start(f32[1,1]{1,0:T(1,128)} %add.72), channel_id=1, source_target_pairs={{0,4},{1,5},{2,6},{3,7},{4,0},{5,1},{6,2},{7,3},{8,12},{9,13},{10,... | collective-permute-start | bytes 20 | tf_op jit(solution)/shard_map/ppermute | solution.py:260
  30.4 0.2 collective-permute-done.2
  31.3 4.4 %collective-permute-start.3 = (f32[1,1]{1,0:T(1,128)}, f32[1,1]{1,0:T(1,128)}, u32[]{:S(2)}, u32[]{:S(2)}) collective-permute-start(f32[1,1]{1,0:T(1,128)} %add.73), channel_id=1, source_target_pairs={{0,8},{1,9},{2,10},{3,11},{4,12},{5,13},{6,14},{7,15},{8,0},{9,1},... | collective-permute-start | bytes 20 | tf_op jit(solution)/shard_map/ppermute | solution.py:260
  35.6 0.2 collective-permute-done.3
  36.5 16.2 %partial_scores.1 = f32[1040,512]{1,0:T(8,128)} custom-call(bf16[16,256,1024]{2,1,0:T(8,128)(2,1)} %rotate_train.1.rt_ref, bf16[16,512,256]{2,1,0:T(8,128)(2,1)} %rotate_query.1.hq_ref, f32[1,4096]{1,0:T(1,128)} %reshape.31.eig_ref, f32[1,1]{1,0:T(1,128)S(6)} %add.74.sum_ref, bf16[64,64]{1,0:T(8,128)(2,1)} %bitcast.15, s32[1,1024]{1,0:T(1,128)} %reshape.34.ids_ref), custom_call_target="tpu_custom_call" | custom-call | flops 6442450944 | bytes 14680064 | tf_op jit(solution)/shard_map/partial_scores/pallas_call | solution.py:205
  52.7 0.0 copy-start
  52.7 1.4 %slice.45 = f32[520,512]{1,0:T(8,128)S(1)} slice(f32[1040,512]{1,0:T(8,128)} %partial_scores.1), slice={[520:1040], [0:512]} | slice | bytes 2129920 | tf_op jit(solution)/shard_map/slice | solution.py:288
  54.2 0.1 collective-permute-start.4
  54.3 2.7 %collective-permute-done.4 = f32[520,512]{1,0:T(8,128)S(1)} collective-permute-done((f32[520,512]{1,0:T(8,128)S(1)}, f32[520,512]{1,0:T(8,128)S(1)}, u32[]{:S(2)}, u32[]{:S(2)}) %collective-permute-start.4) | collective-permute-done | bytes 1064992 | tf_op jit(solution)/shard_map/ppermute | solution.py:260
  56.9 0.0 copy-done
  56.9 0.2 slice_add_fusion
  57.2 1.9 %collective-permute-start.5 = (f32[264,512]{1,0:T(8,128)S(1)}, f32[264,512]{1,0:T(8,128)S(1)}, u32[]{:S(2)}, u32[]{:S(2)}) collective-permute-start(f32[264,512]{1,0:T(8,128)S(1)} %slice.48), channel_id=1, source_target_pairs={{0,2},{1,3},{2,0},{3,1},{4,6},{5,7},{6,4},{7,5},{8,10},{9,11},{10,... | collective-permute-start | bytes 1622024 | tf_op jit(solution)/shard_map/ppermute | solution.py:260
  59.2 12.5 %collective-permute-done.5 = f32[264,512]{1,0:T(8,128)S(1)} collective-permute-done((f32[264,512]{1,0:T(8,128)S(1)}, f32[264,512]{1,0:T(8,128)S(1)}, u32[]{:S(2)}, u32[]{:S(2)}) %collective-permute-start.5) | collective-permute-done | bytes 540704 | tf_op jit(solution)/shard_map/ppermute | solution.py:260
  71.7 0.1 maximum_add_fusion
  71.8 1.9 %collective-permute-start.6 = (f32[136,512]{1,0:T(8,128)S(1)}, f32[136,512]{1,0:T(8,128)S(1)}, u32[]{:S(2)}, u32[]{:S(2)}) collective-permute-start(f32[136,512]{1,0:T(8,128)S(1)} %slice.51), channel_id=1, source_target_pairs={{0,4},{1,5},{2,6},{3,7},{4,0},{5,1},{6,2},{7,3},{8,12},{9,13},{10,... | collective-permute-start | bytes 835592 | tf_op jit(solution)/shard_map/ppermute | solution.py:260
  73.7 6.2 %collective-permute-done.6 = f32[136,512]{1,0:T(8,128)S(1)} collective-permute-done((f32[136,512]{1,0:T(8,128)S(1)}, f32[136,512]{1,0:T(8,128)S(1)}, u32[]{:S(2)}, u32[]{:S(2)}) %collective-permute-start.6) | collective-permute-done | bytes 278560 | tf_op jit(solution)/shard_map/ppermute | solution.py:260
  79.9 2.7 %collective-permute-start.7 = (f32[72,512]{1,0:T(8,128)S(1)}, f32[72,512]{1,0:T(8,128)S(1)}, u32[]{:S(2)}, u32[]{:S(2)}) collective-permute-start(f32[72,512]{1,0:T(8,128)S(1)} %slice.54), channel_id=1, source_target_pairs={{0,8},{1,9},{2,10},{3,11},{4,12},{5,13},{6,14},{7,15},{8,0},{9,1},... | collective-permute-start | bytes 442376 | tf_op jit(solution)/shard_map/ppermute | solution.py:260
  82.7 0.7 copy.9.tids_ref
  83.4 0.7 pad_maximum_fusion.mine_ref
  84.1 4.2 %collective-permute-done.7.got_ref = f32[72,512]{1,0:T(8,128)S(1)} collective-permute-done((f32[72,512]{1,0:T(8,128)S(1)}, f32[72,512]{1,0:T(8,128)S(1)}, u32[]{:S(2)}, u32[]{:S(2)}) %collective-permute-start.7) | collective-permute-done | bytes 147488 | tf_op jit(solution)/shard_map/ppermute | solution.py:260
  88.3 0.0 copy-start.1
  88.3 0.7 copy-done.1
  89.0 2.2 %finish.1 = f32[64,512]{1,0:T(8,128)} custom-call(f32[72,512]{1,0:T(8,128)} %pad_maximum_fusion.mine_ref, f32[72,512]{1,0:T(8,128)} %copy-done.1, s32[1,512]{1,0:T(1,128)} %bitcast.17, s32[64,1]{1,0:T(8,128)} %copy.9.tids_ref), custom_call_target="tpu_custom_call" | custom-call | tf_op jit(solution)/shard_map/finish/pallas_call | solution.py:249
  (11 shorter events, 0.2 us)
Async XLA Ops:
  2.6 18.3 %collective-permute-start = (f32[1,1]{1,0:T(1,128)}, f32[1,1]{1,0:T(1,128)}, u32[]{:S(2)}, u32[]{:S(2)}) collective-permute-start(f32[1,1]{1,0:T(1,128)} %bitcast.5), channel_id=1, source_target_pairs={{0,1},{1,0},{2,3},{3,2},{4,5},{5,4},{6,7},{7,6},{8,9},{9,8},{10,11... | collective-permute-start | bytes 20 | tf_op jit(solution)/shard_map/ppermute | solution.py:260
  22.2 4.1 %collective-permute-start.1 = (f32[1,1]{1,0:T(1,128)}, f32[1,1]{1,0:T(1,128)}, u32[]{:S(2)}, u32[]{:S(2)}) collective-permute-start(f32[1,1]{1,0:T(1,128)} %add.71), channel_id=1, source_target_pairs={{0,2},{1,3},{2,0},{3,1},{4,6},{5,7},{6,4},{7,5},{8,10},{9,11},{10,... | collective-permute-start | bytes 20 | tf_op jit(solution)/shard_map/ppermute | solution.py:260
  27.0 3.6 %collective-permute-start.2 = (f32[1,1]{1,0:T(1,128)}, f32[1,1]{1,0:T(1,128)}, u32[]{:S(2)}, u32[]{:S(2)}) collective-permute-start(f32[1,1]{1,0:T(1,128)} %add.72), channel_id=1, source_target_pairs={{0,4},{1,5},{2,6},{3,7},{4,0},{5,1},{6,2},{7,3},{8,12},{9,13},{10,... | collective-permute-start | bytes 20 | tf_op jit(solution)/shard_map/ppermute | solution.py:260
  31.3 4.6 %collective-permute-start.3 = (f32[1,1]{1,0:T(1,128)}, f32[1,1]{1,0:T(1,128)}, u32[]{:S(2)}, u32[]{:S(2)}) collective-permute-start(f32[1,1]{1,0:T(1,128)} %add.73), channel_id=1, source_target_pairs={{0,8},{1,9},{2,10},{3,11},{4,12},{5,13},{6,14},{7,15},{8,0},{9,1},... | collective-permute-start | bytes 20 | tf_op jit(solution)/shard_map/ppermute | solution.py:260
  52.7 4.2 %copy-start = (f32[1040,512]{1,0:T(8,128)S(1)}, f32[1040,512]{1,0:T(8,128)}, u32[]{:S(2)}) copy-start(f32[1040,512]{1,0:T(8,128)} %partial_scores.1) | copy-start | bytes 6389764
  54.2 2.7 %collective-permute-start.4 = (f32[520,512]{1,0:T(8,128)S(1)}, f32[520,512]{1,0:T(8,128)S(1)}, u32[]{:S(2)}, u32[]{:S(2)}) collective-permute-start(f32[520,512]{1,0:T(8,128)S(1)} %slice.45), channel_id=1, source_target_pairs={{0,1},{1,0},{2,3},{3,2},{4,5},{5,4},{6,7},{7,6},{8,9},{9,8},{10,11... | collective-permute-start | bytes 3194888 | tf_op jit(solution)/shard_map/ppermute | solution.py:260
  57.2 14.5 %collective-permute-start.5 = (f32[264,512]{1,0:T(8,128)S(1)}, f32[264,512]{1,0:T(8,128)S(1)}, u32[]{:S(2)}, u32[]{:S(2)}) collective-permute-start(f32[264,512]{1,0:T(8,128)S(1)} %slice.48), channel_id=1, source_target_pairs={{0,2},{1,3},{2,0},{3,1},{4,6},{5,7},{6,4},{7,5},{8,10},{9,11},{10,... | collective-permute-start | bytes 1622024 | tf_op jit(solution)/shard_map/ppermute | solution.py:260
  71.8 8.1 %collective-permute-start.6 = (f32[136,512]{1,0:T(8,128)S(1)}, f32[136,512]{1,0:T(8,128)S(1)}, u32[]{:S(2)}, u32[]{:S(2)}) collective-permute-start(f32[136,512]{1,0:T(8,128)S(1)} %slice.51), channel_id=1, source_target_pairs={{0,4},{1,5},{2,6},{3,7},{4,0},{5,1},{6,2},{7,3},{8,12},{9,13},{10,... | collective-permute-start | bytes 835592 | tf_op jit(solution)/shard_map/ppermute | solution.py:260
  79.9 8.4 %collective-permute-start.7 = (f32[72,512]{1,0:T(8,128)S(1)}, f32[72,512]{1,0:T(8,128)S(1)}, u32[]{:S(2)}, u32[]{:S(2)}) collective-permute-start(f32[72,512]{1,0:T(8,128)S(1)} %slice.54), channel_id=1, source_target_pairs={{0,8},{1,9},{2,10},{3,11},{4,12},{5,13},{6,14},{7,15},{8,0},{9,1},... | collective-permute-start | bytes 442376 | tf_op jit(solution)/shard_map/ppermute | solution.py:260
  88.3 0.7 copy-start.1

commit v2 on v0

v2 whole, which is shorter than its diff:
```python
import functools

import jax
import jax.numpy as jnp
from jax import lax
from jax.experimental import pallas as pl
from jax.experimental.pallas import tpu as pltpu
from jax.sharding import PartitionSpec as P

BF16 = jnp.bfloat16
F32 = jnp.float32
VMEM_LIMIT = 56 * 1024 * 1024
CHUNKS = 2
NN = (((1,), (0,)), ((), ()))
NT = (((1,), (1,)), ((), ()))


def dot(a, b, dims=NN):
    return lax.dot_general(a, b, dims, preferred_element_type=F32)


def iota(shape, dim):
    return lax.broadcasted_iota(jnp.int32, shape, dim)


def onehot(cond):
    return jnp.where(cond, 1.0, 0.0).astype(BF16)


def even_first(place, side):
    return place % (side // 2) * 2 + place // (side // 2)


def inner_weight(basis, side, pack):
    wide = side * pack
    rows = onehot(iota((wide, side), 0) // pack == iota((wide, side), 1))
    cols = onehot(iota((side, wide), 1) % side == iota((side, wide), 0))
    full = dot(dot(rows, basis, NT).astype(BF16), cols)
    keep = iota((wide, wide), 0) % pack == iota((wide, wide), 1) // side
    return jnp.where(keep, full, 0.0).astype(BF16)


def outer_weight(basis, side, pack):
    wide = side * pack
    rows = onehot(even_first(iota((wide, side), 0) % side, side) == iota((wide, side), 1))
    k = iota((side, wide), 1)
    cols = onehot(k // (pack * pack) * pack + k % pack == iota((side, wide), 0))
    full = dot(dot(rows, basis, NT).astype(BF16), cols)
    keep = iota((wide, wide), 0) // side == iota((wide, wide), 1) // pack % pack
    return jnp.where(keep, full, 0.0).astype(BF16)


def outer_weight_t(basis, side, pack):
    wide = side * pack
    k = iota((wide, side), 0)
    rows = onehot(k // (pack * pack) * pack + k % pack == iota((wide, side), 1))
    cols = onehot(even_first(iota((side, wide), 1) % side, side) == iota((side, wide), 0))
    full = dot(dot(rows, basis).astype(BF16), cols)
    keep = iota((wide, wide), 1) // side == iota((wide, wide), 0) // pack % pack
    return jnp.where(keep, full, 0.0).astype(BF16)


def halves(x_ref, weight, half_ref, side, pack):
    wide = side * pack
    groups = side // pack
    unit = pack * pack
    for g in range(groups):
        part = dot(weight, x_ref[:, g * wide : (g + 1) * wide], NT).astype(BF16)
        half_ref[:, g * unit : (g + 1) * unit, :] = part.reshape(groups, unit, part.shape[1])


def in_vmem(x):
    return pltpu.with_memory_space_constraint(x, pltpu.VMEM)


WHOLE = pl.BlockSpec(memory_space=pltpu.VMEM)
IN_HBM = pl.BlockSpec(memory_space=pltpu.HBM)
ANYWHERE = pl.BlockSpec(memory_space=pl.ANY)


def kernel_call(body, name, args, outs, scratch=(), specs=None, flops=0, limit=VMEM_LIMIT):
    specs = specs or [WHOLE] * len(args)
    place = {id(IN_HBM): pltpu.HBM, id(WHOLE): pltpu.VMEM}
    args = [
        pltpu.with_memory_space_constraint(a, place[id(s)]) if id(s) in place and a.size > 2048 or s is IN_HBM else a
        for a, s in zip(args, specs)
    ]
    return pl.pallas_call(
        body,
        out_shape=tuple(pltpu.VMEM(shape, dtype) for shape, dtype in outs),
        in_specs=specs,
        out_specs=tuple([WHOLE] * len(outs)),
        scratch_shapes=list(scratch),
        compiler_params=pltpu.CompilerParams(vmem_limit_bytes=limit),
        cost_estimate=pl.CostEstimate(flops=flops, bytes_accessed=0, transcendentals=0),
        name=name,
    )(*args)


def fetch(pairs, sems):
    copies = [pltpu.make_async_copy(src, dst, sems.at[i]) for i, (src, dst) in enumerate(pairs)]
    for copy in copies:
        copy.start()
    return copies


def prepare_kernel(devices, side, pack, *refs):
    _, tids_any, qids_any, eig_any, inner_any, outer_any, x_any = refs[:7]
    sel_t_ref, sel_q_ref, eig_t_ref, w3_ref, w4_ref, w4t_ref, x_ref = refs[7:14]
    tids_ref, qids_ref, eig_ref, inner_ref, outer_ref, sems = refs[14:]
    small = ((tids_any, tids_ref), (qids_any, qids_ref), (eig_any, eig_ref), (inner_any, inner_ref), (outer_any, outer_ref))
    copies = fetch(small + ((x_any, x_ref),), sems)
    for copy in copies[:-1]:
        copy.wait()
    me = lax.axis_index("layer")
    train, queries = sel_t_ref.shape[0], sel_q_ref.shape[0]
    ids = jnp.broadcast_to(tids_ref[...], (8, train))
    lane = iota((8, train), 1)
    step = train // devices
    core = me % 2
    while step < train:
        bit = (lane // step) % 2
        other = jnp.where(bit == 0, pltpu.roll(ids, train - step, 1), pltpu.roll(ids, step, 1))
        ids = jnp.where(me % 2 == 1, other, ids)
        me = me // 2
        step *= 2
    owner = (core + lane // (train // devices)) % 2
    step = 2 * (train // devices)
    low, high = (lane // step) % 2, (lane // (2 * step)) % 2
    other = jnp.where(low > high, pltpu.roll(ids, train - step, 1), jnp.where(low < high, pltpu.roll(ids, step, 1), ids))
    ids = jnp.where(owner == 1, other, ids)
    for s in range(0, train, 128):
        col = jnp.broadcast_to(ids[0:1, s : s + 128], (128, 128)).T
        for c in range(0, train, 128):
            sel_t_ref[s : s + 128, c : c + 128] = onehot(col == iota((128, 128), 1) + c)
    sel_q_ref[...] = onehot(iota((queries, queries), 0) == qids_ref[...])
    eig = jnp.concatenate([eig_ref[:, c : c + 2 * side] for c in range(0, side * side, 2 * side)], axis=0)
    eig = eig.T
    eig = jnp.concatenate([eig[:side], eig[side:]], axis=1)
    for j in range(side):
        eig_t_ref[:, j * side : (j + 1) * side] = eig[j : j + 1, :]
    w3_ref[...] = inner_weight(inner_ref[...], side, pack)
    w4_ref[...] = outer_weight(outer_ref[...], side, pack)
    w4t_ref[...] = outer_weight_t(outer_ref[...], side, pack)
    copies[-1].wait()


def prepare(after, tids, qids, eig, inner, outer, x, devices):
    train, queries, side = tids.shape[1], qids.shape[1], inner.shape[0]
    pack = 256 // side
    wide = side * pack
    return kernel_call(
        functools.partial(prepare_kernel, devices, side, pack),
        "prepare",
        (after, tids, qids, eig, inner, outer, x),
        [((train, train), BF16), ((queries, queries), BF16), (eig.shape, F32)]
        + [((wide, wide), BF16)] * 3
        + [(x.shape, BF16)],
        [pltpu.VMEM(a.shape, a.dtype) for a in (tids, qids, eig, inner, outer)] + [pltpu.SemaphoreType.DMA((6,))],
        [ANYWHERE] + [IN_HBM] * 6,
        limit=6 << 20,
    )


def query_kernel(side, after_ref, x_ref, w3_ref, next_any, out_ref, next_ref, half_ref, sems):
    copies = fetch(((next_any.at[: next_ref.shape[0]], next_ref),), sems)
    pack = w3_ref.shape[0] // side
    halves(x_ref, w3_ref[...], half_ref, side, pack)
    for g in range(side // pack):
        out_ref[g] = half_ref[g].T
    copies[0].wait()


def rotate_query(after, x, w3, upcoming, rows_next, side):
    rows, feat = x.shape
    wide = w3.shape[0]
    groups = feat // wide
    return kernel_call(
        functools.partial(query_kernel, side),
        "rotate_query",
        (after, x, w3, upcoming),
        [((groups, rows, wide), BF16), ((rows_next, feat), BF16)],
        [pltpu.VMEM((groups, wide, rows), BF16), pltpu.SemaphoreType.DMA((1,))],
        [ANYWHERE, WHOLE, WHOLE, IN_HBM],
        flops=2 * rows * feat * wide,
        limit=12 << 20,
    )


def train_kernel(side, start, after_ref, x_ref, w3_ref, w4_ref, next_any, out_ref, *rest):
    half_ref, sems = rest[-2:]
    copies = []
    if start:
        (next_ref,) = rest[:-2]
        copies = fetch(((next_any.at[start : start + next_ref.shape[0]], next_ref),), sems)
    halves(x_ref, w3_ref[...], half_ref, side, w3_ref.shape[0] // side)
    w4 = w4_ref[...]
    for g in range(out_ref.shape[0]):
        out_ref[g] = dot(w4, half_ref[g]).astype(BF16)
    for copy in copies:
        copy.wait()


def rotate_train(after, x, w3, w4, upcoming, start, side):
    rows, feat = x.shape
    wide = w3.shape[0]
    groups = feat // wide
    outs = [((groups, wide, rows), BF16)]
    if start:
        outs.append(((rows, feat), BF16))
    return kernel_call(
        functools.partial(train_kernel, side, start),
        "rotate_train",
        (after, x, w3, w4, upcoming),
        outs,
        [pltpu.VMEM((groups, wide, rows), BF16), pltpu.SemaphoreType.DMA((1,))],
        [ANYWHERE, WHOLE, WHOLE, WHOLE, IN_HBM],
        flops=4 * rows * feat * wide,
        limit=12 << 20,
    )


def score_kernel(scale, devices, start, with_self, parts, *refs):
    refs = refs[1:]
    rt_refs = refs[:parts]
    hq_ref, eig_ref, sum_ref, w4t_ref, sel_ref, mine_ref, sent_ref, d_ref, p_ref = refs[parts:]
    groups, wide, cols = rt_refs[0].shape
    train = cols * parts
    queries = mine_ref.shape[1]
    feat = groups * wide
    inv = 1.0 / (eig_ref[...] + sum_ref[0:1, 0:1] * scale)
    w4t = w4t_ref[...]
    for g in range(groups):
        d = dot(hq_ref[g, start : start + queries, :], w4t) * inv[:, g * wide : (g + 1) * wide]
        d_ref[:, g * wide : (g + 1) * wide] = d.astype(BF16)
    for i, rt_ref in enumerate(rt_refs):
        rt = rt_ref[...].reshape(feat, cols)
        for t in range(0, cols, 256):
            p = dot(d_ref[...], rt[:, t : t + 256])
            hi = p.astype(BF16)
            at = i * cols + t
            p_ref[0, :, at : at + 256] = hi
            p_ref[1, :, at : at + 256] = (p - hi.astype(F32)).astype(BF16)
    half = train // 2
    columns = train // devices
    bits = devices.bit_length() - 1
    rows = min(half, 512)
    for base in range(0, train, rows):
        pick = sel_ref[base : base + rows, :]
        got = dot(pick, p_ref[0], NT) + dot(pick, p_ref[1], NT)
        for k in range(rows // columns):
            block = base // columns + k
            place = sum(((block >> i) & 1) << (bits - 1 - i) for i in range(bits))
            ref = (mine_ref, sent_ref)[place * columns // half]
            at = place * columns % half
            ref[at : at + columns, :] = got[k * columns : (k + 1) * columns, :]
    if with_self:
        sums = []
        for rt_ref in rt_refs:
            for t in range(0, cols, 128):
                acc = jnp.zeros((8, 128), F32)
                for g in range(groups):
                    col = jnp.broadcast_to(inv[:, g * wide : (g + 1) * wide], (128, wide)).T
                    r = rt_ref[g, :, t : t + 128].astype(F32)
                    acc = acc + (r * r * col).reshape(wide // 8, 8, 128).sum(0)
                sums.append(acc.sum(0, keepdims=True))
        per = queries // 128
        tail = [jnp.concatenate(sums[i : i + per], axis=1) for i in range(0, len(sums), per)]
        tail += [jnp.zeros((1, queries), F32)] * (8 - len(tail))
        tail = jnp.concatenate(tail, axis=0)
        mine_ref[half : half + 8, :] = tail
        sent_ref[half : half + 8, :] = tail


def partial_scores(after, rts, hq, eig, eig_sum, w4t, sel, scale, devices, start, queries, with_self):
    groups, wide, cols = rts[0].shape
    train = cols * len(rts)
    rows = train // 2 + 8 * with_self
    return kernel_call(
        functools.partial(score_kernel, scale, devices, start, with_self, len(rts)),
        "partial_scores",
        (after, *rts, hq, eig, eig_sum, w4t, sel),
        [((rows, queries), F32)] * 2,
        [pltpu.VMEM((queries, groups * wide), BF16), pltpu.VMEM((2, queries, train), BF16)],
        [ANYWHERE] + [WHOLE] * (len(rts) + 5),
        flops=2 * queries * train * (groups * wide + 2 * train),
        limit=16 << 20,
    )


def final_kernel(*refs):
    sel_t_ref, sel_ref, out_ref = refs[-3:]
    columns, queries = out_ref.shape
    train = sel_t_ref.shape[1]
    sums = [refs[i][...] + refs[i + 1][...] for i in range(0, len(refs) - 3, 2)]
    total = jnp.concatenate([s[:columns] for s in sums], axis=1)
    tail = sums[0][columns:]
    self_row = jnp.concatenate([tail[i : i + 1] for i in range(train // tail.shape[1])], axis=1)
    own = sel_t_ref[: max(columns, 16), :].astype(F32)[:columns]
    scaled = total * lax.rsqrt((own * self_row).sum(1, keepdims=True))
    hi = scaled.astype(BF16)
    rest = scaled - hi.astype(F32)
    mid = rest.astype(BF16)
    low = (rest - mid.astype(F32)).astype(BF16)
    sel = sel_ref[...]
    out_ref[...] = dot(hi, sel) + dot(mid, sel) + dot(low, sel)


def finish(pairs, sel_t, sel_q, columns):
    args = [a for pair in pairs for a in pair]
    return pl.pallas_call(
        final_kernel,
        out_shape=jax.ShapeDtypeStruct((columns, sel_q.shape[0]), F32),
        in_specs=[WHOLE] * (len(args) + 2),
        out_specs=WHOLE,
        compiler_params=pltpu.CompilerParams(vmem_limit_bytes=8 << 20),
        name="finish",
    )(*args, in_vmem(sel_t), in_vmem(sel_q))


def sum_kernel(x_ref, out_ref):
    out_ref[...] = jnp.broadcast_to(jnp.sum(x_ref[...], axis=1, keepdims=True), out_ref.shape)


def next_halves(mine, got, rows):
    total = mine + got
    rows //= 2
    return jnp.concatenate([total[:rows], total[2 * rows :]]), total[rows:]


def halving_step(x, step, devices):
    swap = {1: 2, 2: 1} if devices > 4 else {}
    pairs = [(i, i ^ (1 << (swap.get(step, step) if i % 2 else step))) for i in range(devices)]
    return lax.ppermute(x, "layer", pairs)


def exchange(x, bit, devices):
    return lax.ppermute(x, "layer", [(i, i ^ bit) for i in range(devices)])


def shards(query_pool, train_store, query_ids, train_ids, out_basis, in_basis, eigenvalues):
    devices = lax.axis_size("layer")
    bits = devices.bit_length() - 1
    train = train_store.shape[0]
    queries = query_pool.shape[0]
    side = out_basis.shape[1]
    columns = train // devices
    inner, outer = in_basis[0], out_basis[0]

    scale = 0.1 / (eigenvalues.shape[1] * devices)
    tids, qids = train_ids.reshape(1, train), query_ids.reshape(1, queries)
    xq, xt = query_pool.reshape(queries, -1), train_store.reshape(train, -1)

    half = train // 2
    eig_sum = kernel_call(sum_kernel, "eig_sum", (eigenvalues,), [((1, 128), F32)], limit=1 << 20)[0]
    for b in range(bits):
        got = exchange(eig_sum, 1 << b, devices)
        if b == 0:
            sel_t, sel_q, eig, w3, w4, w4t, xq = prepare(eig_sum, tids, qids, eigenvalues, inner, outer, xq, devices)
        elif b == 1:
            hq, xa = rotate_query(eig_sum, xq, w3, xt, half, side)
        elif b == 2:
            rta, xb = rotate_train(eig_sum, xa, w3, w4, xt, half, side)
        elif b == 3:
            (rtb,) = rotate_train(eig_sum, xb, w3, w4, xt, 0, side)
        eig_sum = eig_sum + got

    chunk = queries // CHUNKS
    after = eig_sum
    works = []
    for c in range(CHUNKS):
        mine, sent = partial_scores(
            after, (rta, rtb), hq, eig, eig_sum, w4t, sel_t, scale, devices, c * chunk, chunk, c == 0
        )
        mine, after = next_halves(mine, halving_step(sent, 0, devices), half)
        works.append((mine, after))
    pairs = []
    for mine, sent in works:
        for b in range(1, bits):
            got = halving_step(sent, b, devices)
            if b < bits - 1:
                mine, sent = next_halves(mine, got, half >> b)
        pairs.append((mine, got))
    return finish(pairs, sel_t, sel_q, columns).T


def solution(mesh):
    placed = (
        P("grp", "layer", None),
        P("grp", "layer", None),
        P("grp"),
        P("grp"),
        P("layer", None, None),
        P("layer", None, None),
        P("layer", None),
    )
    return jax.shard_map(
        shards, mesh=mesh, in_specs=placed, out_specs=P("grp", "layer"), check_vma=False
    )
```

time: 209 us -> 52 us (0.25)
  blocking collectives: 65.2 us -> 0 us
  local copies, waits for them, and re-layouts: 49.6 us -> 0.84 us
  matrix products: 45.1 us -> 0 us
  Pallas kernels: 0 us -> 20.5 us
  starting transfers between devices: 0.01 us -> 15.9 us
  waiting for transfers between devices: 29.2 us -> 14 us
  between operations: 14.1 us -> 0.23 us
  other arithmetic: 4.48 us -> 0.3 us
    psum x2 -> x0, blocking collectives: 65.2 us -> none  [the longest x1 35.5 us: shards(): eig_sum = lax.psum(jnp.sum(eigenvalues), 'layer')]
    gather x4 -> x0, local copies, waits for them, and re-layouts: 49.4 us -> none  [the longest x2 31.5 us: shards(): window_all = train_store[train_ids]]
    dot_general x4 -> x0, matrix products: 45.1 us -> none  [the longest x1 21.3 us: rotate(): jnp.einsum('op,roj->rpj', outer, half, preferred_element_type=jnp.float32)]
    reduce_scatter x1 -> x0, waiting for transfers between devices: 29.2 us -> none  [shards(): lax.psum_scatter(partial_value, 'layer', scatter_dimension=1, tiled=True)]
    pallas_call x0 -> x8, Pallas kernels: none -> 20.5 us  [the longest x7 19.3 us: kernel_call(): pl.pallas_call(body, out_shape=tuple((pltpu.VMEM(shape, dtype) for shape,...]
    ppermute x0 -> x12, starting transfers between devices: none -> 15.9 us  [the longest x8 8.54 us: halving_step(): return lax.ppermute(x, 'layer', pairs)]
    ppermute x0 -> x12, waiting for transfers between devices: none -> 14 us  [the longest x8 14 us: halving_step(): return lax.ppermute(x, 'layer', pairs)]
  transfers between devices with their start and end apart: 1 -> 12, of which waited for: 1 -> 8; matrix products, arithmetic and copies ran while one was open for 0% -> 1% of each run, Pallas kernels for 0% -> 20%
where the time goes in v2:
time: 52 us; the launch traced here: 51.7 us
  Pallas kernels  20.5 us (39%)
  starting transfers between devices  15.9 us (31%)
  waiting for transfers between devices  14 us (27%)
  local copies, waits for them, and re-layouts  0.84 us (2%)
    pallas_call x7, Pallas kernels, kernel_call(): pl.pallas_call(body, out_shape=tuple((pltpu.VMEM(shape, dtype) for shape,...  19.3 us
    ppermute x8, waiting for transfers between devices, halving_step(): return lax.ppermute(x, 'layer', pairs)  14 us
    ppermute x8, starting transfers between devices, halving_step(): return lax.ppermute(x, 'layer', pairs)  8.54 us
    ppermute x4, starting transfers between devices, exchange(): return lax.ppermute(x, 'layer', [(i, i ^ bit) for i in range(devices)])  7.33 us
    pallas_call x1, Pallas kernels, finish(): pl.pallas_call(final_kernel, out_shape=jax.ShapeDtypeStruct((columns, sel...  1.12 us
  transfers between devices with their start and end apart: 12, of which 8 were waited for; matrix products, arithmetic and copies ran while one was open for 1% of the time, Pallas kernels for 20%

profile of v2, /device:TPU:0, one launch (start us, length us, event | category | flops | bytes accessed | tf_op | source)
XLA Modules:
  0.0 51.7 jit_solution(7639447802068771633)
XLA Ops:
  0.0 0.0 copy-start
  0.0 0.7 %copy-done = f32[1,4096]{1,0:T(1,128)S(1)} copy-done((f32[1,4096]{1,0:T(1,128)S(1)}, f32[1,4096]{1,0:T(1,128)}, u32[]{:S(2)}) %copy-start) | copy-done | bytes 16408
  0.7 0.1 eig_sum.1.refs_0_
  0.8 0.5 collective-permute-start
  1.3 2.3 %prepare.1 = (bf16[1024,1024]{1,0:T(8,128)(2,1)S(1)}, bf16[512,512]{1,0:T(8,128)(2,1)S(1)}, f32[1,4096]{1,0:T(1,128)S(1)}, bf16[256,256]{1,0:T(8,128)(2,1)S(1)},...) custom-call(f32[1,128]{1,0:T(1,128)S(1)} %eig_sum.1.refs_0_, ...), custom_call_target="tpu_custom_call" | custom-call | tf_op jit(solution)/shard_map/prepare/pallas_call | solution.py:88
  3.6 0.0 collective-permute-done
  3.6 2.6 %collective-permute-start.1 = (f32[1,128]{1,0:T(1,128)S(1)}, f32[1,128]{1,0:T(1,128)S(1)}, u32[]{:S(2)}, u32[]{:S(2)}) collective-permute-start(f32[1,128]{1,0:T(1,128)S(1)} %add.30.after_ref), channel_id=1, source_target_pairs={{0,2},{1,3},{2,0},{3,1},{4,6},{5,7},{6,4},{7,5},{8,10},{9,11},{10,... | collective-permute-start | bytes 1544 | tf_op jit(solution)/shard_map/ppermute | solution.py:338
  6.2 2.2 %rotate_query.1 = (bf16[16,512,256]{2,1,0:T(8,128)(2,1)S(1)}, bf16[512,4096]{1,0:T(8,128)(2,1)S(1)}) custom-call(f32[1,128]{1,0:T(1,128)S(1)} %add.30.after_ref, bf16[512,4096]{1,0:T(8,128)(2,1)S(1)} %get-tuple-element.20.x_ref, bf16[256,256]{1,0:T(8,128)(2,1)S(1)} %get-tuple-element.21.w3_ref, bf16[1024,4096]{1,0:T(8,128)(2,1)} %bitcast.7), custom_call_target="tpu_custom_call" | custom-call | flops 1073741824 | tf_op jit(solution)/shard_map/rotate_query/pallas_call | solution.py:88
  8.4 0.0 collective-permute-done.1
  8.4 1.6 %collective-permute-start.2 = (f32[1,128]{1,0:T(1,128)S(1)}, f32[1,128]{1,0:T(1,128)S(1)}, u32[]{:S(2)}, u32[]{:S(2)}) collective-permute-start(f32[1,128]{1,0:T(1,128)S(1)} %add.31.after_ref), channel_id=1, source_target_pairs={{0,4},{1,5},{2,6},{3,7},{4,0},{5,1},{6,2},{7,3},{8,12},{9,13},{10,... | collective-permute-start | bytes 1544 | tf_op jit(solution)/shard_map/ppermute | solution.py:338
  10.1 3.3 %rotate_train.2 = (bf16[16,256,512]{2,1,0:T(8,128)(2,1)S(1)}, bf16[512,4096]{1,0:T(8,128)(2,1)S(1)}) custom-call(f32[1,128]{1,0:T(1,128)S(1)} %add.31.after_ref, bf16[512,4096]{1,0:T(8,128)(2,1)S(1)} %get-tuple-element.22.x_ref, bf16[256,256]{1,0:T(8,128)(2,1)S(1)} %get-tuple-element.21.w3_ref, bf16[256,256]{1,0:T(8,128)(2,1)S(1)} %get-tuple-element.23.w4_ref, ...), custom_call_target="tpu_custom_call" | custom-call | flops 2147483648 | tf_op jit(solution)/shard_map/rotate_train/pallas_call | solution.py:88
  13.4 0.0 collective-permute-done.2
  13.4 2.7 %collective-permute-start.3 = (f32[1,128]{1,0:T(1,128)S(1)}, f32[1,128]{1,0:T(1,128)S(1)}, u32[]{:S(2)}, u32[]{:S(2)}) collective-permute-start(f32[1,128]{1,0:T(1,128)S(1)} %add.32.after_ref), channel_id=1, source_target_pairs={{0,8},{1,9},{2,10},{3,11},{4,12},{5,13},{6,14},{7,15},{8,0},{9,1},... | collective-permute-start | bytes 1544 | tf_op jit(solution)/shard_map/ppermute | solution.py:338
  16.1 2.5 %rotate_train.3.refs_2_ = bf16[16,256,512]{2,1,0:T(8,128)(2,1)S(1)} custom-call(f32[1,128]{1,0:T(1,128)S(1)} %add.32.after_ref, bf16[512,4096]{1,0:T(8,128)(2,1)S(1)} %get-tuple-element.25.x_ref, bf16[256,256]{1,0:T(8,128)(2,1)S(1)} %get-tuple-element.21.w3_ref, bf16[256,256]{1,0:T(8,128)(2,1)S(1)} %get-tuple-element.23.w4_ref, bf16[1024,4096]{1,0:T(8,128)(2,1)} %bitcast.9), custom_call_target="tpu_custom_call" | custom-call | flops 2147483648 | tf_op jit(solution)/shard_map/rotate_train/pallas_call | solution.py:88
  18.6 0.0 collective-permute-done.3
  18.6 4.9 %partial_scores.2 = (f32[520,256]{1,0:T(8,128)S(1)}, f32[520,256]{1,0:T(8,128)S(1)}) custom-call(f32[1,128]{1,0:T(1,128)S(1)} %add.33.refs_0_.refs_5_, bf16[16,256,512]{2,1,0:T(8,128)(2,1)S(1)} %get-tuple-element.24.refs_1_, bf16[16,256,512]{2,1,0:T(8,128)(2,1)S(1)} %rotate_train.3.refs_2_, bf16[16,512,256]{2,1,0:T(8,128)(2,1)S(1)} %get-tuple-element.26.refs_3_, ...), custom_call_target="tpu_custom_call" | custom-call | flops 3221225472 | tf_op jit(solution)/shard_map/partial_scores/pallas_call | solution.py:88
  23.5 0.1 collective-permute-start.4
  23.6 1.9 %collective-permute-done.4 = f32[520,256]{1,0:T(8,128)S(1)} collective-permute-done((f32[520,256]{1,0:T(8,128)S(1)}, f32[520,256]{1,0:T(8,128)S(1)}, u32[]{:S(2)}, u32[]{:S(2)}) %collective-permute-start.4) | collective-permute-done | bytes 532512 | tf_op jit(solution)/shard_map/ppermute | solution.py:334
  25.5 0.1 add.34
  25.6 4.0 %partial_scores.3 = (f32[512,256]{1,0:T(8,128)S(1)}, f32[512,256]{1,0:T(8,128)S(1)}) custom-call(f32[264,256]{1,0:T(8,128)S(1)} %slice.62.refs_0_, bf16[16,256,512]{2,1,0:T(8,128)(2,1)S(1)} %get-tuple-element.24.refs_1_, bf16[16,256,512]{2,1,0:T(8,128)(2,1)S(1)} %rotate_train.3.refs_2_, bf16[16,512,256]{2,1,0:T(8,128)(2,1)S(1)} %get-tuple-element.26.refs_3_, ...), custom_call_target="tpu_custom_call" | custom-call | flops 3221225472 | tf_op jit(solution)/shard_map/partial_scores/pallas_call | solution.py:88
  29.6 0.2 collective-permute-start.8
  29.8 1.2 %collective-permute-start.5 = (f32[264,256]{1,0:T(8,128)S(1)}, f32[264,256]{1,0:T(8,128)S(1)}, u32[]{:S(2)}, u32[]{:S(2)}) collective-permute-start(f32[264,256]{1,0:T(8,128)S(1)} %slice.62.refs_0_), channel_id=1, source_target_pairs={{0,2},{1,5},{2,0},{3,7},{4,6},{5,1},{6,4},{7,3},{8,10},{9,13},{10,... | collective-permute-start | bytes 811016 | tf_op jit(solution)/shard_map/ppermute | solution.py:334
  31.1 0.5 %collective-permute-done.8 = f32[512,256]{1,0:T(8,128)S(1)} collective-permute-done((f32[512,256]{1,0:T(8,128)S(1)}, f32[512,256]{1,0:T(8,128)S(1)}, u32[]{:S(2)}, u32[]{:S(2)}) %collective-permute-start.8) | collective-permute-done | bytes 524320 | tf_op jit(solution)/shard_map/ppermute | solution.py:334
  31.6 0.1 add.37
  31.7 1.3 %collective-permute-start.9 = (f32[256,256]{1,0:T(8,128)S(1)}, f32[256,256]{1,0:T(8,128)S(1)}, u32[]{:S(2)}, u32[]{:S(2)}) collective-permute-start(f32[256,256]{1,0:T(8,128)S(1)} %slice.70), channel_id=1, source_target_pairs={{0,2},{1,5},{2,0},{3,7},{4,6},{5,1},{6,4},{7,3},{8,10},{9,13},{10,... | collective-permute-start | bytes 786440 | tf_op jit(solution)/shard_map/ppermute | solution.py:334
  33.1 3.2 %collective-permute-done.5 = f32[264,256]{1,0:T(8,128)S(1)} collective-permute-done((f32[264,256]{1,0:T(8,128)S(1)}, f32[264,256]{1,0:T(8,128)S(1)}, u32[]{:S(2)}, u32[]{:S(2)}) %collective-permute-start.5) | collective-permute-done | bytes 270368 | tf_op jit(solution)/shard_map/ppermute | solution.py:334
  36.4 0.5 %collective-permute-start.6 = (f32[136,256]{1,0:T(8,128)S(1)}, f32[136,256]{1,0:T(8,128)S(1)}, u32[]{:S(2)}, u32[]{:S(2)}) collective-permute-start(f32[136,256]{1,0:T(8,128)S(1)} %slice.65), channel_id=1, source_target_pairs={{0,4},{1,3},{2,6},{3,1},{4,0},{5,7},{6,2},{7,5},{8,12},{9,11},{10,... | collective-permute-start | bytes 417800 | tf_op jit(solution)/shard_map/ppermute | solution.py:334
  36.9 2.7 %collective-permute-done.9 = f32[256,256]{1,0:T(8,128)S(1)} collective-permute-done((f32[256,256]{1,0:T(8,128)S(1)}, f32[256,256]{1,0:T(8,128)S(1)}, u32[]{:S(2)}, u32[]{:S(2)}) %collective-permute-start.9) | collective-permute-done | bytes 262176 | tf_op jit(solution)/shard_map/ppermute | solution.py:334
  39.7 0.5 %collective-permute-start.10 = (f32[128,256]{1,0:T(8,128)S(1)}, f32[128,256]{1,0:T(8,128)S(1)}, u32[]{:S(2)}, u32[]{:S(2)}) collective-permute-start(f32[128,256]{1,0:T(8,128)S(1)} %slice.72), channel_id=1, source_target_pairs={{0,4},{1,3},{2,6},{3,1},{4,0},{5,7},{6,2},{7,5},{8,12},{9,11},{10,... | collective-permute-start | bytes 393224 | tf_op jit(solution)/shard_map/ppermute | solution.py:334
  40.2 1.3 %collective-permute-done.6 = f32[136,256]{1,0:T(8,128)S(1)} collective-permute-done((f32[136,256]{1,0:T(8,128)S(1)}, f32[136,256]{1,0:T(8,128)S(1)}, u32[]{:S(2)}, u32[]{:S(2)}) %collective-permute-start.6) | collective-permute-done | bytes 139296 | tf_op jit(solution)/shard_map/ppermute | solution.py:334
  41.6 2.0 %collective-permute-start.7 = (f32[72,256]{1,0:T(8,128)S(1)}, f32[72,256]{1,0:T(8,128)S(1)}, u32[]{:S(2)}, u32[]{:S(2)}) collective-permute-start(f32[72,256]{1,0:T(8,128)S(1)} %slice.68), channel_id=1, source_target_pairs={{0,8},{1,9},{2,10},{3,11},{4,12},{5,13},{6,14},{7,15},{8,0},{9,1},... | collective-permute-start | bytes 221192 | tf_op jit(solution)/shard_map/ppermute | solution.py:334
  43.6 1.1 %collective-permute-done.10 = f32[128,256]{1,0:T(8,128)S(1)} collective-permute-done((f32[128,256]{1,0:T(8,128)S(1)}, f32[128,256]{1,0:T(8,128)S(1)}, u32[]{:S(2)}, u32[]{:S(2)}) %collective-permute-start.10) | collective-permute-done | bytes 131104 | tf_op jit(solution)/shard_map/ppermute | solution.py:334
  44.8 2.6 %collective-permute-start.11 = (f32[64,256]{1,0:T(8,128)S(1)}, f32[64,256]{1,0:T(8,128)S(1)}, u32[]{:S(2)}, u32[]{:S(2)}) collective-permute-start(f32[64,256]{1,0:T(8,128)S(1)} %get-tuple-element.35), channel_id=1, source_target_pairs={{0,8},{1,9},{2,10},{3,11},{4,12},{5,13},{6,14},{7,15},{8,0},{9,1},... | collective-permute-start | bytes 196616 | tf_op jit(solution)/shard_map/ppermute | solution.py:334
  47.4 1.7 %collective-permute-done.7.refs_1_ = f32[72,256]{1,0:T(8,128)S(1)} collective-permute-done((f32[72,256]{1,0:T(8,128)S(1)}, f32[72,256]{1,0:T(8,128)S(1)}, u32[]{:S(2)}, u32[]{:S(2)}) %collective-permute-start.7) | collective-permute-done | bytes 73760 | tf_op jit(solution)/shard_map/ppermute | solution.py:334
  49.1 1.5 %collective-permute-done.11.refs_3_ = f32[64,256]{1,0:T(8,128)S(1)} collective-permute-done((f32[64,256]{1,0:T(8,128)S(1)}, f32[64,256]{1,0:T(8,128)S(1)}, u32[]{:S(2)}, u32[]{:S(2)}) %collective-permute-start.11) | collective-permute-done | bytes 65568 | tf_op jit(solution)/shard_map/ppermute | solution.py:334
  50.6 1.1 %finish.1 = f32[64,512]{1,0:T(8,128)} custom-call(f32[72,256]{1,0:T(8,128)S(1)} %pad_maximum_fusion.refs_0_, f32[72,256]{1,0:T(8,128)S(1)} %collective-permute-done.7.refs_1_, f32[64,256]{1,0:T(8,128)S(1)} %get-tuple-element.36.refs_2_, f32[64,256]{1,0:T(8,128)S(1)} %collective-permute-done.11.refs_3_, ...), custom_call_target="tpu_custom_call" | custom-call | tf_op jit(solution)/shard_map/finish/pallas_call | solution.py:311
  (21 shorter events, 0.3 us)
Async XLA Ops:
  0.0 0.7 %copy-start = (f32[1,4096]{1,0:T(1,128)S(1)}, f32[1,4096]{1,0:T(1,128)}, u32[]{:S(2)}) copy-start(f32[1,4096]{1,0:T(1,128)} %refs_3_.1) | copy-start | bytes 49156
  0.8 2.8 %collective-permute-start = (f32[1,128]{1,0:T(1,128)S(1)}, f32[1,128]{1,0:T(1,128)S(1)}, u32[]{:S(2)}, u32[]{:S(2)}) collective-permute-start(f32[1,128]{1,0:T(1,128)S(1)} %eig_sum.1.refs_0_), channel_id=1, source_target_pairs={{0,1},{1,0},{2,3},{3,2},{4,5},{5,4},{6,7},{7,6},{8,9},{9,8},{10,11... | collective-permute-start | bytes 1544 | tf_op jit(solution)/shard_map/ppermute | solution.py:338
  3.6 4.8 %collective-permute-start.1 = (f32[1,128]{1,0:T(1,128)S(1)}, f32[1,128]{1,0:T(1,128)S(1)}, u32[]{:S(2)}, u32[]{:S(2)}) collective-permute-start(f32[1,128]{1,0:T(1,128)S(1)} %add.30.after_ref), channel_id=1, source_target_pairs={{0,2},{1,3},{2,0},{3,1},{4,6},{5,7},{6,4},{7,5},{8,10},{9,11},{10,... | collective-permute-start | bytes 1544 | tf_op jit(solution)/shard_map/ppermute | solution.py:338
  8.4 5.0 %collective-permute-start.2 = (f32[1,128]{1,0:T(1,128)S(1)}, f32[1,128]{1,0:T(1,128)S(1)}, u32[]{:S(2)}, u32[]{:S(2)}) collective-permute-start(f32[1,128]{1,0:T(1,128)S(1)} %add.31.after_ref), channel_id=1, source_target_pairs={{0,4},{1,5},{2,6},{3,7},{4,0},{5,1},{6,2},{7,3},{8,12},{9,13},{10,... | collective-permute-start | bytes 1544 | tf_op jit(solution)/shard_map/ppermute | solution.py:338
  13.4 5.1 %collective-permute-start.3 = (f32[1,128]{1,0:T(1,128)S(1)}, f32[1,128]{1,0:T(1,128)S(1)}, u32[]{:S(2)}, u32[]{:S(2)}) collective-permute-start(f32[1,128]{1,0:T(1,128)S(1)} %add.32.after_ref), channel_id=1, source_target_pairs={{0,8},{1,9},{2,10},{3,11},{4,12},{5,13},{6,14},{7,15},{8,0},{9,1},... | collective-permute-start | bytes 1544 | tf_op jit(solution)/shard_map/ppermute | solution.py:338
  23.5 2.0 %collective-permute-start.4 = (f32[520,256]{1,0:T(8,128)S(1)}, f32[520,256]{1,0:T(8,128)S(1)}, u32[]{:S(2)}, u32[]{:S(2)}) collective-permute-start(f32[520,256]{1,0:T(8,128)S(1)} %get-tuple-element.31), channel_id=1, source_target_pairs={{0,1},{1,0},{2,3},{3,2},{4,5},{5,4},{6,7},{7,6},{8,9},{9,8},{10,11... | collective-permute-start | bytes 1597448 | tf_op jit(solution)/shard_map/ppermute | solution.py:334
  29.6 2.0 %collective-permute-start.8 = (f32[512,256]{1,0:T(8,128)S(1)}, f32[512,256]{1,0:T(8,128)S(1)}, u32[]{:S(2)}, u32[]{:S(2)}) collective-permute-start(f32[512,256]{1,0:T(8,128)S(1)} %get-tuple-element.33), channel_id=1, source_target_pairs={{0,1},{1,0},{2,3},{3,2},{4,5},{5,4},{6,7},{7,6},{8,9},{9,8},{10,11... | collective-permute-start | bytes 1572872 | tf_op jit(solution)/shard_map/ppermute | solution.py:334
  29.8 6.5 %collective-permute-start.5 = (f32[264,256]{1,0:T(8,128)S(1)}, f32[264,256]{1,0:T(8,128)S(1)}, u32[]{:S(2)}, u32[]{:S(2)}) collective-permute-start(f32[264,256]{1,0:T(8,128)S(1)} %slice.62.refs_0_), channel_id=1, source_target_pairs={{0,2},{1,5},{2,0},{3,7},{4,6},{5,1},{6,4},{7,3},{8,10},{9,13},{10,... | collective-permute-start | bytes 811016 | tf_op jit(solution)/shard_map/ppermute | solution.py:334
  31.7 7.9 %collective-permute-start.9 = (f32[256,256]{1,0:T(8,128)S(1)}, f32[256,256]{1,0:T(8,128)S(1)}, u32[]{:S(2)}, u32[]{:S(2)}) collective-permute-start(f32[256,256]{1,0:T(8,128)S(1)} %slice.70), channel_id=1, source_target_pairs={{0,2},{1,5},{2,0},{3,7},{4,6},{5,1},{6,4},{7,3},{8,10},{9,13},{10,... | collective-permute-start | bytes 786440 | tf_op jit(solution)/shard_map/ppermute | solution.py:334
  36.4 5.1 %collective-permute-start.6 = (f32[136,256]{1,0:T(8,128)S(1)}, f32[136,256]{1,0:T(8,128)S(1)}, u32[]{:S(2)}, u32[]{:S(2)}) collective-permute-start(f32[136,256]{1,0:T(8,128)S(1)} %slice.65), channel_id=1, source_target_pairs={{0,4},{1,3},{2,6},{3,1},{4,0},{5,7},{6,2},{7,5},{8,12},{9,11},{10,... | collective-permute-start | bytes 417800 | tf_op jit(solution)/shard_map/ppermute | solution.py:334
  39.7 5.1 %collective-permute-start.10 = (f32[128,256]{1,0:T(8,128)S(1)}, f32[128,256]{1,0:T(8,128)S(1)}, u32[]{:S(2)}, u32[]{:S(2)}) collective-permute-start(f32[128,256]{1,0:T(8,128)S(1)} %slice.72), channel_id=1, source_target_pairs={{0,4},{1,3},{2,6},{3,1},{4,0},{5,7},{6,2},{7,5},{8,12},{9,11},{10,... | collective-permute-start | bytes 393224 | tf_op jit(solution)/shard_map/ppermute | solution.py:334
  41.6 7.5 %collective-permute-start.7 = (f32[72,256]{1,0:T(8,128)S(1)}, f32[72,256]{1,0:T(8,128)S(1)}, u32[]{:S(2)}, u32[]{:S(2)}) collective-permute-start(f32[72,256]{1,0:T(8,128)S(1)} %slice.68), channel_id=1, source_target_pairs={{0,8},{1,9},{2,10},{3,11},{4,12},{5,13},{6,14},{7,15},{8,0},{9,1},... | collective-permute-start | bytes 221192 | tf_op jit(solution)/shard_map/ppermute | solution.py:334
  44.8 5.8 %collective-permute-start.11 = (f32[64,256]{1,0:T(8,128)S(1)}, f32[64,256]{1,0:T(8,128)S(1)}, u32[]{:S(2)}, u32[]{:S(2)}) collective-permute-start(f32[64,256]{1,0:T(8,128)S(1)} %get-tuple-element.35), channel_id=1, source_target_pairs={{0,8},{1,9},{2,10},{3,11},{4,12},{5,13},{6,14},{7,15},{8,0},{9,1},... | collective-permute-start | bytes 196616 | tf_op jit(solution)/shard_map/ppermute | solution.py:334

commit v3 on v2

v3 whole, which is shorter than its diff:
```python
import functools

import jax
import jax.numpy as jnp
from jax import lax
from jax.experimental import pallas as pl
from jax.experimental.pallas import tpu as pltpu
from jax.sharding import PartitionSpec as P

BF16 = jnp.bfloat16
F32 = jnp.float32
VMEM_LIMIT = 56 * 1024 * 1024
NN = (((1,), (0,)), ((), ()))
NT = (((1,), (1,)), ((), ()))


def dot(a, b, dims=NN):
    return lax.dot_general(a, b, dims, preferred_element_type=F32)


def iota(shape, dim):
    return lax.broadcasted_iota(jnp.int32, shape, dim)


def onehot(cond):
    return jnp.where(cond, 1.0, 0.0).astype(BF16)


def even_first(place, side):
    return place % (side // 2) * 2 + place // (side // 2)


def inner_weight(basis, side, pack):
    wide = side * pack
    rows = onehot(iota((wide, side), 0) // pack == iota((wide, side), 1))
    cols = onehot(iota((side, wide), 1) % side == iota((side, wide), 0))
    full = dot(dot(rows, basis, NT).astype(BF16), cols)
    keep = iota((wide, wide), 0) % pack == iota((wide, wide), 1) // side
    return jnp.where(keep, full, 0.0).astype(BF16)


def outer_weight(basis, side, pack):
    wide = side * pack
    rows = onehot(even_first(iota((wide, side), 0) % side, side) == iota((wide, side), 1))
    k = iota((side, wide), 1)
    cols = onehot(k // (pack * pack) * pack + k % pack == iota((side, wide), 0))
    full = dot(dot(rows, basis, NT).astype(BF16), cols)
    keep = iota((wide, wide), 0) // side == iota((wide, wide), 1) // pack % pack
    return jnp.where(keep, full, 0.0).astype(BF16)


def outer_weight_t(basis, side, pack):
    wide = side * pack
    k = iota((wide, side), 0)
    rows = onehot(k // (pack * pack) * pack + k % pack == iota((wide, side), 1))
    cols = onehot(even_first(iota((side, wide), 1) % side, side) == iota((side, wide), 0))
    full = dot(dot(rows, basis).astype(BF16), cols)
    keep = iota((wide, wide), 1) // side == iota((wide, wide), 0) // pack % pack
    return jnp.where(keep, full, 0.0).astype(BF16)


def halves(x_ref, weight, half_ref, side, pack):
    wide = side * pack
    groups = side // pack
    unit = pack * pack
    for g in range(groups):
        part = dot(weight, x_ref[:, g * wide : (g + 1) * wide], NT).astype(BF16)
        half_ref[:, g * unit : (g + 1) * unit, :] = part.reshape(groups, unit, part.shape[1])


def in_vmem(x):
    return pltpu.with_memory_space_constraint(x, pltpu.VMEM)


WHOLE = pl.BlockSpec(memory_space=pltpu.VMEM)
IN_HBM = pl.BlockSpec(memory_space=pltpu.HBM)
ANYWHERE = pl.BlockSpec(memory_space=pl.ANY)


def kernel_call(body, name, args, outs, scratch=(), specs=None, flops=0, limit=VMEM_LIMIT, aliases=None):
    specs = specs or [WHOLE] * len(args)
    place = {id(IN_HBM): pltpu.HBM, id(WHOLE): pltpu.VMEM}
    args = [
        pltpu.with_memory_space_constraint(a, place[id(s)]) if id(s) in place and a.size > 2048 or s is IN_HBM else a
        for a, s in zip(args, specs)
    ]
    return pl.pallas_call(
        body,
        out_shape=tuple(pltpu.VMEM(shape, dtype) for shape, dtype in outs),
        in_specs=specs,
        out_specs=tuple([WHOLE] * len(outs)),
        scratch_shapes=list(scratch),
        input_output_aliases=aliases or {},
        compiler_params=pltpu.CompilerParams(vmem_limit_bytes=limit),
        cost_estimate=pl.CostEstimate(flops=flops, bytes_accessed=0, transcendentals=0),
        name=name,
    )(*args)


def fetch(pairs, sems):
    copies = [pltpu.make_async_copy(src, dst, sems.at[i]) for i, (src, dst) in enumerate(pairs)]
    for copy in copies:
        copy.start()
    return copies


def beside_fetch(compute):
    pl.when(lax.axis_index("layer") >= 0)(compute)


def rows_from(x_any, x_ref, start, stop):
    return x_any.at[start:stop], x_ref.at[start:stop]


def swap_bits(ids, low, high, columns, where=True):
    train = ids.shape[1]
    block = iota(ids.shape, 1) // columns
    a, b = (block >> low) & 1, (block >> high) & 1
    shift = ((1 << high) - (1 << low)) * columns
    up, down = pltpu.roll(ids, train - shift, 1), pltpu.roll(ids, shift, 1)
    return jnp.where((a > b) & where, up, jnp.where((a < b) & where, down, ids))


def prepare_kernel(devices, side, pack, have, *refs):
    tids_ref, qids_ref, eig_ref, inner_ref, outer_ref, x_any = refs[1:7]
    sel_t_ref, sel_q_ref, eig_t_ref, w3_ref, w4_ref, w4t_ref, x_ref = refs[8:15]
    copies = fetch((rows_from(x_any, x_ref, have, x_ref.shape[0]),), refs[15])
    @beside_fetch
    def _():
        me = lax.axis_index("layer")
        train, queries = sel_t_ref.shape[0], sel_q_ref.shape[0]
        ids = jnp.broadcast_to(tids_ref[...], (8, train))
        lane = iota((8, train), 1)
        step = train // devices
        core = me % 2
        while step < train:
            bit = (lane // step) % 2
            other = jnp.where(bit == 0, pltpu.roll(ids, train - step, 1), pltpu.roll(ids, step, 1))
            ids = jnp.where(me % 2 == 1, other, ids)
            me = me // 2
            step *= 2
        columns = train // devices
        bits = devices.bit_length() - 1
        if bits > 2:
            ids = swap_bits(ids, 1, 2, columns, (core + lane // columns) % 2 == 1)
        for b in range(bits // 2):
            ids = swap_bits(ids, b, bits - 1 - b, columns)
        for s in range(0, train, 128):
            col = jnp.broadcast_to(ids[0:1, s : s + 128], (128, 128)).T
            for c in range(0, train, 128):
                sel_t_ref[s : s + 128, c : c + 128] = onehot(col == iota((128, 128), 1) + c)
        sel_q_ref[...] = onehot(iota((queries, queries), 0) == qids_ref[...])
        eig = jnp.concatenate([eig_ref[:, c : c + 2 * side] for c in range(0, side * side, 2 * side)], axis=0)
        eig = eig.T
        eig = jnp.concatenate([eig[:side], eig[side:]], axis=1)
        for j in range(side):
            eig_t_ref[:, j * side : (j + 1) * side] = eig[j : j + 1, :]
        w3_ref[...] = inner_weight(inner_ref[...], side, pack)
        w4_ref[...] = outer_weight(outer_ref[...], side, pack)
        w4t_ref[...] = outer_weight_t(outer_ref[...], side, pack)

    copies[-1].wait()


def prepare(after, tids, qids, eig, inner, outer, x, part, have, devices):
    train, queries, side = tids.shape[1], qids.shape[1], inner.shape[0]
    pack = 256 // side
    wide = side * pack
    return kernel_call(
        functools.partial(prepare_kernel, devices, side, pack, have),
        "prepare",
        (after, tids, qids, eig, inner, outer, x, part),
        [((train, train), BF16), ((queries, queries), BF16), (eig.shape, F32)]
        + [((wide, wide), BF16)] * 3
        + [(x.shape, BF16)],
        [pltpu.SemaphoreType.DMA((1,))],
        [ANYWHERE] + [WHOLE] * 5 + [IN_HBM, WHOLE],
        limit=6 << 20,
        aliases={7: 6},
    )


def query_kernel(side, ahead, after_ref, x_ref, w3_ref, next_any, out_ref, next_ref, last_ref, half_ref, sems):
    rows = next_ref.shape[0]
    copies = fetch((rows_from(next_any, next_ref, 0, rows), (next_any.at[rows : rows + ahead], last_ref.at[:ahead])), sems)
    @beside_fetch
    def _():
        pack = w3_ref.shape[0] // side
        wide = w3_ref.shape[0]
        groups, unit = side // pack, pack * pack
        w3 = w3_ref[...]
        queries = x_ref.shape[0]
        block = min(queries, 256)
        for r in range(0, queries + block, block):
            for g in range(groups):
                if r < queries:
                    part = dot(w3, x_ref[r : r + block, g * wide : (g + 1) * wide], NT).astype(BF16)
                    half_ref[:, g * unit : (g + 1) * unit, r : r + block] = part.reshape(groups, unit, block)
                if r:
                    out_ref[g, r - block : r, :] = half_ref[g, :, r - block : r].T

    for copy in copies:
        copy.wait()


def rotate_query(after, x, w3, upcoming, rows_next, ahead, side):
    rows, feat = x.shape
    wide = w3.shape[0]
    groups = feat // wide
    return kernel_call(
        functools.partial(query_kernel, side, ahead),
        "rotate_query",
        (after, x, w3, upcoming),
        [((groups, rows, wide), BF16), ((rows_next, feat), BF16), ((rows_next, feat), BF16)],
        [pltpu.VMEM((groups, wide, rows), BF16), pltpu.SemaphoreType.DMA((2,))],
        [ANYWHERE, WHOLE, WHOLE, IN_HBM],
        flops=2 * rows * feat * wide,
        limit=12 << 20,
    )


def rotate_rows(side, x_ref, w3_ref, w4_ref, out_ref, half_ref):
    halves(x_ref, w3_ref[...], half_ref, side, w3_ref.shape[0] // side)
    w4 = w4_ref[...]
    for g in range(out_ref.shape[0]):
        out_ref[g] = dot(w4, half_ref[g]).astype(BF16)


def train_kernel(side, after_ref, x_ref, w3_ref, w4_ref, out_ref, half_ref):
    rotate_rows(side, x_ref, w3_ref, w4_ref, out_ref, half_ref)


def train_fetch_kernel(side, have, after_ref, x_ref, w3_ref, w4_ref, next_any, part_ref, out_ref, next_ref, half_ref, sems):
    rows = next_ref.shape[0]
    copies = fetch(((next_any.at[rows + have :], next_ref.at[have:]),), sems)

    @beside_fetch
    def _():
        rotate_rows(side, x_ref, w3_ref, w4_ref, out_ref, half_ref)

    copies[0].wait()


def rotate_train(after, x, w3, w4, side, upcoming=None, part=None, have=0):
    rows, feat = x.shape
    wide = w3.shape[0]
    groups = feat // wide
    body, args, sems, extra = functools.partial(train_kernel, side), (), [], {}
    outs = [((groups, wide, rows), BF16)]
    specs = [ANYWHERE, WHOLE, WHOLE, WHOLE]
    if upcoming is not None:
        body, args = functools.partial(train_fetch_kernel, side, have), (upcoming, part)
        outs.append(((rows, feat), BF16))
        sems = [pltpu.SemaphoreType.DMA((1,))]
        specs += [IN_HBM, WHOLE]
        extra = {"aliases": {5: 1}}
    return kernel_call(
        body,
        "rotate_train",
        (after, x, w3, w4, *args),
        outs,
        [pltpu.VMEM((groups, wide, rows), BF16)] + sems,
        specs,
        flops=4 * rows * feat * wide,
        limit=12 << 20,
        **extra,
    )


def damped_queries(d_ref, hq_ref, w4t_ref, inv, start):
    queries = d_ref.shape[0]
    groups, _, wide = hq_ref.shape
    w4t = w4t_ref[...]
    for g in range(groups):
        d = dot(hq_ref[g, start : start + queries, :], w4t) * inv[:, g * wide : (g + 1) * wide]
        d_ref[:, g * wide : (g + 1) * wide] = d.astype(BF16)


def multiply(p_ref, d_ref, rt_ref, at, inv_cols=()):
    groups, wide, cols = rt_ref.shape
    rt = rt_ref[...].reshape(groups * wide, cols)
    sums = []
    for t in range(0, cols, 256):
        p = dot(d_ref[...], rt[:, t : t + 256])
        if inv_cols:
            sums += self_sums(rt_ref, inv_cols, t, 256)
        hi = p.astype(BF16)
        p_ref[0, :, at + t : at + t + 256] = hi
        p_ref[1, :, at + t : at + t + 256] = (p - hi.astype(F32)).astype(BF16)
    return sums


def select_rows(p_refs, sel_ref, start, out_ref, rows):
    at, got = 0, None
    for p_ref in p_refs:
        cols = p_ref.shape[2]
        pick = sel_ref[start : start + rows, at : at + cols]
        for i in range(2):
            part = dot(pick, p_ref[i], NT)
            got = part if got is None else got + part
        at += cols
    out_ref[:rows, :] = got


def self_sums(rt_ref, inv_cols, at, cols):
    sums = []
    for t in range(at, at + cols, 128):
        acc = jnp.zeros((8, 128), F32)
        for g, col in enumerate(inv_cols):
            r = rt_ref[g, :, t : t + 128].astype(F32)
            acc = acc + (r * r * col[...]).reshape(-1, 8, 128).sum(0)
        sums.append(acc.sum(0, keepdims=True))
    return sums


def on_lines(sums, queries):
    per = queries // 128
    tail = [jnp.concatenate(sums[i : i + per], axis=1) for i in range(0, len(sums), per)]
    tail += [jnp.zeros((1, queries), F32)] * (8 - len(tail))
    return jnp.concatenate(tail, axis=0)


def score_kernel(scale, rta_ref, rtb_ref, hq_ref, eig_ref, sum_ref, w4t_ref, sel_ref, sent_ref, p_ref, tail_ref, d_ref, inv_ref):
    inv = 1.0 / (eig_ref[...] + sum_ref[0:1, 0:1] * scale)
    damped_queries(d_ref, hq_ref, w4t_ref, inv, 0)
    groups, wide, _ = rta_ref.shape
    for g in range(groups):
        inv_ref[g] = jnp.broadcast_to(inv[:, g * wide : (g + 1) * wide], (128, wide)).T
    inv_cols = [inv_ref.at[g] for g in range(groups)]
    sums = multiply(p_ref, d_ref, rta_ref, 0, inv_cols)
    sums += multiply(p_ref, d_ref, rtb_ref, rta_ref.shape[2], inv_cols)
    half = sel_ref.shape[0] // 2
    select_rows((p_ref,), sel_ref, half, sent_ref, half)
    tail = on_lines(sums, sent_ref.shape[1])
    sent_ref[half:, :] = tail
    tail_ref[...] = tail


def partial_scores(rts, hq, eig, eig_sum, w4t, sel, scale, queries):
    train = sel.shape[0]
    feat = eig.shape[1]
    return kernel_call(
        functools.partial(score_kernel, scale),
        "scores_self",
        (*rts, hq, eig, eig_sum, w4t, sel),
        [((train // 2 + 8, queries), F32), ((2, queries, train), BF16), ((8, queries), F32)],
        [pltpu.VMEM((queries, feat), BF16), pltpu.VMEM((*rts[0].shape[:2], 128), F32)],
        limit=16 << 20,
    )


def score_first_kernel(scale, start, after_ref, rt_ref, hq_ref, eig_ref, sum_ref, w4t_ref, d_ref, p_ref):
    inv = 1.0 / (eig_ref[...] + sum_ref[0:1, 0:1] * scale)
    damped_queries(d_ref, hq_ref, w4t_ref, inv, start)
    multiply(p_ref, d_ref, rt_ref, 0)


def score_first(after, rt, hq, eig, eig_sum, w4t, scale, start, queries):
    feat, cols = eig.shape[1], rt.shape[2]
    return kernel_call(
        functools.partial(score_first_kernel, scale, start),
        "scores_first",
        (after, rt, hq, eig, eig_sum, w4t),
        [((queries, feat), BF16), ((2, queries, cols), BF16)],
        (),
        [ANYWHERE] + [WHOLE] * 5,
        limit=8 << 20,
    )


def score_second_kernel(after_ref, rt_ref, d_ref, pa_ref, sel_ref, sent_ref, p_ref):
    multiply(p_ref, d_ref, rt_ref, 0)
    half = sel_ref.shape[0] // 2
    select_rows((pa_ref, p_ref), sel_ref, half, sent_ref, half)


def score_second(after, rt, d, pa, sel):
    queries = d.shape[0]
    train, cols = sel.shape[0], rt.shape[2]
    return kernel_call(
        score_second_kernel,
        "scores_second",
        (after, rt, d, pa, sel),
        [((train // 2, queries), F32), ((2, queries, cols), BF16)],
        (),
        [ANYWHERE] + [WHOLE] * 4,
        limit=8 << 20,
    )


def keep_kernel(parts, *refs):
    sel_ref, out_ref = refs[parts + 1], refs[-1]
    half = sel_ref.shape[0] // 2
    select_rows(refs[1 : parts + 1], sel_ref, 0, out_ref, half)
    if len(refs) > parts + 3:
        out_ref[half:, :] = refs[parts + 2][...]


def keep_rows(after, ps, sel, tail=None):
    queries = ps[0].shape[1]
    args = (after, *ps, sel) + (() if tail is None else (tail,))
    return kernel_call(
        functools.partial(keep_kernel, len(ps)),
        "keep_rows",
        args,
        [((sel.shape[0] // 2 + (0 if tail is None else 8), queries), F32)],
        (),
        [ANYWHERE] + [WHOLE] * (len(args) - 1),
        limit=8 << 20,
    )[0]


def pick_queries(scaled, sel):
    hi = scaled.astype(BF16)
    rest = scaled - hi.astype(F32)
    mid = rest.astype(BF16)
    low = (rest - mid.astype(F32)).astype(BF16)
    return dot(hi, sel) + dot(mid, sel) + dot(low, sel)


def finish_first_kernel(mine_ref, got_ref, sel_t_ref, sel_q_ref, out_ref, norm_ref):
    columns = out_ref.shape[0]
    width = mine_ref.shape[1]
    total = mine_ref[...] + got_ref[...]
    train = sel_t_ref.shape[1]
    self_row = jnp.concatenate([total[columns + i : columns + i + 1] for i in range(train // width)], axis=1)
    own = sel_t_ref[: max(columns, 16), :].astype(F32)[:columns]
    norm = lax.rsqrt((own * self_row).sum(1, keepdims=True))
    norm_ref[...] = jnp.broadcast_to(norm, norm_ref.shape)
    out_ref[...] = pick_queries(total[:columns] * norm, sel_q_ref[:width, :])


def finish_second_kernel(mine_ref, got_ref, first_ref, norm_ref, sel_q_ref, out_ref):
    width = mine_ref.shape[1]
    total = (mine_ref[...] + got_ref[...]) * norm_ref[:, 0:1]
    out_ref[...] = first_ref[...] + pick_queries(total, sel_q_ref[sel_q_ref.shape[0] - width :, :])


def finish(first, second, sel_t, sel_q, columns):
    queries = sel_q.shape[0]
    out, norm = kernel_call(
        finish_first_kernel,
        "finish_first",
        (*first, sel_t, sel_q),
        [((columns, queries), F32), ((columns, 128), F32)],
        limit=4 << 20,
    )
    args = [in_vmem(a) for a in (*second, out, norm, sel_q)]
    return pl.pallas_call(
        finish_second_kernel,
        out_shape=jax.ShapeDtypeStruct((columns, queries), F32),
        in_specs=[WHOLE] * len(args),
        out_specs=WHOLE,
        compiler_params=pltpu.CompilerParams(vmem_limit_bytes=4 << 20),
        name="finish_second",
    )(*args)


def sum_kernel(ahead, count, *refs):
    smalls, x_any, out_ref, held, part_ref, sems = refs[:count], refs[count], refs[count + 1], refs[count + 2 : -2], refs[-2], refs[-1]
    copies = fetch((*zip(smalls, held), rows_from(x_any, part_ref, 0, ahead)), sems)
    copies[0].wait()
    x_ref = held[0]
    out_ref[...] = jnp.broadcast_to(jnp.sum(x_ref[...], axis=1, keepdims=True), out_ref.shape)
    for copy in copies[1:]:
        copy.wait()


def next_halves(mine, got, rows):
    total = mine + got
    rows //= 2
    return jnp.concatenate([total[:rows], total[2 * rows :]]), total[rows:]


def halving_step(x, step, devices):
    swap = {1: 2, 2: 1} if devices > 4 else {}
    pairs = [(i, i ^ (1 << (swap.get(step, step) if i % 2 else step))) for i in range(devices)]
    return lax.ppermute(x, "layer", pairs)


def exchange(x, bit, devices):
    return lax.ppermute(x, "layer", [(i, i ^ bit) for i in range(devices)])


def shards(query_pool, train_store, query_ids, train_ids, out_basis, in_basis, eigenvalues):
    devices = lax.axis_size("layer")
    bits = devices.bit_length() - 1
    train = train_store.shape[0]
    queries = query_pool.shape[0]
    side = out_basis.shape[1]
    columns = train // devices
    inner, outer = in_basis[0], out_basis[0]

    scale = 0.1 / (eigenvalues.shape[1] * devices)
    tids, qids = train_ids.reshape(1, train), query_ids.reshape(1, queries)
    xq, xt = query_pool.reshape(queries, -1), train_store.reshape(train, -1)

    half = train // 2
    have_q, have_b = 128, 64
    smalls = (eigenvalues, tids, qids, inner, outer)
    eig_sum, eig_v, tids_v, qids_v, inner_v, outer_v, xq_part = kernel_call(
        functools.partial(sum_kernel, have_q, len(smalls)),
        "eig_sum",
        (*smalls, xq),
        [((1, 128), F32)] + [(a.shape, a.dtype) for a in smalls] + [(xq.shape, BF16)],
        [pltpu.SemaphoreType.DMA((6,))],
        [IN_HBM] * 6,
        limit=1 << 20,
    )
    for b in range(bits):
        got = exchange(eig_sum, 1 << b, devices)
        if b == 0:
            sel_t, sel_q, eig, w3, w4, w4t, xq = prepare(
                eig_sum, tids_v, qids_v, eig_v, inner_v, outer_v, xq, xq_part, have_q, devices
            )
        elif b == 1:
            hq, xa, xb = rotate_query(eig_sum, xq, w3, xt, half, have_b, side)
        elif b == 2:
            rta, xb = rotate_train(eig_sum, xa, w3, w4, side, xt, xb, have_b)
        elif b == 3:
            (rtb,) = rotate_train(eig_sum, xb, w3, w4, side)
        eig_sum = eig_sum + got

    chunk = queries // 2
    sent_a, p_a, tail = partial_scores((rta, rtb), hq, eig, eig_sum, w4t, sel_t, scale, chunk)
    got_a = halving_step(sent_a, 0, devices)
    mine_a = keep_rows(sent_a, [p_a], sel_t, tail)
    d, p_b1 = score_first(sent_a, rta, hq, eig, eig_sum, w4t, scale, chunk, chunk)
    mine_a, sent_a = next_halves(mine_a, got_a, half)
    sent_b, p_b2 = score_second(sent_a, rtb, d, p_b1, sel_t)
    got_b = halving_step(sent_b, 0, devices)
    mine_b = keep_rows(sent_b, [p_b1, p_b2], sel_t)
    got_a = halving_step(sent_a, 1, devices)
    pairs = [(mine_a, got_a), (mine_b, got_b)]
    for b in range(1, bits):
        for c in range(2):
            step = b + 1 - c
            if step < bits:
                mine, sent = next_halves(*pairs[c], half >> (step - 1))
                pairs[c] = (mine, halving_step(sent, step, devices))
    return finish(*pairs, sel_t, sel_q, columns).T


def solution(mesh):
    placed = (
        P("grp", "layer", None),
        P("grp", "layer", None),
        P("grp"),
        P("grp"),
        P("layer", None, None),
        P("layer", None, None),
        P("layer", None),
    )
    return jax.shard_map(
        shards, mesh=mesh, in_specs=placed, out_specs=P("grp", "layer"), check_vma=False
    )
```

time: 52 us -> 50.9 us (0.979)
  waiting for transfers between devices: 14 us -> 12.2 us
  Pallas kernels: 20.5 us -> 21.6 us
  local copies, waits for them, and re-layouts: 0.84 us -> 0.12 us
    ppermute x8, waiting for transfers between devices: 14 us -> 12.2 us  [halving_step(): return lax.ppermute(x, 'layer', pairs)]
    pallas_call x7 -> x11, Pallas kernels: 19.3 us -> 20.7 us  [kernel_call(): pl.pallas_call(body, out_shape=tuple((pltpu.VMEM(shape, dtype) for shape,...]
    unnamed x2 -> x0, local copies, waits for them, and re-layouts: 0.72 us -> none
  transfers between devices with their start and end apart: 12 -> 12, of which waited for: 8 -> 6; matrix products, arithmetic and copies ran while one was open for 1% -> 1% of each run, Pallas kernels for 20% -> 26%
where the time goes in v3:
time: 50.9 us; the launch traced here: 50.6 us
  Pallas kernels  21.6 us (42%)
  starting transfers between devices  16.1 us (32%)
  waiting for transfers between devices  12.2 us (24%)
    pallas_call x11, Pallas kernels, kernel_call(): pl.pallas_call(body, out_shape=tuple((pltpu.VMEM(shape, dtype) for shape,...  20.7 us
    ppermute x8, waiting for transfers between devices, halving_step(): return lax.ppermute(x, 'layer', pairs)  12.2 us
    ppermute x8, starting transfers between devices, halving_step(): return lax.ppermute(x, 'layer', pairs)  8.67 us
    ppermute x4, starting transfers between devices, exchange(): return lax.ppermute(x, 'layer', [(i, i ^ bit) for i in range(devices)])  7.42 us
  transfers between devices with their start and end apart: 12, of which 6 were waited for; matrix products, arithmetic and copies ran while one was open for 1% of the time, Pallas kernels for 26%

profile of v3, /device:TPU:0, one launch (start us, length us, event | category | flops | bytes accessed | tf_op | source)
XLA Modules:
  0.0 50.6 jit_solution(5512656722775921216)
XLA Ops:
  0.0 1.4 %eig_sum.1 = (f32[1,128]{1,0:T(1,128)S(1)}, f32[1,4096]{1,0:T(1,128)S(1)}, s32[1,1024]{1,0:T(1,128)S(1)}, s32[1,512]{1,0:T(1,128)S(1)}, bf16[64,64]{1,0:T(8,128)...) custom-call(f32[1,4096]{1,0:T(1,128)} %refs_0_.1, s32[1,1024]{1,0:T(1,128)} %bitcast.13, ...), custom_call_target="tpu_custom_call" | custom-call | tf_op jit(solution)/shard_map/eig_sum/pallas_call | solution.py:87
  1.4 0.5 %collective-permute-start = (f32[1,128]{1,0:T(1,128)S(1)}, f32[1,128]{1,0:T(1,128)S(1)}, u32[]{:S(2)}, u32[]{:S(2)}) collective-permute-start(f32[1,128]{1,0:T(1,128)S(1)} %get-tuple-element.33.refs_0_), channel_id=1, source_target_pairs={{0,1},{1,0},{2,3},{3,2},{4,5},{5,4},{6,7},{7,6},{8,9},{9,8},{10,11... | collective-permute-start | bytes 1544 | tf_op jit(solution)/shard_map/ppermute | solution.py:482
  1.9 1.9 %prepare.1 = (bf16[1024,1024]{1,0:T(8,128)(2,1)S(1)}, bf16[512,512]{1,0:T(8,128)(2,1)S(1)}, f32[1,4096]{1,0:T(1,128)S(1)}, bf16[256,256]{1,0:T(8,128)(2,1)S(1)},...) custom-call(f32[1,128]{1,0:T(1,128)S(1)} %get-tuple-element.33.refs_, ...), custom_call_target="tpu_custom_call", output_to_operand_aliasing={{6}: (7, {})} | custom-call | tf_op jit(solution)/shard_map/prepare/pallas_call | solution.py:87
  3.8 0.0 collective-permute-done
  3.8 2.6 %collective-permute-start.1 = (f32[1,128]{1,0:T(1,128)S(1)}, f32[1,128]{1,0:T(1,128)S(1)}, u32[]{:S(2)}, u32[]{:S(2)}) collective-permute-start(f32[1,128]{1,0:T(1,128)S(1)} %add.30.after_ref), channel_id=1, source_target_pairs={{0,2},{1,3},{2,0},{3,1},{4,6},{5,7},{6,4},{7,5},{8,10},{9,11},{10,... | collective-permute-start | bytes 1544 | tf_op jit(solution)/shard_map/ppermute | solution.py:482
  6.4 2.3 %rotate_query.1 = (bf16[16,512,256]{2,1,0:T(8,128)(2,1)S(1)}, bf16[512,4096]{1,0:T(8,128)(2,1)S(1)}, bf16[512,4096]{1,0:T(8,128)(2,1)S(1)}) custom-call(f32[1,128]{1,0:T(1,128)S(1)} %add.30.after_ref, bf16[512,4096]{1,0:T(8,128)(2,1)S(1)} %get-tuple-element.40.x_ref, bf16[256,256]{1,0:T(8,128)(2,1)S(1)} %get-tuple-element.41.w3_ref, bf16[1024,4096]{1,0:T(8,128)(2,1)} %bitcast.7), custom_call_target="tpu_custom_call" | custom-call | flops 1073741824 | tf_op jit(solution)/shard_map/rotate_query/pallas_call | solution.py:87
  8.7 0.0 collective-permute-done.1
  8.8 1.6 %collective-permute-start.2 = (f32[1,128]{1,0:T(1,128)S(1)}, f32[1,128]{1,0:T(1,128)S(1)}, u32[]{:S(2)}, u32[]{:S(2)}) collective-permute-start(f32[1,128]{1,0:T(1,128)S(1)} %add.31.after_ref), channel_id=1, source_target_pairs={{0,4},{1,5},{2,6},{3,7},{4,0},{5,1},{6,2},{7,3},{8,12},{9,13},{10,... | collective-permute-start | bytes 1544 | tf_op jit(solution)/shard_map/ppermute | solution.py:482
  10.4 2.6 %rotate_train.2 = (bf16[16,256,512]{2,1,0:T(8,128)(2,1)S(1)}, bf16[512,4096]{1,0:T(8,128)(2,1)S(1)}) custom-call(f32[1,128]{1,0:T(1,128)S(1)} %add.31.after_ref, bf16[512,4096]{1,0:T(8,128)(2,1)S(1)} %get-tuple-element.42.x_ref, bf16[256,256]{1,0:T(8,128)(2,1)S(1)} %get-tuple-element.41.w3_ref, ...), custom_call_target="tpu_custom_call", output_to_operand_aliasing={{1}: (5, {})} | custom-call | flops 2147483648 | tf_op jit(solution)/shard_map/rotate_train/pallas_call | solution.py:87
  13.1 0.0 collective-permute-done.2
  13.1 2.7 %collective-permute-start.3 = (f32[1,128]{1,0:T(1,128)S(1)}, f32[1,128]{1,0:T(1,128)S(1)}, u32[]{:S(2)}, u32[]{:S(2)}) collective-permute-start(f32[1,128]{1,0:T(1,128)S(1)} %add.32.after_ref), channel_id=1, source_target_pairs={{0,8},{1,9},{2,10},{3,11},{4,12},{5,13},{6,14},{7,15},{8,0},{9,1},... | collective-permute-start | bytes 1544 | tf_op jit(solution)/shard_map/ppermute | solution.py:482
  15.7 2.5 %rotate_train.3.rtb_ref.rt_ref = bf16[16,256,512]{2,1,0:T(8,128)(2,1)S(1)} custom-call(f32[1,128]{1,0:T(1,128)S(1)} %add.32.after_ref, bf16[512,4096]{1,0:T(8,128)(2,1)S(1)} %get-tuple-element.46.x_ref, bf16[256,256]{1,0:T(8,128)(2,1)S(1)} %get-tuple-element.41.w3_ref, bf16[256,256]{1,0:T(8,128)(2,1)S(1)} %get-tuple-element.43.w4_ref), custom_call_target="tpu_custom_call" | custom-call | flops 2147483648 | tf_op jit(solution)/shard_map/rotate_train/pallas_call | solution.py:87
  18.2 0.0 collective-permute-done.3
  18.2 4.5 %scores_self.1 = (f32[520,256]{1,0:T(8,128)S(1)}, bf16[2,256,1024]{2,1,0:T(8,128)(2,1)S(1)}, f32[8,256]{1,0:T(8,128)S(1)}) custom-call(bf16[16,256,512]{2,1,0:T(8,128)(2,1)S(1)} %get-tuple-element.45.rta_ref.rt_ref, bf16[16,256,512]{2,1,0:T(8,128)(2,1)S(1)} %rotate_train.3.rtb_ref.rt_ref, bf16[16,512,256]{2,1,0:T(8,128)(2,1)S(1)} %get-tuple-element.47.hq_ref, ...), custom_call_target="tpu_custom_call" | custom-call | tf_op jit(solution)/shard_map/scores_self/pallas_call | solution.py:87
  22.7 0.1 collective-permute-start.4
  22.8 1.8 %scores_first.1 = (bf16[256,4096]{1,0:T(8,128)(2,1)S(1)}, bf16[2,256,512]{2,1,0:T(8,128)(2,1)S(1)}) custom-call(f32[520,256]{1,0:T(8,128)S(1)} %get-tuple-element.51.refs_0_.after_ref, bf16[16,256,512]{2,1,0:T(8,128)(2,1)S(1)} %get-tuple-element.45.rta_ref.rt_ref, bf16[16,512,256]{2,1,0:T(8,128)(2,1)S(1)} %get-tuple-element.47.hq_ref, ...), custom_call_target="tpu_custom_call" | custom-call | tf_op jit(solution)/shard_map/scores_first/pallas_call | solution.py:87
  24.6 0.7 %keep_rows.2 = f32[520,256]{1,0:T(8,128)S(1)} custom-call(f32[520,256]{1,0:T(8,128)S(1)} %get-tuple-element.51.refs_0_.after_ref, bf16[2,256,1024]{2,1,0:T(8,128)(2,1)S(1)} %get-tuple-element.52.refs_1_, bf16[1024,1024]{1,0:T(8,128)(2,1)S(1)} %get-tuple-element.50.sel_ref.refs_2_.refs_3_.sel_t_ref, f32[8,256]{1,0:T(8,128)S(1)} %get-tuple-element.53.refs_3_), custom_call_target="tpu_custom_call" | custom-call | tf_op jit(solution)/shard_map/keep_rows/pallas_call | solution.py:87
  25.4 0.0 collective-permute-done.4
  25.4 0.1 add.34
  25.5 1.9 %scores_second.1 = (f32[512,256]{1,0:T(8,128)S(1)}, bf16[2,256,512]{2,1,0:T(8,128)(2,1)S(1)}) custom-call(f32[264,256]{1,0:T(8,128)S(1)} %slice.60.after_ref, bf16[16,256,512]{2,1,0:T(8,128)(2,1)S(1)} %rotate_train.3.rtb_ref.rt_ref, bf16[256,4096]{1,0:T(8,128)(2,1)S(1)} %get-tuple-element.54.d_ref, ...), custom_call_target="tpu_custom_call" | custom-call | tf_op jit(solution)/shard_map/scores_second/pallas_call | solution.py:87
  27.4 0.6 %collective-permute-start.5 = (f32[512,256]{1,0:T(8,128)S(1)}, f32[512,256]{1,0:T(8,128)S(1)}, u32[]{:S(2)}, u32[]{:S(2)}) collective-permute-start(f32[512,256]{1,0:T(8,128)S(1)} %get-tuple-element.56.refs_0_), channel_id=1, source_target_pairs={{0,1},{1,0},{2,3},{3,2},{4,5},{5,4},{6,7},{7,6},{8,9},{9,8},{10,11... | collective-permute-start | bytes 1572872 | tf_op jit(solution)/shard_map/ppermute | solution.py:478
  28.0 1.1 %collective-permute-start.9 = (f32[264,256]{1,0:T(8,128)S(1)}, f32[264,256]{1,0:T(8,128)S(1)}, u32[]{:S(2)}, u32[]{:S(2)}) collective-permute-start(f32[264,256]{1,0:T(8,128)S(1)} %slice.60.after_ref), channel_id=1, source_target_pairs={{0,2},{1,5},{2,0},{3,7},{4,6},{5,1},{6,4},{7,3},{8,10},{9,13},{10,... | collective-permute-start | bytes 811016 | tf_op jit(solution)/shard_map/ppermute | solution.py:478
  29.1 0.7 %keep_rows.3 = f32[512,256]{1,0:T(8,128)S(1)} custom-call(f32[512,256]{1,0:T(8,128)S(1)} %get-tuple-element.56.refs_0_, bf16[2,256,512]{2,1,0:T(8,128)(2,1)S(1)} %get-tuple-element.55.pa_ref.refs_1_, bf16[2,256,512]{2,1,0:T(8,128)(2,1)S(1)} %get-tuple-element.57.refs_2_, bf16[1024,1024]{1,0:T(8,128)(2,1)S(1)} %get-tuple-element.50.sel_ref.refs_2_.refs_3_.sel_t_ref), custom_call_target="tpu_custom_call" | custom-call | tf_op jit(solution)/shard_map/keep_rows/pallas_call | solution.py:87
  29.9 0.0 collective-permute-done.5
  29.9 0.1 add.35
  30.0 1.0 %collective-permute-start.6 = (f32[256,256]{1,0:T(8,128)S(1)}, f32[256,256]{1,0:T(8,128)S(1)}, u32[]{:S(2)}, u32[]{:S(2)}) collective-permute-start(f32[256,256]{1,0:T(8,128)S(1)} %slice.62), channel_id=1, source_target_pairs={{0,2},{1,5},{2,0},{3,7},{4,6},{5,1},{6,4},{7,3},{8,10},{9,13},{10,... | collective-permute-start | bytes 786440 | tf_op jit(solution)/shard_map/ppermute | solution.py:478
  31.0 3.5 %collective-permute-done.9 = f32[264,256]{1,0:T(8,128)S(1)} collective-permute-done((f32[264,256]{1,0:T(8,128)S(1)}, f32[264,256]{1,0:T(8,128)S(1)}, u32[]{:S(2)}, u32[]{:S(2)}) %collective-permute-start.9) | collective-permute-done | bytes 270368 | tf_op jit(solution)/shard_map/ppermute | solution.py:478
  34.5 0.9 %collective-permute-start.10 = (f32[136,256]{1,0:T(8,128)S(1)}, f32[136,256]{1,0:T(8,128)S(1)}, u32[]{:S(2)}, u32[]{:S(2)}) collective-permute-start(f32[136,256]{1,0:T(8,128)S(1)} %slice.71), channel_id=1, source_target_pairs={{0,4},{1,3},{2,6},{3,1},{4,0},{5,7},{6,2},{7,5},{8,12},{9,11},{10,... | collective-permute-start | bytes 417800 | tf_op jit(solution)/shard_map/ppermute | solution.py:478
  35.4 2.6 %collective-permute-done.6 = f32[256,256]{1,0:T(8,128)S(1)} collective-permute-done((f32[256,256]{1,0:T(8,128)S(1)}, f32[256,256]{1,0:T(8,128)S(1)}, u32[]{:S(2)}, u32[]{:S(2)}) %collective-permute-start.6) | collective-permute-done | bytes 262176 | tf_op jit(solution)/shard_map/ppermute | solution.py:478
  38.1 0.9 %collective-permute-start.7 = (f32[128,256]{1,0:T(8,128)S(1)}, f32[128,256]{1,0:T(8,128)S(1)}, u32[]{:S(2)}, u32[]{:S(2)}) collective-permute-start(f32[128,256]{1,0:T(8,128)S(1)} %slice.64), channel_id=1, source_target_pairs={{0,4},{1,3},{2,6},{3,1},{4,0},{5,7},{6,2},{7,5},{8,12},{9,11},{10,... | collective-permute-start | bytes 393224 | tf_op jit(solution)/shard_map/ppermute | solution.py:478
  38.9 0.7 %collective-permute-done.10 = f32[136,256]{1,0:T(8,128)S(1)} collective-permute-done((f32[136,256]{1,0:T(8,128)S(1)}, f32[136,256]{1,0:T(8,128)S(1)}, u32[]{:S(2)}, u32[]{:S(2)}) %collective-permute-start.10) | collective-permute-done | bytes 139296 | tf_op jit(solution)/shard_map/ppermute | solution.py:478
  39.7 2.0 %collective-permute-start.11 = (f32[72,256]{1,0:T(8,128)S(1)}, f32[72,256]{1,0:T(8,128)S(1)}, u32[]{:S(2)}, u32[]{:S(2)}) collective-permute-start(f32[72,256]{1,0:T(8,128)S(1)} %slice.74), channel_id=1, source_target_pairs={{0,8},{1,9},{2,10},{3,11},{4,12},{5,13},{6,14},{7,15},{8,0},{9,1},... | collective-permute-start | bytes 221192 | tf_op jit(solution)/shard_map/ppermute | solution.py:478
  41.7 1.9 %collective-permute-done.7 = f32[128,256]{1,0:T(8,128)S(1)} collective-permute-done((f32[128,256]{1,0:T(8,128)S(1)}, f32[128,256]{1,0:T(8,128)S(1)}, u32[]{:S(2)}, u32[]{:S(2)}) %collective-permute-start.7) | collective-permute-done | bytes 131104 | tf_op jit(solution)/shard_map/ppermute | solution.py:478
  43.7 2.2 %collective-permute-start.8 = (f32[64,256]{1,0:T(8,128)S(1)}, f32[64,256]{1,0:T(8,128)S(1)}, u32[]{:S(2)}, u32[]{:S(2)}) collective-permute-start(f32[64,256]{1,0:T(8,128)S(1)} %get-tuple-element.61), channel_id=1, source_target_pairs={{0,8},{1,9},{2,10},{3,11},{4,12},{5,13},{6,14},{7,15},{8,0},{9,1},... | collective-permute-start | bytes 196616 | tf_op jit(solution)/shard_map/ppermute | solution.py:478
  45.9 1.3 %collective-permute-done.11.got_ref = f32[72,256]{1,0:T(8,128)S(1)} collective-permute-done((f32[72,256]{1,0:T(8,128)S(1)}, f32[72,256]{1,0:T(8,128)S(1)}, u32[]{:S(2)}, u32[]{:S(2)}) %collective-permute-start.11) | collective-permute-done | bytes 73760 | tf_op jit(solution)/shard_map/ppermute | solution.py:478
  47.2 0.3 finish_first.1
  47.6 2.1 %collective-permute-done.8.got_ref = f32[64,256]{1,0:T(8,128)S(1)} collective-permute-done((f32[64,256]{1,0:T(8,128)S(1)}, f32[64,256]{1,0:T(8,128)S(1)}, u32[]{:S(2)}, u32[]{:S(2)}) %collective-permute-start.8) | collective-permute-done | bytes 65568 | tf_op jit(solution)/shard_map/ppermute | solution.py:478
  49.7 1.0 %finish_second.1 = f32[64,512]{1,0:T(8,128)} custom-call(f32[64,256]{1,0:T(8,128)S(1)} %get-tuple-element.62.mine_ref, f32[64,256]{1,0:T(8,128)S(1)} %collective-permute-done.8.got_ref, f32[64,512]{1,0:T(8,128)S(1)} %get-tuple-element.59.first_ref, f32[64,128]{1,0:T(8,128)S(1)} %get-tuple-element.60.norm_ref, bf16[512,512]{1,0:T(8,128)(2,1)S(1)} %get-tuple-element.58.sel_q_ref), custom_call_target="tpu_custom_call" | custom-call | tf_op jit(solution)/shard_map/finish_second/pallas_call | solution.py:449
  (21 shorter events, 0.3 us)
Async XLA Ops:
  1.4 2.4 %collective-permute-start = (f32[1,128]{1,0:T(1,128)S(1)}, f32[1,128]{1,0:T(1,128)S(1)}, u32[]{:S(2)}, u32[]{:S(2)}) collective-permute-start(f32[1,128]{1,0:T(1,128)S(1)} %get-tuple-element.33.refs_0_), channel_id=1, source_target_pairs={{0,1},{1,0},{2,3},{3,2},{4,5},{5,4},{6,7},{7,6},{8,9},{9,8},{10,11... | collective-permute-start | bytes 1544 | tf_op jit(solution)/shard_map/ppermute | solution.py:482
  3.8 4.9 %collective-permute-start.1 = (f32[1,128]{1,0:T(1,128)S(1)}, f32[1,128]{1,0:T(1,128)S(1)}, u32[]{:S(2)}, u32[]{:S(2)}) collective-permute-start(f32[1,128]{1,0:T(1,128)S(1)} %add.30.after_ref), channel_id=1, source_target_pairs={{0,2},{1,3},{2,0},{3,1},{4,6},{5,7},{6,4},{7,5},{8,10},{9,11},{10,... | collective-permute-start | bytes 1544 | tf_op jit(solution)/shard_map/ppermute | solution.py:482
  8.8 4.3 %collective-permute-start.2 = (f32[1,128]{1,0:T(1,128)S(1)}, f32[1,128]{1,0:T(1,128)S(1)}, u32[]{:S(2)}, u32[]{:S(2)}) collective-permute-start(f32[1,128]{1,0:T(1,128)S(1)} %add.31.after_ref), channel_id=1, source_target_pairs={{0,4},{1,5},{2,6},{3,7},{4,0},{5,1},{6,2},{7,3},{8,12},{9,13},{10,... | collective-permute-start | bytes 1544 | tf_op jit(solution)/shard_map/ppermute | solution.py:482
  13.1 5.1 %collective-permute-start.3 = (f32[1,128]{1,0:T(1,128)S(1)}, f32[1,128]{1,0:T(1,128)S(1)}, u32[]{:S(2)}, u32[]{:S(2)}) collective-permute-start(f32[1,128]{1,0:T(1,128)S(1)} %add.32.after_ref), channel_id=1, source_target_pairs={{0,8},{1,9},{2,10},{3,11},{4,12},{5,13},{6,14},{7,15},{8,0},{9,1},... | collective-permute-start | bytes 1544 | tf_op jit(solution)/shard_map/ppermute | solution.py:482
  22.7 2.7 %collective-permute-start.4 = (f32[520,256]{1,0:T(8,128)S(1)}, f32[520,256]{1,0:T(8,128)S(1)}, u32[]{:S(2)}, u32[]{:S(2)}) collective-permute-start(f32[520,256]{1,0:T(8,128)S(1)} %get-tuple-element.51.refs_0_.after_ref), channel_id=1, source_target_pairs={{0,1},{1,0},{2,3},{3,2},{4,5},{5,4},{6,7},{7,6},{8,9},{9,8},{10,11... | collective-permute-start | bytes 1597448 | tf_op jit(solution)/shard_map/ppermute | solution.py:478
  27.4 2.4 %collective-permute-start.5 = (f32[512,256]{1,0:T(8,128)S(1)}, f32[512,256]{1,0:T(8,128)S(1)}, u32[]{:S(2)}, u32[]{:S(2)}) collective-permute-start(f32[512,256]{1,0:T(8,128)S(1)} %get-tuple-element.56.refs_0_), channel_id=1, source_target_pairs={{0,1},{1,0},{2,3},{3,2},{4,5},{5,4},{6,7},{7,6},{8,9},{9,8},{10,11... | collective-permute-start | bytes 1572872 | tf_op jit(solution)/shard_map/ppermute | solution.py:478
  28.0 6.5 %collective-permute-start.9 = (f32[264,256]{1,0:T(8,128)S(1)}, f32[264,256]{1,0:T(8,128)S(1)}, u32[]{:S(2)}, u32[]{:S(2)}) collective-permute-start(f32[264,256]{1,0:T(8,128)S(1)} %slice.60.after_ref), channel_id=1, source_target_pairs={{0,2},{1,5},{2,0},{3,7},{4,6},{5,1},{6,4},{7,3},{8,10},{9,13},{10,... | collective-permute-start | bytes 811016 | tf_op jit(solution)/shard_map/ppermute | solution.py:478
  30.0 8.0 %collective-permute-start.6 = (f32[256,256]{1,0:T(8,128)S(1)}, f32[256,256]{1,0:T(8,128)S(1)}, u32[]{:S(2)}, u32[]{:S(2)}) collective-permute-start(f32[256,256]{1,0:T(8,128)S(1)} %slice.62), channel_id=1, source_target_pairs={{0,2},{1,5},{2,0},{3,7},{4,6},{5,1},{6,4},{7,3},{8,10},{9,13},{10,... | collective-permute-start | bytes 786440 | tf_op jit(solution)/shard_map/ppermute | solution.py:478
  34.5 5.1 %collective-permute-start.10 = (f32[136,256]{1,0:T(8,128)S(1)}, f32[136,256]{1,0:T(8,128)S(1)}, u32[]{:S(2)}, u32[]{:S(2)}) collective-permute-start(f32[136,256]{1,0:T(8,128)S(1)} %slice.71), channel_id=1, source_target_pairs={{0,4},{1,3},{2,6},{3,1},{4,0},{5,7},{6,2},{7,5},{8,12},{9,11},{10,... | collective-permute-start | bytes 417800 | tf_op jit(solution)/shard_map/ppermute | solution.py:478
  38.1 5.6 %collective-permute-start.7 = (f32[128,256]{1,0:T(8,128)S(1)}, f32[128,256]{1,0:T(8,128)S(1)}, u32[]{:S(2)}, u32[]{:S(2)}) collective-permute-start(f32[128,256]{1,0:T(8,128)S(1)} %slice.64), channel_id=1, source_target_pairs={{0,4},{1,3},{2,6},{3,1},{4,0},{5,7},{6,2},{7,5},{8,12},{9,11},{10,... | collective-permute-start | bytes 393224 | tf_op jit(solution)/shard_map/ppermute | solution.py:478
  39.7 7.5 %collective-permute-start.11 = (f32[72,256]{1,0:T(8,128)S(1)}, f32[72,256]{1,0:T(8,128)S(1)}, u32[]{:S(2)}, u32[]{:S(2)}) collective-permute-start(f32[72,256]{1,0:T(8,128)S(1)} %slice.74), channel_id=1, source_target_pairs={{0,8},{1,9},{2,10},{3,11},{4,12},{5,13},{6,14},{7,15},{8,0},{9,1},... | collective-permute-start | bytes 221192 | tf_op jit(solution)/shard_map/ppermute | solution.py:478
  43.7 5.9 %collective-permute-start.8 = (f32[64,256]{1,0:T(8,128)S(1)}, f32[64,256]{1,0:T(8,128)S(1)}, u32[]{:S(2)}, u32[]{:S(2)}) collective-permute-start(f32[64,256]{1,0:T(8,128)S(1)} %get-tuple-element.61), channel_id=1, source_target_pairs={{0,8},{1,9},{2,10},{3,11},{4,12},{5,13},{6,14},{7,15},{8,0},{9,1},... | collective-permute-start | bytes 196616 | tf_op jit(solution)/shard_map/ppermute | solution.py:478

commit v4 on v3

--- a/solution.py
+++ b/solution.py
@@ -388,22 +388,23 @@
     )
 
 
-def keep_kernel(parts, *refs):
+def keep_kernel(start, parts, *refs):
     sel_ref, out_ref = refs[parts + 1], refs[-1]
-    half = sel_ref.shape[0] // 2
-    select_rows(refs[1 : parts + 1], sel_ref, 0, out_ref, half)
+    rows = sel_ref.shape[0] // 4
+    select_rows(refs[1 : parts + 1], sel_ref, start, out_ref, rows)
     if len(refs) > parts + 3:
-        out_ref[half:, :] = refs[parts + 2][...]
-
-
-def keep_rows(after, ps, sel, tail=None):
+        out_ref[rows:, :] = refs[parts + 2][...]
+
+
+def keep_rows(after, ps, sel, later, tail=None):
     queries = ps[0].shape[1]
+    rows = sel.shape[0] // 4
     args = (after, *ps, sel) + (() if tail is None else (tail,))
     return kernel_call(
-        functools.partial(keep_kernel, len(ps)),
-        "keep_rows",
+        functools.partial(keep_kernel, 0 if later else rows, len(ps)),
+        "keep_later" if later else "keep_first",
         args,
-        [((sel.shape[0] // 2 + (0 if tail is None else 8), queries), F32)],
+        [((rows + (0 if tail is None else 8), queries), F32)],
         (),
         [ANYWHERE] + [WHOLE] * (len(args) - 1),
         limit=8 << 20,
@@ -496,7 +497,7 @@
     xq, xt = query_pool.reshape(queries, -1), train_store.reshape(train, -1)
 
     half = train // 2
-    have_q, have_b = 128, 64
+    have_q, have_b = 32, 16
     smalls = (eigenvalues, tids, qids, inner, outer)
     eig_sum, eig_v, tids_v, qids_v, inner_v, outer_v, xq_part = kernel_call(
         functools.partial(sum_kernel, have_q, len(smalls)),
@@ -524,20 +525,22 @@
     chunk = queries // 2
     sent_a, p_a, tail = partial_scores((rta, rtb), hq, eig, eig_sum, w4t, sel_t, scale, chunk)
     got_a = halving_step(sent_a, 0, devices)
-    mine_a = keep_rows(sent_a, [p_a], sel_t, tail)
+    quarter = half // 2
+    first_a = keep_rows(sent_a, [p_a], sel_t, False, tail)
     d, p_b1 = score_first(sent_a, rta, hq, eig, eig_sum, w4t, scale, chunk, chunk)
-    mine_a, sent_a = next_halves(mine_a, got_a, half)
+    sent_a = first_a + got_a[quarter:]
     sent_b, p_b2 = score_second(sent_a, rtb, d, p_b1, sel_t)
     got_b = halving_step(sent_b, 0, devices)
-    mine_b = keep_rows(sent_b, [p_b1, p_b2], sel_t)
-    got_a = halving_step(sent_a, 1, devices)
-    pairs = [(mine_a, got_a), (mine_b, got_b)]
-    for b in range(1, bits):
+    first_b = keep_rows(sent_b, [p_b1, p_b2], sel_t, False)
+    next_a = halving_step(sent_a, 1, devices)
+    sent_b = first_b + got_b[quarter:]
+    mine_a = keep_rows(sent_b, [p_a], sel_t, True, tail) + jnp.concatenate([got_a[:quarter], got_a[half:]])
+    mine_b = keep_rows(sent_b, [p_b1, p_b2], sel_t, True) + got_b[:quarter]
+    pairs = [(mine_a, next_a), (mine_b, halving_step(sent_b, 1, devices))]
+    for step in range(2, bits):
         for c in range(2):
-            step = b + 1 - c
-            if step < bits:
-                mine, sent = next_halves(*pairs[c], half >> (step - 1))
-                pairs[c] = (mine, halving_step(sent, step, devices))
+            mine, sent = next_halves(*pairs[c], half >> (step - 1))
+            pairs[c] = (mine, halving_step(sent, step, devices))
     return finish(*pairs, sel_t, sel_q, columns).T
 
 

time: 50.9 us -> 49.5 us (0.972)
  waiting for transfers between devices: 12.2 us -> 9.91 us
  starting transfers between devices: 16.1 us -> 16.9 us
    ppermute x8, waiting for transfers between devices: 12.2 us -> 9.9 us  [halving_step(): return lax.ppermute(x, 'layer', pairs)]
    ppermute x8, starting transfers between devices: 8.67 us -> 9.47 us  [halving_step(): return lax.ppermute(x, 'layer', pairs)]
    pallas_call x11 -> x13, Pallas kernels: 20.7 us -> 20.9 us  [kernel_call(): pl.pallas_call(body, out_shape=tuple((pltpu.VMEM(shape, dtype) for shape,...]
  transfers between devices with their start and end apart: 12 -> 12, of which waited for: 6 -> 6; matrix products, arithmetic and copies ran while one was open for 1% -> 1% of each run, Pallas kernels for 26% -> 27%
where the time goes in v4:
time: 49.5 us; the launch traced here: 49.3 us
  Pallas kernels  21.9 us (44%)
  starting transfers between devices  16.9 us (34%)
  waiting for transfers between devices  9.91 us (20%)
    pallas_call x13, Pallas kernels, kernel_call(): pl.pallas_call(body, out_shape=tuple((pltpu.VMEM(shape, dtype) for shape,...  20.9 us
    ppermute x8, waiting for transfers between devices, halving_step(): return lax.ppermute(x, 'layer', pairs)  9.9 us
    ppermute x8, starting transfers between devices, halving_step(): return lax.ppermute(x, 'layer', pairs)  9.47 us
    ppermute x4, starting transfers between devices, exchange(): return lax.ppermute(x, 'layer', [(i, i ^ bit) for i in range(devices)])  7.41 us
  transfers between devices with their start and end apart: 12, of which 6 were waited for; matrix products, arithmetic and copies ran while one was open for 1% of the time, Pallas kernels for 27%

profile of v4, /device:TPU:0, one launch (start us, length us, event | category | flops | bytes accessed | tf_op | source)
XLA Modules:
  0.0 49.3 jit_solution(6182052996245929205)
XLA Ops:
  0.0 1.1 %eig_sum.1 = (f32[1,128]{1,0:T(1,128)S(1)}, f32[1,4096]{1,0:T(1,128)S(1)}, s32[1,1024]{1,0:T(1,128)S(1)}, s32[1,512]{1,0:T(1,128)S(1)}, bf16[64,64]{1,0:T(8,128)...) custom-call(f32[1,4096]{1,0:T(1,128)} %refs_0_.1, s32[1,1024]{1,0:T(1,128)} %bitcast.13, ...), custom_call_target="tpu_custom_call" | custom-call | tf_op jit(solution)/shard_map/eig_sum/pallas_call | solution.py:87
  1.1 0.5 %collective-permute-start = (f32[1,128]{1,0:T(1,128)S(1)}, f32[1,128]{1,0:T(1,128)S(1)}, u32[]{:S(2)}, u32[]{:S(2)}) collective-permute-start(f32[1,128]{1,0:T(1,128)S(1)} %get-tuple-element.33.refs_0_), channel_id=1, source_target_pairs={{0,1},{1,0},{2,3},{3,2},{4,5},{5,4},{6,7},{7,6},{8,9},{9,8},{10,11... | collective-permute-start | bytes 1544 | tf_op jit(solution)/shard_map/ppermute | solution.py:483
  1.6 2.1 %prepare.1 = (bf16[1024,1024]{1,0:T(8,128)(2,1)S(1)}, bf16[512,512]{1,0:T(8,128)(2,1)S(1)}, f32[1,4096]{1,0:T(1,128)S(1)}, bf16[256,256]{1,0:T(8,128)(2,1)S(1)},...) custom-call(f32[1,128]{1,0:T(1,128)S(1)} %get-tuple-element.33.refs_, ...), custom_call_target="tpu_custom_call", output_to_operand_aliasing={{6}: (7, {})} | custom-call | tf_op jit(solution)/shard_map/prepare/pallas_call | solution.py:87
  3.7 0.0 collective-permute-done
  3.8 2.6 %collective-permute-start.1 = (f32[1,128]{1,0:T(1,128)S(1)}, f32[1,128]{1,0:T(1,128)S(1)}, u32[]{:S(2)}, u32[]{:S(2)}) collective-permute-start(f32[1,128]{1,0:T(1,128)S(1)} %add.36.after_ref), channel_id=1, source_target_pairs={{0,2},{1,3},{2,0},{3,1},{4,6},{5,7},{6,4},{7,5},{8,10},{9,11},{10,... | collective-permute-start | bytes 1544 | tf_op jit(solution)/shard_map/ppermute | solution.py:483
  6.4 2.2 %rotate_query.1 = (bf16[16,512,256]{2,1,0:T(8,128)(2,1)S(1)}, bf16[512,4096]{1,0:T(8,128)(2,1)S(1)}, bf16[512,4096]{1,0:T(8,128)(2,1)S(1)}) custom-call(f32[1,128]{1,0:T(1,128)S(1)} %add.36.after_ref, bf16[512,4096]{1,0:T(8,128)(2,1)S(1)} %get-tuple-element.40.x_ref, bf16[256,256]{1,0:T(8,128)(2,1)S(1)} %get-tuple-element.41.w3_ref, bf16[1024,4096]{1,0:T(8,128)(2,1)} %bitcast.7), custom_call_target="tpu_custom_call" | custom-call | flops 1073741824 | tf_op jit(solution)/shard_map/rotate_query/pallas_call | solution.py:87
  8.6 0.0 collective-permute-done.1
  8.6 1.6 %collective-permute-start.2 = (f32[1,128]{1,0:T(1,128)S(1)}, f32[1,128]{1,0:T(1,128)S(1)}, u32[]{:S(2)}, u32[]{:S(2)}) collective-permute-start(f32[1,128]{1,0:T(1,128)S(1)} %add.37.after_ref), channel_id=1, source_target_pairs={{0,4},{1,5},{2,6},{3,7},{4,0},{5,1},{6,2},{7,3},{8,12},{9,13},{10,... | collective-permute-start | bytes 1544 | tf_op jit(solution)/shard_map/ppermute | solution.py:483
  10.2 2.6 %rotate_train.2 = (bf16[16,256,512]{2,1,0:T(8,128)(2,1)S(1)}, bf16[512,4096]{1,0:T(8,128)(2,1)S(1)}) custom-call(f32[1,128]{1,0:T(1,128)S(1)} %add.37.after_ref, bf16[512,4096]{1,0:T(8,128)(2,1)S(1)} %get-tuple-element.42.x_ref, bf16[256,256]{1,0:T(8,128)(2,1)S(1)} %get-tuple-element.41.w3_ref, ...), custom_call_target="tpu_custom_call", output_to_operand_aliasing={{1}: (5, {})} | custom-call | flops 2147483648 | tf_op jit(solution)/shard_map/rotate_train/pallas_call | solution.py:87
  12.9 0.0 collective-permute-done.2
  12.9 2.6 %collective-permute-start.3 = (f32[1,128]{1,0:T(1,128)S(1)}, f32[1,128]{1,0:T(1,128)S(1)}, u32[]{:S(2)}, u32[]{:S(2)}) collective-permute-start(f32[1,128]{1,0:T(1,128)S(1)} %add.38.after_ref), channel_id=1, source_target_pairs={{0,8},{1,9},{2,10},{3,11},{4,12},{5,13},{6,14},{7,15},{8,0},{9,1},... | collective-permute-start | bytes 1544 | tf_op jit(solution)/shard_map/ppermute | solution.py:483
  15.6 2.5 %rotate_train.3.rtb_ref.rt_ref = bf16[16,256,512]{2,1,0:T(8,128)(2,1)S(1)} custom-call(f32[1,128]{1,0:T(1,128)S(1)} %add.38.after_ref, bf16[512,4096]{1,0:T(8,128)(2,1)S(1)} %get-tuple-element.46.x_ref, bf16[256,256]{1,0:T(8,128)(2,1)S(1)} %get-tuple-element.41.w3_ref, bf16[256,256]{1,0:T(8,128)(2,1)S(1)} %get-tuple-element.43.w4_ref), custom_call_target="tpu_custom_call" | custom-call | flops 2147483648 | tf_op jit(solution)/shard_map/rotate_train/pallas_call | solution.py:87
  18.0 0.0 collective-permute-done.3
  18.1 4.4 %scores_self.1 = (f32[520,256]{1,0:T(8,128)S(1)}, bf16[2,256,1024]{2,1,0:T(8,128)(2,1)S(1)}, f32[8,256]{1,0:T(8,128)S(1)}) custom-call(bf16[16,256,512]{2,1,0:T(8,128)(2,1)S(1)} %get-tuple-element.45.rta_ref.rt_ref, bf16[16,256,512]{2,1,0:T(8,128)(2,1)S(1)} %rotate_train.3.rtb_ref.rt_ref, bf16[16,512,256]{2,1,0:T(8,128)(2,1)S(1)} %get-tuple-element.47.hq_ref, ...), custom_call_target="tpu_custom_call" | custom-call | tf_op jit(solution)/shard_map/scores_self/pallas_call | solution.py:87
  22.5 0.1 collective-permute-start.4
  22.6 1.8 %scores_first.1 = (bf16[256,4096]{1,0:T(8,128)(2,1)S(1)}, bf16[2,256,512]{2,1,0:T(8,128)(2,1)S(1)}) custom-call(f32[520,256]{1,0:T(8,128)S(1)} %get-tuple-element.51.refs_0_.after_ref, bf16[16,256,512]{2,1,0:T(8,128)(2,1)S(1)} %get-tuple-element.45.rta_ref.rt_ref, bf16[16,512,256]{2,1,0:T(8,128)(2,1)S(1)} %get-tuple-element.47.hq_ref, ...), custom_call_target="tpu_custom_call" | custom-call | tf_op jit(solution)/shard_map/scores_first/pallas_call | solution.py:87
  24.4 0.5 keep_first.2
  24.9 0.0 collective-permute-done.4
  24.9 2.0 %scores_second.1 = (f32[512,256]{1,0:T(8,128)S(1)}, bf16[2,256,512]{2,1,0:T(8,128)(2,1)S(1)}) custom-call(f32[264,256]{1,0:T(8,128)S(1)} %slice_add_fusion.after_ref, bf16[16,256,512]{2,1,0:T(8,128)(2,1)S(1)} %rotate_train.3.rtb_ref.rt_ref, bf16[256,4096]{1,0:T(8,128)(2,1)S(1)} %get-tuple-element.54.d_ref, ...), custom_call_target="tpu_custom_call" | custom-call | tf_op jit(solution)/shard_map/scores_second/pallas_call | solution.py:87
  26.9 0.6 %collective-permute-start.5 = (f32[512,256]{1,0:T(8,128)S(1)}, f32[512,256]{1,0:T(8,128)S(1)}, u32[]{:S(2)}, u32[]{:S(2)}) collective-permute-start(f32[512,256]{1,0:T(8,128)S(1)} %get-tuple-element.56.refs_0_), channel_id=1, source_target_pairs={{0,1},{1,0},{2,3},{3,2},{4,5},{5,4},{6,7},{7,6},{8,9},{9,8},{10,11... | collective-permute-start | bytes 1572872 | tf_op jit(solution)/shard_map/ppermute | solution.py:479
  27.5 1.3 %collective-permute-start.9 = (f32[264,256]{1,0:T(8,128)S(1)}, f32[264,256]{1,0:T(8,128)S(1)}, u32[]{:S(2)}, u32[]{:S(2)}) collective-permute-start(f32[264,256]{1,0:T(8,128)S(1)} %slice_add_fusion.after_ref), channel_id=1, source_target_pairs={{0,2},{1,5},{2,0},{3,7},{4,6},{5,1},{6,4},{7,3},{8,10},{9,13},{10,... | collective-permute-start | bytes 811016 | tf_op jit(solution)/shard_map/ppermute | solution.py:479
  28.7 0.5 keep_first.3
  29.2 0.0 collective-permute-done.5
  29.2 1.1 %collective-permute-start.6 = (f32[256,256]{1,0:T(8,128)S(1)}, f32[256,256]{1,0:T(8,128)S(1)}, u32[]{:S(2)}, u32[]{:S(2)}) collective-permute-start(f32[256,256]{1,0:T(8,128)S(1)} %slice_add_fusion.2.refs_0_), channel_id=1, source_target_pairs={{0,2},{1,5},{2,0},{3,7},{4,6},{5,1},{6,4},{7,3},{8,10},{9,13},{10,... | collective-permute-start | bytes 786440 | tf_op jit(solution)/shard_map/ppermute | solution.py:479
  30.4 0.5 keep_later.3
  30.9 3.0 %collective-permute-done.9 = f32[264,256]{1,0:T(8,128)S(1)} collective-permute-done((f32[264,256]{1,0:T(8,128)S(1)}, f32[264,256]{1,0:T(8,128)S(1)}, u32[]{:S(2)}, u32[]{:S(2)}) %collective-permute-start.9) | collective-permute-done | bytes 270368 | tf_op jit(solution)/shard_map/ppermute | solution.py:479
  33.9 0.1 fusion
  34.0 0.5 keep_later.2
  34.5 0.9 %collective-permute-start.10 = (f32[136,256]{1,0:T(8,128)S(1)}, f32[136,256]{1,0:T(8,128)S(1)}, u32[]{:S(2)}, u32[]{:S(2)}) collective-permute-start(f32[136,256]{1,0:T(8,128)S(1)} %slice.71), channel_id=1, source_target_pairs={{0,4},{1,3},{2,6},{3,1},{4,0},{5,7},{6,2},{7,5},{8,12},{9,11},{10,... | collective-permute-start | bytes 417800 | tf_op jit(solution)/shard_map/ppermute | solution.py:479
  35.4 1.6 %collective-permute-done.6 = f32[256,256]{1,0:T(8,128)S(1)} collective-permute-done((f32[256,256]{1,0:T(8,128)S(1)}, f32[256,256]{1,0:T(8,128)S(1)}, u32[]{:S(2)}, u32[]{:S(2)}) %collective-permute-start.6) | collective-permute-done | bytes 262176 | tf_op jit(solution)/shard_map/ppermute | solution.py:479
  37.0 0.1 fusion.1
  37.1 0.9 %collective-permute-start.7 = (f32[128,256]{1,0:T(8,128)S(1)}, f32[128,256]{1,0:T(8,128)S(1)}, u32[]{:S(2)}, u32[]{:S(2)}) collective-permute-start(f32[128,256]{1,0:T(8,128)S(1)} %slice.64), channel_id=1, source_target_pairs={{0,4},{1,3},{2,6},{3,1},{4,0},{5,7},{6,2},{7,5},{8,12},{9,11},{10,... | collective-permute-start | bytes 393224 | tf_op jit(solution)/shard_map/ppermute | solution.py:479
  38.0 1.7 %collective-permute-done.10 = f32[136,256]{1,0:T(8,128)S(1)} collective-permute-done((f32[136,256]{1,0:T(8,128)S(1)}, f32[136,256]{1,0:T(8,128)S(1)}, u32[]{:S(2)}, u32[]{:S(2)}) %collective-permute-start.10) | collective-permute-done | bytes 139296 | tf_op jit(solution)/shard_map/ppermute | solution.py:479
  39.7 2.0 %collective-permute-start.11 = (f32[72,256]{1,0:T(8,128)S(1)}, f32[72,256]{1,0:T(8,128)S(1)}, u32[]{:S(2)}, u32[]{:S(2)}) collective-permute-start(f32[72,256]{1,0:T(8,128)S(1)} %slice.74), channel_id=1, source_target_pairs={{0,8},{1,9},{2,10},{3,11},{4,12},{5,13},{6,14},{7,15},{8,0},{9,1},... | collective-permute-start | bytes 221192 | tf_op jit(solution)/shard_map/ppermute | solution.py:479
  41.7 0.8 %collective-permute-done.7 = f32[128,256]{1,0:T(8,128)S(1)} collective-permute-done((f32[128,256]{1,0:T(8,128)S(1)}, f32[128,256]{1,0:T(8,128)S(1)}, u32[]{:S(2)}, u32[]{:S(2)}) %collective-permute-start.7) | collective-permute-done | bytes 131104 | tf_op jit(solution)/shard_map/ppermute | solution.py:479
  42.6 2.7 %collective-permute-start.8 = (f32[64,256]{1,0:T(8,128)S(1)}, f32[64,256]{1,0:T(8,128)S(1)}, u32[]{:S(2)}, u32[]{:S(2)}) collective-permute-start(f32[64,256]{1,0:T(8,128)S(1)} %get-tuple-element.61), channel_id=1, source_target_pairs={{0,8},{1,9},{2,10},{3,11},{4,12},{5,13},{6,14},{7,15},{8,0},{9,1},... | collective-permute-start | bytes 196616 | tf_op jit(solution)/shard_map/ppermute | solution.py:479
  45.2 1.5 %collective-permute-done.11.got_ref = f32[72,256]{1,0:T(8,128)S(1)} collective-permute-done((f32[72,256]{1,0:T(8,128)S(1)}, f32[72,256]{1,0:T(8,128)S(1)}, u32[]{:S(2)}, u32[]{:S(2)}) %collective-permute-start.11) | collective-permute-done | bytes 73760 | tf_op jit(solution)/shard_map/ppermute | solution.py:479
  46.7 0.3 finish_first.1
  47.1 1.3 %collective-permute-done.8.got_ref = f32[64,256]{1,0:T(8,128)S(1)} collective-permute-done((f32[64,256]{1,0:T(8,128)S(1)}, f32[64,256]{1,0:T(8,128)S(1)}, u32[]{:S(2)}, u32[]{:S(2)}) %collective-permute-start.8) | collective-permute-done | bytes 65568 | tf_op jit(solution)/shard_map/ppermute | solution.py:479
  48.3 1.0 %finish_second.1 = f32[64,512]{1,0:T(8,128)} custom-call(f32[64,256]{1,0:T(8,128)S(1)} %get-tuple-element.62.mine_ref, f32[64,256]{1,0:T(8,128)S(1)} %collective-permute-done.8.got_ref, f32[64,512]{1,0:T(8,128)S(1)} %get-tuple-element.59.first_ref, f32[64,128]{1,0:T(8,128)S(1)} %get-tuple-element.60.norm_ref, bf16[512,512]{1,0:T(8,128)(2,1)S(1)} %get-tuple-element.58.sel_q_ref), custom_call_target="tpu_custom_call" | custom-call | tf_op jit(solution)/shard_map/finish_second/pallas_call | solution.py:450
  (19 shorter events, 0.2 us)
Async XLA Ops:
  1.1 2.6 %collective-permute-start = (f32[1,128]{1,0:T(1,128)S(1)}, f32[1,128]{1,0:T(1,128)S(1)}, u32[]{:S(2)}, u32[]{:S(2)}) collective-permute-start(f32[1,128]{1,0:T(1,128)S(1)} %get-tuple-element.33.refs_0_), channel_id=1, source_target_pairs={{0,1},{1,0},{2,3},{3,2},{4,5},{5,4},{6,7},{7,6},{8,9},{9,8},{10,11... | collective-permute-start | bytes 1544 | tf_op jit(solution)/shard_map/ppermute | solution.py:483
  3.8 4.8 %collective-permute-start.1 = (f32[1,128]{1,0:T(1,128)S(1)}, f32[1,128]{1,0:T(1,128)S(1)}, u32[]{:S(2)}, u32[]{:S(2)}) collective-permute-start(f32[1,128]{1,0:T(1,128)S(1)} %add.36.after_ref), channel_id=1, source_target_pairs={{0,2},{1,3},{2,0},{3,1},{4,6},{5,7},{6,4},{7,5},{8,10},{9,11},{10,... | collective-permute-start | bytes 1544 | tf_op jit(solution)/shard_map/ppermute | solution.py:483
  8.6 4.3 %collective-permute-start.2 = (f32[1,128]{1,0:T(1,128)S(1)}, f32[1,128]{1,0:T(1,128)S(1)}, u32[]{:S(2)}, u32[]{:S(2)}) collective-permute-start(f32[1,128]{1,0:T(1,128)S(1)} %add.37.after_ref), channel_id=1, source_target_pairs={{0,4},{1,5},{2,6},{3,7},{4,0},{5,1},{6,2},{7,3},{8,12},{9,13},{10,... | collective-permute-start | bytes 1544 | tf_op jit(solution)/shard_map/ppermute | solution.py:483
  12.9 5.1 %collective-permute-start.3 = (f32[1,128]{1,0:T(1,128)S(1)}, f32[1,128]{1,0:T(1,128)S(1)}, u32[]{:S(2)}, u32[]{:S(2)}) collective-permute-start(f32[1,128]{1,0:T(1,128)S(1)} %add.38.after_ref), channel_id=1, source_target_pairs={{0,8},{1,9},{2,10},{3,11},{4,12},{5,13},{6,14},{7,15},{8,0},{9,1},... | collective-permute-start | bytes 1544 | tf_op jit(solution)/shard_map/ppermute | solution.py:483
  22.5 2.4 %collective-permute-start.4 = (f32[520,256]{1,0:T(8,128)S(1)}, f32[520,256]{1,0:T(8,128)S(1)}, u32[]{:S(2)}, u32[]{:S(2)}) collective-permute-start(f32[520,256]{1,0:T(8,128)S(1)} %get-tuple-element.51.refs_0_.after_ref), channel_id=1, source_target_pairs={{0,1},{1,0},{2,3},{3,2},{4,5},{5,4},{6,7},{7,6},{8,9},{9,8},{10,11... | collective-permute-start | bytes 1597448 | tf_op jit(solution)/shard_map/ppermute | solution.py:479
  26.9 2.3 %collective-permute-start.5 = (f32[512,256]{1,0:T(8,128)S(1)}, f32[512,256]{1,0:T(8,128)S(1)}, u32[]{:S(2)}, u32[]{:S(2)}) collective-permute-start(f32[512,256]{1,0:T(8,128)S(1)} %get-tuple-element.56.refs_0_), channel_id=1, source_target_pairs={{0,1},{1,0},{2,3},{3,2},{4,5},{5,4},{6,7},{7,6},{8,9},{9,8},{10,11... | collective-permute-start | bytes 1572872 | tf_op jit(solution)/shard_map/ppermute | solution.py:479
  27.5 6.5 %collective-permute-start.9 = (f32[264,256]{1,0:T(8,128)S(1)}, f32[264,256]{1,0:T(8,128)S(1)}, u32[]{:S(2)}, u32[]{:S(2)}) collective-permute-start(f32[264,256]{1,0:T(8,128)S(1)} %slice_add_fusion.after_ref), channel_id=1, source_target_pairs={{0,2},{1,5},{2,0},{3,7},{4,6},{5,1},{6,4},{7,3},{8,10},{9,13},{10,... | collective-permute-start | bytes 811016 | tf_op jit(solution)/shard_map/ppermute | solution.py:479
  29.2 7.7 %collective-permute-start.6 = (f32[256,256]{1,0:T(8,128)S(1)}, f32[256,256]{1,0:T(8,128)S(1)}, u32[]{:S(2)}, u32[]{:S(2)}) collective-permute-start(f32[256,256]{1,0:T(8,128)S(1)} %slice_add_fusion.2.refs_0_), channel_id=1, source_target_pairs={{0,2},{1,5},{2,0},{3,7},{4,6},{5,1},{6,4},{7,3},{8,10},{9,13},{10,... | collective-permute-start | bytes 786440 | tf_op jit(solution)/shard_map/ppermute | solution.py:479
  34.5 5.1 %collective-permute-start.10 = (f32[136,256]{1,0:T(8,128)S(1)}, f32[136,256]{1,0:T(8,128)S(1)}, u32[]{:S(2)}, u32[]{:S(2)}) collective-permute-start(f32[136,256]{1,0:T(8,128)S(1)} %slice.71), channel_id=1, source_target_pairs={{0,4},{1,3},{2,6},{3,1},{4,0},{5,7},{6,2},{7,5},{8,12},{9,11},{10,... | collective-permute-start | bytes 417800 | tf_op jit(solution)/shard_map/ppermute | solution.py:479
  37.1 5.4 %collective-permute-start.7 = (f32[128,256]{1,0:T(8,128)S(1)}, f32[128,256]{1,0:T(8,128)S(1)}, u32[]{:S(2)}, u32[]{:S(2)}) collective-permute-start(f32[128,256]{1,0:T(8,128)S(1)} %slice.64), channel_id=1, source_target_pairs={{0,4},{1,3},{2,6},{3,1},{4,0},{5,7},{6,2},{7,5},{8,12},{9,11},{10,... | collective-permute-start | bytes 393224 | tf_op jit(solution)/shard_map/ppermute | solution.py:479
  39.7 7.1 %collective-permute-start.11 = (f32[72,256]{1,0:T(8,128)S(1)}, f32[72,256]{1,0:T(8,128)S(1)}, u32[]{:S(2)}, u32[]{:S(2)}) collective-permute-start(f32[72,256]{1,0:T(8,128)S(1)} %slice.74), channel_id=1, source_target_pairs={{0,8},{1,9},{2,10},{3,11},{4,12},{5,13},{6,14},{7,15},{8,0},{9,1},... | collective-permute-start | bytes 221192 | tf_op jit(solution)/shard_map/ppermute | solution.py:479
  42.6 5.8 %collective-permute-start.8 = (f32[64,256]{1,0:T(8,128)S(1)}, f32[64,256]{1,0:T(8,128)S(1)}, u32[]{:S(2)}, u32[]{:S(2)}) collective-permute-start(f32[64,256]{1,0:T(8,128)S(1)} %get-tuple-element.61), channel_id=1, source_target_pairs={{0,8},{1,9},{2,10},{3,11},{4,12},{5,13},{6,14},{7,15},{8,0},{9,1},... | collective-permute-start | bytes 196616 | tf_op jit(solution)/shard_map/ppermute | solution.py:479

commit v5 on v4

--- a/solution.py
+++ b/solution.py
@@ -180,7 +180,7 @@
     )
 
 
-def query_kernel(side, ahead, after_ref, x_ref, w3_ref, next_any, out_ref, next_ref, last_ref, half_ref, sems):
+def query_kernel(side, ahead, after_ref, x_ref, w3_ref, w4t_ref, next_any, turned_ref, next_ref, last_ref, half_ref, sems):
     rows = next_ref.shape[0]
     copies = fetch((rows_from(next_any, next_ref, 0, rows), (next_any.at[rows : rows + ahead], last_ref.at[:ahead])), sems)
     @beside_fetch
@@ -188,7 +188,7 @@
         pack = w3_ref.shape[0] // side
         wide = w3_ref.shape[0]
         groups, unit = side // pack, pack * pack
-        w3 = w3_ref[...]
+        w3, w4t = w3_ref[...], w4t_ref[...]
         queries = x_ref.shape[0]
         block = min(queries, 256)
         for r in range(0, queries + block, block):
@@ -197,23 +197,24 @@
                     part = dot(w3, x_ref[r : r + block, g * wide : (g + 1) * wide], NT).astype(BF16)
                     half_ref[:, g * unit : (g + 1) * unit, r : r + block] = part.reshape(groups, unit, block)
                 if r:
-                    out_ref[g, r - block : r, :] = half_ref[g, :, r - block : r].T
+                    turned = half_ref[g, :, r - block : r].T
+                    turned_ref[r - block : r, g * wide : (g + 1) * wide] = dot(turned, w4t)
 
     for copy in copies:
         copy.wait()
 
 
-def rotate_query(after, x, w3, upcoming, rows_next, ahead, side):
+def rotate_query(after, x, w3, w4t, upcoming, rows_next, ahead, side):
     rows, feat = x.shape
     wide = w3.shape[0]
     groups = feat // wide
     return kernel_call(
         functools.partial(query_kernel, side, ahead),
         "rotate_query",
-        (after, x, w3, upcoming),
-        [((groups, rows, wide), BF16), ((rows_next, feat), BF16), ((rows_next, feat), BF16)],
+        (after, x, w3, w4t, upcoming),
+        [((rows, feat), F32), ((rows_next, feat), BF16), ((rows_next, feat), BF16)],
         [pltpu.VMEM((groups, wide, rows), BF16), pltpu.SemaphoreType.DMA((2,))],
-        [ANYWHERE, WHOLE, WHOLE, IN_HBM],
+        [ANYWHERE, WHOLE, WHOLE, WHOLE, IN_HBM],
         flops=2 * rows * feat * wide,
         limit=12 << 20,
     )
@@ -267,15 +268,6 @@
     )
 
 
-def damped_queries(d_ref, hq_ref, w4t_ref, inv, start):
-    queries = d_ref.shape[0]
-    groups, _, wide = hq_ref.shape
-    w4t = w4t_ref[...]
-    for g in range(groups):
-        d = dot(hq_ref[g, start : start + queries, :], w4t) * inv[:, g * wide : (g + 1) * wide]
-        d_ref[:, g * wide : (g + 1) * wide] = d.astype(BF16)
-
-
 def multiply(p_ref, d_ref, rt_ref, at, inv_cols=()):
     groups, wide, cols = rt_ref.shape
     rt = rt_ref[...].reshape(groups * wide, cols)
@@ -320,9 +312,9 @@
     return jnp.concatenate(tail, axis=0)
 
 
-def score_kernel(scale, rta_ref, rtb_ref, hq_ref, eig_ref, sum_ref, w4t_ref, sel_ref, sent_ref, p_ref, tail_ref, d_ref, inv_ref):
+def score_kernel(scale, rta_ref, rtb_ref, turned_ref, eig_ref, sum_ref, sel_ref, sent_ref, p_ref, tail_ref, d_ref, inv_ref):
     inv = 1.0 / (eig_ref[...] + sum_ref[0:1, 0:1] * scale)
-    damped_queries(d_ref, hq_ref, w4t_ref, inv, 0)
+    d_ref[...] = (turned_ref[: d_ref.shape[0], :] * inv).astype(BF16)
     groups, wide, _ = rta_ref.shape
     for g in range(groups):
         inv_ref[g] = jnp.broadcast_to(inv[:, g * wide : (g + 1) * wide], (128, wide)).T
@@ -336,34 +328,34 @@
     tail_ref[...] = tail
 
 
-def partial_scores(rts, hq, eig, eig_sum, w4t, sel, scale, queries):
+def partial_scores(rts, turned, eig, eig_sum, sel, scale, queries):
     train = sel.shape[0]
-    feat = eig.shape[1]
+    feat = turned.shape[1]
     return kernel_call(
         functools.partial(score_kernel, scale),
         "scores_self",
-        (*rts, hq, eig, eig_sum, w4t, sel),
+        (*rts, turned, eig, eig_sum, sel),
         [((train // 2 + 8, queries), F32), ((2, queries, train), BF16), ((8, queries), F32)],
         [pltpu.VMEM((queries, feat), BF16), pltpu.VMEM((*rts[0].shape[:2], 128), F32)],
         limit=16 << 20,
     )
 
 
-def score_first_kernel(scale, start, after_ref, rt_ref, hq_ref, eig_ref, sum_ref, w4t_ref, d_ref, p_ref):
+def score_first_kernel(scale, start, after_ref, rt_ref, turned_ref, eig_ref, sum_ref, d_ref, p_ref):
     inv = 1.0 / (eig_ref[...] + sum_ref[0:1, 0:1] * scale)
-    damped_queries(d_ref, hq_ref, w4t_ref, inv, start)
+    d_ref[...] = (turned_ref[start : start + d_ref.shape[0], :] * inv).astype(BF16)
     multiply(p_ref, d_ref, rt_ref, 0)
 
 
-def score_first(after, rt, hq, eig, eig_sum, w4t, scale, start, queries):
+def score_first(after, rt, turned, eig, eig_sum, scale, start, queries):
     feat, cols = eig.shape[1], rt.shape[2]
     return kernel_call(
         functools.partial(score_first_kernel, scale, start),
         "scores_first",
-        (after, rt, hq, eig, eig_sum, w4t),
+        (after, rt, turned, eig, eig_sum),
         [((queries, feat), BF16), ((2, queries, cols), BF16)],
         (),
-        [ANYWHERE] + [WHOLE] * 5,
+        [ANYWHERE] + [WHOLE] * 4,
         limit=8 << 20,
     )
 
@@ -515,7 +507,7 @@
                 eig_sum, tids_v, qids_v, eig_v, inner_v, outer_v, xq, xq_part, have_q, devices
             )
         elif b == 1:
-            hq, xa, xb = rotate_query(eig_sum, xq, w3, xt, half, have_b, side)
+            turned, xa, xb = rotate_query(eig_sum, xq, w3, w4t, xt, half, have_b, side)
         elif b == 2:
             rta, xb = rotate_train(eig_sum, xa, w3, w4, side, xt, xb, have_b)
         elif b == 3:
@@ -523,11 +515,11 @@
         eig_sum = eig_sum + got
 
     chunk = queries // 2
-    sent_a, p_a, tail = partial_scores((rta, rtb), hq, eig, eig_sum, w4t, sel_t, scale, chunk)
+    sent_a, p_a, tail = partial_scores((rta, rtb), turned, eig, eig_sum, sel_t, scale, chunk)
     got_a = halving_step(sent_a, 0, devices)
     quarter = half // 2
     first_a = keep_rows(sent_a, [p_a], sel_t, False, tail)
-    d, p_b1 = score_first(sent_a, rta, hq, eig, eig_sum, w4t, scale, chunk, chunk)
+    d, p_b1 = score_first(sent_a, rta, turned, eig, eig_sum, scale, chunk, chunk)
     sent_a = first_a + got_a[quarter:]
     sent_b, p_b2 = score_second(sent_a, rtb, d, p_b1, sel_t)
     got_b = halving_step(sent_b, 0, devices)

time: 49.5 us -> 49.3 us (level)
  starting transfers between devices: 16.9 us -> 16.3 us
  waiting for transfers between devices: 9.91 us -> 10.5 us
    ppermute x8, waiting for transfers between devices: 9.9 us -> 10.5 us  [halving_step(): return lax.ppermute(x, 'layer', pairs)]
    ppermute x8, starting transfers between devices: 9.47 us -> 8.85 us  [halving_step(): return lax.ppermute(x, 'layer', pairs)]
  transfers between devices with their start and end apart: 12 -> 12, of which waited for: 6 -> 7; matrix products, arithmetic and copies ran while one was open for 1% -> 1% of each run, Pallas kernels for 27% -> 27%
where the time goes in v5:
time: 49.3 us; the launch traced here: 49.1 us
  Pallas kernels  21.6 us (44%)
  starting transfers between devices  16.3 us (33%)
  waiting for transfers between devices  10.5 us (21%)
    pallas_call x13, Pallas kernels, kernel_call(): pl.pallas_call(body, out_shape=tuple((pltpu.VMEM(shape, dtype) for shape,...  20.7 us
    ppermute x8, waiting for transfers between devices, halving_step(): return lax.ppermute(x, 'layer', pairs)  10.5 us
    ppermute x8, starting transfers between devices, halving_step(): return lax.ppermute(x, 'layer', pairs)  8.85 us
    ppermute x4, starting transfers between devices, exchange(): return lax.ppermute(x, 'layer', [(i, i ^ bit) for i in range(devices)])  7.42 us
  transfers between devices with their start and end apart: 12, of which 7 were waited for; matrix products, arithmetic and copies ran while one was open for 1% of the time, Pallas kernels for 27%

profile of v5, /device:TPU:0, one launch (start us, length us, event | category | flops | bytes accessed | tf_op | source)
XLA Modules:
  0.0 49.1 jit_solution(12855950362965953082)
XLA Ops:
  0.0 1.1 %eig_sum.1 = (f32[1,128]{1,0:T(1,128)S(1)}, f32[1,4096]{1,0:T(1,128)S(1)}, s32[1,1024]{1,0:T(1,128)S(1)}, s32[1,512]{1,0:T(1,128)S(1)}, bf16[64,64]{1,0:T(8,128)...) custom-call(f32[1,4096]{1,0:T(1,128)} %refs_0_.1, s32[1,1024]{1,0:T(1,128)} %bitcast.13, ...), custom_call_target="tpu_custom_call" | custom-call | tf_op jit(solution)/shard_map/eig_sum/pallas_call | solution.py:87
  1.1 0.5 %collective-permute-start = (f32[1,128]{1,0:T(1,128)S(1)}, f32[1,128]{1,0:T(1,128)S(1)}, u32[]{:S(2)}, u32[]{:S(2)}) collective-permute-start(f32[1,128]{1,0:T(1,128)S(1)} %get-tuple-element.33.refs_0_), channel_id=1, source_target_pairs={{0,1},{1,0},{2,3},{3,2},{4,5},{5,4},{6,7},{7,6},{8,9},{9,8},{10,11... | collective-permute-start | bytes 1544 | tf_op jit(solution)/shard_map/ppermute | solution.py:475
  1.6 2.1 %prepare.1 = (bf16[1024,1024]{1,0:T(8,128)(2,1)S(1)}, bf16[512,512]{1,0:T(8,128)(2,1)S(1)}, f32[1,4096]{1,0:T(1,128)S(1)}, bf16[256,256]{1,0:T(8,128)(2,1)S(1)},...) custom-call(f32[1,128]{1,0:T(1,128)S(1)} %get-tuple-element.33.refs_, ...), custom_call_target="tpu_custom_call", output_to_operand_aliasing={{6}: (7, {})} | custom-call | tf_op jit(solution)/shard_map/prepare/pallas_call | solution.py:87
  3.7 0.0 collective-permute-done
  3.8 2.6 %collective-permute-start.1 = (f32[1,128]{1,0:T(1,128)S(1)}, f32[1,128]{1,0:T(1,128)S(1)}, u32[]{:S(2)}, u32[]{:S(2)}) collective-permute-start(f32[1,128]{1,0:T(1,128)S(1)} %add.36.after_ref), channel_id=1, source_target_pairs={{0,2},{1,3},{2,0},{3,1},{4,6},{5,7},{6,4},{7,5},{8,10},{9,11},{10,... | collective-permute-start | bytes 1544 | tf_op jit(solution)/shard_map/ppermute | solution.py:475
  6.4 2.6 %rotate_query.1 = (f32[512,4096]{1,0:T(8,128)S(1)}, bf16[512,4096]{1,0:T(8,128)(2,1)S(1)}, bf16[512,4096]{1,0:T(8,128)(2,1)S(1)}) custom-call(f32[1,128]{1,0:T(1,128)S(1)} %add.36.after_ref, bf16[512,4096]{1,0:T(8,128)(2,1)S(1)} %get-tuple-element.40.x_ref, bf16[256,256]{1,0:T(8,128)(2,1)S(1)} %get-tuple-element.41.w3_ref, ...), custom_call_target="tpu_custom_call" | custom-call | flops 1073741824 | tf_op jit(solution)/shard_map/rotate_query/pallas_call | solution.py:87
  9.0 0.0 collective-permute-done.1
  9.0 1.6 %collective-permute-start.2 = (f32[1,128]{1,0:T(1,128)S(1)}, f32[1,128]{1,0:T(1,128)S(1)}, u32[]{:S(2)}, u32[]{:S(2)}) collective-permute-start(f32[1,128]{1,0:T(1,128)S(1)} %add.37.after_ref), channel_id=1, source_target_pairs={{0,4},{1,5},{2,6},{3,7},{4,0},{5,1},{6,2},{7,3},{8,12},{9,13},{10,... | collective-permute-start | bytes 1544 | tf_op jit(solution)/shard_map/ppermute | solution.py:475
  10.7 2.6 %rotate_train.2 = (bf16[16,256,512]{2,1,0:T(8,128)(2,1)S(1)}, bf16[512,4096]{1,0:T(8,128)(2,1)S(1)}) custom-call(f32[1,128]{1,0:T(1,128)S(1)} %add.37.after_ref, bf16[512,4096]{1,0:T(8,128)(2,1)S(1)} %get-tuple-element.43.x_ref, bf16[256,256]{1,0:T(8,128)(2,1)S(1)} %get-tuple-element.41.w3_ref, ...), custom_call_target="tpu_custom_call", output_to_operand_aliasing={{1}: (5, {})} | custom-call | flops 2147483648 | tf_op jit(solution)/shard_map/rotate_train/pallas_call | solution.py:87
  13.3 0.0 collective-permute-done.2
  13.3 2.7 %collective-permute-start.3 = (f32[1,128]{1,0:T(1,128)S(1)}, f32[1,128]{1,0:T(1,128)S(1)}, u32[]{:S(2)}, u32[]{:S(2)}) collective-permute-start(f32[1,128]{1,0:T(1,128)S(1)} %add.38.after_ref), channel_id=1, source_target_pairs={{0,8},{1,9},{2,10},{3,11},{4,12},{5,13},{6,14},{7,15},{8,0},{9,1},... | collective-permute-start | bytes 1544 | tf_op jit(solution)/shard_map/ppermute | solution.py:475
  16.0 2.5 %rotate_train.3.rtb_ref.rt_ref = bf16[16,256,512]{2,1,0:T(8,128)(2,1)S(1)} custom-call(f32[1,128]{1,0:T(1,128)S(1)} %add.38.after_ref, bf16[512,4096]{1,0:T(8,128)(2,1)S(1)} %get-tuple-element.47.x_ref, bf16[256,256]{1,0:T(8,128)(2,1)S(1)} %get-tuple-element.41.w3_ref, bf16[256,256]{1,0:T(8,128)(2,1)S(1)} %get-tuple-element.44.w4_ref), custom_call_target="tpu_custom_call" | custom-call | flops 2147483648 | tf_op jit(solution)/shard_map/rotate_train/pallas_call | solution.py:87
  18.5 0.0 collective-permute-done.3
  18.5 4.2 %scores_self.1 = (f32[520,256]{1,0:T(8,128)S(1)}, bf16[2,256,1024]{2,1,0:T(8,128)(2,1)S(1)}, f32[8,256]{1,0:T(8,128)S(1)}) custom-call(bf16[16,256,512]{2,1,0:T(8,128)(2,1)S(1)} %get-tuple-element.46.rta_ref.rt_ref, bf16[16,256,512]{2,1,0:T(8,128)(2,1)S(1)} %rotate_train.3.rtb_ref.rt_ref, f32[512,4096]{1,0:T(8,128)S(1)} %get-tuple-element.48.turned_ref, ...), custom_call_target="tpu_custom_call" | custom-call | tf_op jit(solution)/shard_map/scores_self/pallas_call | solution.py:87
  22.7 0.1 collective-permute-start.4
  22.8 1.4 %scores_first.1 = (bf16[256,4096]{1,0:T(8,128)(2,1)S(1)}, bf16[2,256,512]{2,1,0:T(8,128)(2,1)S(1)}) custom-call(f32[520,256]{1,0:T(8,128)S(1)} %get-tuple-element.51.refs_0_.after_ref, bf16[16,256,512]{2,1,0:T(8,128)(2,1)S(1)} %get-tuple-element.46.rta_ref.rt_ref, f32[512,4096]{1,0:T(8,128)S(1)} %get-tuple-element.48.turned_ref, ...), custom_call_target="tpu_custom_call" | custom-call | tf_op jit(solution)/shard_map/scores_first/pallas_call | solution.py:87
  24.2 0.5 keep_first.2
  24.6 0.0 collective-permute-done.4
  24.7 2.0 %scores_second.1 = (f32[512,256]{1,0:T(8,128)S(1)}, bf16[2,256,512]{2,1,0:T(8,128)(2,1)S(1)}) custom-call(f32[264,256]{1,0:T(8,128)S(1)} %slice_add_fusion.after_ref, bf16[16,256,512]{2,1,0:T(8,128)(2,1)S(1)} %rotate_train.3.rtb_ref.rt_ref, bf16[256,4096]{1,0:T(8,128)(2,1)S(1)} %get-tuple-element.54.d_ref, ...), custom_call_target="tpu_custom_call" | custom-call | tf_op jit(solution)/shard_map/scores_second/pallas_call | solution.py:87
  26.7 0.6 %collective-permute-start.5 = (f32[512,256]{1,0:T(8,128)S(1)}, f32[512,256]{1,0:T(8,128)S(1)}, u32[]{:S(2)}, u32[]{:S(2)}) collective-permute-start(f32[512,256]{1,0:T(8,128)S(1)} %get-tuple-element.56.refs_0_), channel_id=1, source_target_pairs={{0,1},{1,0},{2,3},{3,2},{4,5},{5,4},{6,7},{7,6},{8,9},{9,8},{10,11... | collective-permute-start | bytes 1572872 | tf_op jit(solution)/shard_map/ppermute | solution.py:471
  27.2 0.8 %collective-permute-start.9 = (f32[264,256]{1,0:T(8,128)S(1)}, f32[264,256]{1,0:T(8,128)S(1)}, u32[]{:S(2)}, u32[]{:S(2)}) collective-permute-start(f32[264,256]{1,0:T(8,128)S(1)} %slice_add_fusion.after_ref), channel_id=1, source_target_pairs={{0,2},{1,5},{2,0},{3,7},{4,6},{5,1},{6,4},{7,3},{8,10},{9,13},{10,... | collective-permute-start | bytes 811016 | tf_op jit(solution)/shard_map/ppermute | solution.py:471
  28.1 0.5 keep_first.3
  28.5 0.2 collective-permute-done.5
  28.8 1.0 %collective-permute-start.6 = (f32[256,256]{1,0:T(8,128)S(1)}, f32[256,256]{1,0:T(8,128)S(1)}, u32[]{:S(2)}, u32[]{:S(2)}) collective-permute-start(f32[256,256]{1,0:T(8,128)S(1)} %slice_add_fusion.2.refs_0_), channel_id=1, source_target_pairs={{0,2},{1,5},{2,0},{3,7},{4,6},{5,1},{6,4},{7,3},{8,10},{9,13},{10,... | collective-permute-start | bytes 786440 | tf_op jit(solution)/shard_map/ppermute | solution.py:471
  29.9 0.5 keep_later.3
  30.4 3.3 %collective-permute-done.9 = f32[264,256]{1,0:T(8,128)S(1)} collective-permute-done((f32[264,256]{1,0:T(8,128)S(1)}, f32[264,256]{1,0:T(8,128)S(1)}, u32[]{:S(2)}, u32[]{:S(2)}) %collective-permute-start.9) | collective-permute-done | bytes 270368 | tf_op jit(solution)/shard_map/ppermute | solution.py:471
  33.7 0.1 fusion
  33.8 0.5 keep_later.2
  34.3 0.8 %collective-permute-start.10 = (f32[136,256]{1,0:T(8,128)S(1)}, f32[136,256]{1,0:T(8,128)S(1)}, u32[]{:S(2)}, u32[]{:S(2)}) collective-permute-start(f32[136,256]{1,0:T(8,128)S(1)} %slice.71), channel_id=1, source_target_pairs={{0,4},{1,3},{2,6},{3,1},{4,0},{5,7},{6,2},{7,5},{8,12},{9,11},{10,... | collective-permute-start | bytes 417800 | tf_op jit(solution)/shard_map/ppermute | solution.py:471
  35.1 1.6 %collective-permute-done.6 = f32[256,256]{1,0:T(8,128)S(1)} collective-permute-done((f32[256,256]{1,0:T(8,128)S(1)}, f32[256,256]{1,0:T(8,128)S(1)}, u32[]{:S(2)}, u32[]{:S(2)}) %collective-permute-start.6) | collective-permute-done | bytes 262176 | tf_op jit(solution)/shard_map/ppermute | solution.py:471
  36.8 0.1 fusion.1
  36.9 0.8 %collective-permute-start.7 = (f32[128,256]{1,0:T(8,128)S(1)}, f32[128,256]{1,0:T(8,128)S(1)}, u32[]{:S(2)}, u32[]{:S(2)}) collective-permute-start(f32[128,256]{1,0:T(8,128)S(1)} %slice.64), channel_id=1, source_target_pairs={{0,4},{1,3},{2,6},{3,1},{4,0},{5,7},{6,2},{7,5},{8,12},{9,11},{10,... | collective-permute-start | bytes 393224 | tf_op jit(solution)/shard_map/ppermute | solution.py:471
  37.7 1.7 %collective-permute-done.10 = f32[136,256]{1,0:T(8,128)S(1)} collective-permute-done((f32[136,256]{1,0:T(8,128)S(1)}, f32[136,256]{1,0:T(8,128)S(1)}, u32[]{:S(2)}, u32[]{:S(2)}) %collective-permute-start.10) | collective-permute-done | bytes 139296 | tf_op jit(solution)/shard_map/ppermute | solution.py:471
  39.5 2.0 %collective-permute-start.11 = (f32[72,256]{1,0:T(8,128)S(1)}, f32[72,256]{1,0:T(8,128)S(1)}, u32[]{:S(2)}, u32[]{:S(2)}) collective-permute-start(f32[72,256]{1,0:T(8,128)S(1)} %slice.74), channel_id=1, source_target_pairs={{0,8},{1,9},{2,10},{3,11},{4,12},{5,13},{6,14},{7,15},{8,0},{9,1},... | collective-permute-start | bytes 221192 | tf_op jit(solution)/shard_map/ppermute | solution.py:471
  41.5 0.8 %collective-permute-done.7 = f32[128,256]{1,0:T(8,128)S(1)} collective-permute-done((f32[128,256]{1,0:T(8,128)S(1)}, f32[128,256]{1,0:T(8,128)S(1)}, u32[]{:S(2)}, u32[]{:S(2)}) %collective-permute-start.7) | collective-permute-done | bytes 131104 | tf_op jit(solution)/shard_map/ppermute | solution.py:471
  42.3 2.7 %collective-permute-start.8 = (f32[64,256]{1,0:T(8,128)S(1)}, f32[64,256]{1,0:T(8,128)S(1)}, u32[]{:S(2)}, u32[]{:S(2)}) collective-permute-start(f32[64,256]{1,0:T(8,128)S(1)} %get-tuple-element.61), channel_id=1, source_target_pairs={{0,8},{1,9},{2,10},{3,11},{4,12},{5,13},{6,14},{7,15},{8,0},{9,1},... | collective-permute-start | bytes 196616 | tf_op jit(solution)/shard_map/ppermute | solution.py:471
  45.0 1.5 %collective-permute-done.11.got_ref = f32[72,256]{1,0:T(8,128)S(1)} collective-permute-done((f32[72,256]{1,0:T(8,128)S(1)}, f32[72,256]{1,0:T(8,128)S(1)}, u32[]{:S(2)}, u32[]{:S(2)}) %collective-permute-start.11) | collective-permute-done | bytes 73760 | tf_op jit(solution)/shard_map/ppermute | solution.py:471
  46.5 0.3 finish_first.1
  46.8 1.3 %collective-permute-done.8.got_ref = f32[64,256]{1,0:T(8,128)S(1)} collective-permute-done((f32[64,256]{1,0:T(8,128)S(1)}, f32[64,256]{1,0:T(8,128)S(1)}, u32[]{:S(2)}, u32[]{:S(2)}) %collective-permute-start.8) | collective-permute-done | bytes 65568 | tf_op jit(solution)/shard_map/ppermute | solution.py:471
  48.1 1.0 %finish_second.1 = f32[64,512]{1,0:T(8,128)} custom-call(f32[64,256]{1,0:T(8,128)S(1)} %get-tuple-element.62.mine_ref, f32[64,256]{1,0:T(8,128)S(1)} %collective-permute-done.8.got_ref, f32[64,512]{1,0:T(8,128)S(1)} %get-tuple-element.59.first_ref, f32[64,128]{1,0:T(8,128)S(1)} %get-tuple-element.60.norm_ref, bf16[512,512]{1,0:T(8,128)(2,1)S(1)} %get-tuple-element.58.sel_q_ref), custom_call_target="tpu_custom_call" | custom-call | tf_op jit(solution)/shard_map/finish_second/pallas_call | solution.py:442
  (19 shorter events, 0.2 us)
Async XLA Ops:
  1.1 2.6 %collective-permute-start = (f32[1,128]{1,0:T(1,128)S(1)}, f32[1,128]{1,0:T(1,128)S(1)}, u32[]{:S(2)}, u32[]{:S(2)}) collective-permute-start(f32[1,128]{1,0:T(1,128)S(1)} %get-tuple-element.33.refs_0_), channel_id=1, source_target_pairs={{0,1},{1,0},{2,3},{3,2},{4,5},{5,4},{6,7},{7,6},{8,9},{9,8},{10,11... | collective-permute-start | bytes 1544 | tf_op jit(solution)/shard_map/ppermute | solution.py:475
  3.8 5.2 %collective-permute-start.1 = (f32[1,128]{1,0:T(1,128)S(1)}, f32[1,128]{1,0:T(1,128)S(1)}, u32[]{:S(2)}, u32[]{:S(2)}) collective-permute-start(f32[1,128]{1,0:T(1,128)S(1)} %add.36.after_ref), channel_id=1, source_target_pairs={{0,2},{1,3},{2,0},{3,1},{4,6},{5,7},{6,4},{7,5},{8,10},{9,11},{10,... | collective-permute-start | bytes 1544 | tf_op jit(solution)/shard_map/ppermute | solution.py:475
  9.0 4.3 %collective-permute-start.2 = (f32[1,128]{1,0:T(1,128)S(1)}, f32[1,128]{1,0:T(1,128)S(1)}, u32[]{:S(2)}, u32[]{:S(2)}) collective-permute-start(f32[1,128]{1,0:T(1,128)S(1)} %add.37.after_ref), channel_id=1, source_target_pairs={{0,4},{1,5},{2,6},{3,7},{4,0},{5,1},{6,2},{7,3},{8,12},{9,13},{10,... | collective-permute-start | bytes 1544 | tf_op jit(solution)/shard_map/ppermute | solution.py:475
  13.3 5.1 %collective-permute-start.3 = (f32[1,128]{1,0:T(1,128)S(1)}, f32[1,128]{1,0:T(1,128)S(1)}, u32[]{:S(2)}, u32[]{:S(2)}) collective-permute-start(f32[1,128]{1,0:T(1,128)S(1)} %add.38.after_ref), channel_id=1, source_target_pairs={{0,8},{1,9},{2,10},{3,11},{4,12},{5,13},{6,14},{7,15},{8,0},{9,1},... | collective-permute-start | bytes 1544 | tf_op jit(solution)/shard_map/ppermute | solution.py:475
  22.7 2.0 %collective-permute-start.4 = (f32[520,256]{1,0:T(8,128)S(1)}, f32[520,256]{1,0:T(8,128)S(1)}, u32[]{:S(2)}, u32[]{:S(2)}) collective-permute-start(f32[520,256]{1,0:T(8,128)S(1)} %get-tuple-element.51.refs_0_.after_ref), channel_id=1, source_target_pairs={{0,1},{1,0},{2,3},{3,2},{4,5},{5,4},{6,7},{7,6},{8,9},{9,8},{10,11... | collective-permute-start | bytes 1597448 | tf_op jit(solution)/shard_map/ppermute | solution.py:471
  26.7 2.1 %collective-permute-start.5 = (f32[512,256]{1,0:T(8,128)S(1)}, f32[512,256]{1,0:T(8,128)S(1)}, u32[]{:S(2)}, u32[]{:S(2)}) collective-permute-start(f32[512,256]{1,0:T(8,128)S(1)} %get-tuple-element.56.refs_0_), channel_id=1, source_target_pairs={{0,1},{1,0},{2,3},{3,2},{4,5},{5,4},{6,7},{7,6},{8,9},{9,8},{10,11... | collective-permute-start | bytes 1572872 | tf_op jit(solution)/shard_map/ppermute | solution.py:471
  27.2 6.5 %collective-permute-start.9 = (f32[264,256]{1,0:T(8,128)S(1)}, f32[264,256]{1,0:T(8,128)S(1)}, u32[]{:S(2)}, u32[]{:S(2)}) collective-permute-start(f32[264,256]{1,0:T(8,128)S(1)} %slice_add_fusion.after_ref), channel_id=1, source_target_pairs={{0,2},{1,5},{2,0},{3,7},{4,6},{5,1},{6,4},{7,3},{8,10},{9,13},{10,... | collective-permute-start | bytes 811016 | tf_op jit(solution)/shard_map/ppermute | solution.py:471
  28.8 8.0 %collective-permute-start.6 = (f32[256,256]{1,0:T(8,128)S(1)}, f32[256,256]{1,0:T(8,128)S(1)}, u32[]{:S(2)}, u32[]{:S(2)}) collective-permute-start(f32[256,256]{1,0:T(8,128)S(1)} %slice_add_fusion.2.refs_0_), channel_id=1, source_target_pairs={{0,2},{1,5},{2,0},{3,7},{4,6},{5,1},{6,4},{7,3},{8,10},{9,13},{10,... | collective-permute-start | bytes 786440 | tf_op jit(solution)/shard_map/ppermute | solution.py:471
  34.3 5.1 %collective-permute-start.10 = (f32[136,256]{1,0:T(8,128)S(1)}, f32[136,256]{1,0:T(8,128)S(1)}, u32[]{:S(2)}, u32[]{:S(2)}) collective-permute-start(f32[136,256]{1,0:T(8,128)S(1)} %slice.71), channel_id=1, source_target_pairs={{0,4},{1,3},{2,6},{3,1},{4,0},{5,7},{6,2},{7,5},{8,12},{9,11},{10,... | collective-permute-start | bytes 417800 | tf_op jit(solution)/shard_map/ppermute | solution.py:471
  36.9 5.4 %collective-permute-start.7 = (f32[128,256]{1,0:T(8,128)S(1)}, f32[128,256]{1,0:T(8,128)S(1)}, u32[]{:S(2)}, u32[]{:S(2)}) collective-permute-start(f32[128,256]{1,0:T(8,128)S(1)} %slice.64), channel_id=1, source_target_pairs={{0,4},{1,3},{2,6},{3,1},{4,0},{5,7},{6,2},{7,5},{8,12},{9,11},{10,... | collective-permute-start | bytes 393224 | tf_op jit(solution)/shard_map/ppermute | solution.py:471
  39.5 7.0 %collective-permute-start.11 = (f32[72,256]{1,0:T(8,128)S(1)}, f32[72,256]{1,0:T(8,128)S(1)}, u32[]{:S(2)}, u32[]{:S(2)}) collective-permute-start(f32[72,256]{1,0:T(8,128)S(1)} %slice.74), channel_id=1, source_target_pairs={{0,8},{1,9},{2,10},{3,11},{4,12},{5,13},{6,14},{7,15},{8,0},{9,1},... | collective-permute-start | bytes 221192 | tf_op jit(solution)/shard_map/ppermute | solution.py:471
  42.3 5.8 %collective-permute-start.8 = (f32[64,256]{1,0:T(8,128)S(1)}, f32[64,256]{1,0:T(8,128)S(1)}, u32[]{:S(2)}, u32[]{:S(2)}) collective-permute-start(f32[64,256]{1,0:T(8,128)S(1)} %get-tuple-element.61), channel_id=1, source_target_pairs={{0,8},{1,9},{2,10},{3,11},{4,12},{5,13},{6,14},{7,15},{8,0},{9,1},... | collective-permute-start | bytes 196616 | tf_op jit(solution)/shard_map/ppermute | solution.py:471

commit v6 on v5

--- a/solution.py
+++ b/solution.py
@@ -405,10 +405,8 @@
 
 def pick_queries(scaled, sel):
     hi = scaled.astype(BF16)
-    rest = scaled - hi.astype(F32)
-    mid = rest.astype(BF16)
-    low = (rest - mid.astype(F32)).astype(BF16)
-    return dot(hi, sel) + dot(mid, sel) + dot(low, sel)
+    low = (scaled - hi.astype(F32)).astype(BF16)
+    return dot(hi, sel) + dot(low, sel)
 
 
 def finish_first_kernel(mine_ref, got_ref, sel_t_ref, sel_q_ref, out_ref, norm_ref):
@@ -489,7 +487,7 @@
     xq, xt = query_pool.reshape(queries, -1), train_store.reshape(train, -1)
 
     half = train // 2
-    have_q, have_b = 32, 16
+    have_q, have_b = 32, 112
     smalls = (eigenvalues, tids, qids, inner, outer)
     eig_sum, eig_v, tids_v, qids_v, inner_v, outer_v, xq_part = kernel_call(
         functools.partial(sum_kernel, have_q, len(smalls)),

time: 49.3 us -> 49.3 us (level)
  no operation moved by 1% of the time
where the time goes in v6:
time: 49.3 us; the launch traced here: 49 us
  Pallas kernels  21.5 us (44%)
  starting transfers between devices  16.3 us (33%)
  waiting for transfers between devices  10.6 us (22%)
    pallas_call x13, Pallas kernels, kernel_call(): pl.pallas_call(body, out_shape=tuple((pltpu.VMEM(shape, dtype) for shape,...  20.6 us
    ppermute x8, waiting for transfers between devices, halving_step(): return lax.ppermute(x, 'layer', pairs)  10.6 us
    ppermute x8, starting transfers between devices, halving_step(): return lax.ppermute(x, 'layer', pairs)  8.85 us
    ppermute x4, starting transfers between devices, exchange(): return lax.ppermute(x, 'layer', [(i, i ^ bit) for i in range(devices)])  7.42 us
  transfers between devices with their start and end apart: 12, of which 7 were waited for; matrix products, arithmetic and copies ran while one was open for 1% of the time, Pallas kernels for 27%

profile of v6, /device:TPU:0, one launch (start us, length us, event | category | flops | bytes accessed | tf_op | source)
XLA Modules:
  0.0 49.0 jit_solution(16922481412524845968)
XLA Ops:
  0.0 1.1 %eig_sum.1 = (f32[1,128]{1,0:T(1,128)S(1)}, f32[1,4096]{1,0:T(1,128)S(1)}, s32[1,1024]{1,0:T(1,128)S(1)}, s32[1,512]{1,0:T(1,128)S(1)}, bf16[64,64]{1,0:T(8,128)...) custom-call(f32[1,4096]{1,0:T(1,128)} %refs_0_.1, s32[1,1024]{1,0:T(1,128)} %bitcast.13, ...), custom_call_target="tpu_custom_call" | custom-call | tf_op jit(solution)/shard_map/eig_sum/pallas_call | solution.py:87
  1.1 0.5 %collective-permute-start = (f32[1,128]{1,0:T(1,128)S(1)}, f32[1,128]{1,0:T(1,128)S(1)}, u32[]{:S(2)}, u32[]{:S(2)}) collective-permute-start(f32[1,128]{1,0:T(1,128)S(1)} %get-tuple-element.33.refs_0_), channel_id=1, source_target_pairs={{0,1},{1,0},{2,3},{3,2},{4,5},{5,4},{6,7},{7,6},{8,9},{9,8},{10,11... | collective-permute-start | bytes 1544 | tf_op jit(solution)/shard_map/ppermute | solution.py:473
  1.6 2.1 %prepare.1 = (bf16[1024,1024]{1,0:T(8,128)(2,1)S(1)}, bf16[512,512]{1,0:T(8,128)(2,1)S(1)}, f32[1,4096]{1,0:T(1,128)S(1)}, bf16[256,256]{1,0:T(8,128)(2,1)S(1)},...) custom-call(f32[1,128]{1,0:T(1,128)S(1)} %get-tuple-element.33.refs_, ...), custom_call_target="tpu_custom_call", output_to_operand_aliasing={{6}: (7, {})} | custom-call | tf_op jit(solution)/shard_map/prepare/pallas_call | solution.py:87
  3.7 0.0 collective-permute-done
  3.8 2.6 %collective-permute-start.1 = (f32[1,128]{1,0:T(1,128)S(1)}, f32[1,128]{1,0:T(1,128)S(1)}, u32[]{:S(2)}, u32[]{:S(2)}) collective-permute-start(f32[1,128]{1,0:T(1,128)S(1)} %add.36.after_ref), channel_id=1, source_target_pairs={{0,2},{1,3},{2,0},{3,1},{4,6},{5,7},{6,4},{7,5},{8,10},{9,11},{10,... | collective-permute-start | bytes 1544 | tf_op jit(solution)/shard_map/ppermute | solution.py:473
  6.4 2.6 %rotate_query.1 = (f32[512,4096]{1,0:T(8,128)S(1)}, bf16[512,4096]{1,0:T(8,128)(2,1)S(1)}, bf16[512,4096]{1,0:T(8,128)(2,1)S(1)}) custom-call(f32[1,128]{1,0:T(1,128)S(1)} %add.36.after_ref, bf16[512,4096]{1,0:T(8,128)(2,1)S(1)} %get-tuple-element.40.x_ref, bf16[256,256]{1,0:T(8,128)(2,1)S(1)} %get-tuple-element.41.w3_ref, ...), custom_call_target="tpu_custom_call" | custom-call | flops 1073741824 | tf_op jit(solution)/shard_map/rotate_query/pallas_call | solution.py:87
  9.0 0.0 collective-permute-done.1
  9.0 1.6 %collective-permute-start.2 = (f32[1,128]{1,0:T(1,128)S(1)}, f32[1,128]{1,0:T(1,128)S(1)}, u32[]{:S(2)}, u32[]{:S(2)}) collective-permute-start(f32[1,128]{1,0:T(1,128)S(1)} %add.37.after_ref), channel_id=1, source_target_pairs={{0,4},{1,5},{2,6},{3,7},{4,0},{5,1},{6,2},{7,3},{8,12},{9,13},{10,... | collective-permute-start | bytes 1544 | tf_op jit(solution)/shard_map/ppermute | solution.py:473
  10.7 2.6 %rotate_train.2 = (bf16[16,256,512]{2,1,0:T(8,128)(2,1)S(1)}, bf16[512,4096]{1,0:T(8,128)(2,1)S(1)}) custom-call(f32[1,128]{1,0:T(1,128)S(1)} %add.37.after_ref, bf16[512,4096]{1,0:T(8,128)(2,1)S(1)} %get-tuple-element.43.x_ref, bf16[256,256]{1,0:T(8,128)(2,1)S(1)} %get-tuple-element.41.w3_ref, ...), custom_call_target="tpu_custom_call", output_to_operand_aliasing={{1}: (5, {})} | custom-call | flops 2147483648 | tf_op jit(solution)/shard_map/rotate_train/pallas_call | solution.py:87
  13.3 0.0 collective-permute-done.2
  13.3 2.7 %collective-permute-start.3 = (f32[1,128]{1,0:T(1,128)S(1)}, f32[1,128]{1,0:T(1,128)S(1)}, u32[]{:S(2)}, u32[]{:S(2)}) collective-permute-start(f32[1,128]{1,0:T(1,128)S(1)} %add.38.after_ref), channel_id=1, source_target_pairs={{0,8},{1,9},{2,10},{3,11},{4,12},{5,13},{6,14},{7,15},{8,0},{9,1},... | collective-permute-start | bytes 1544 | tf_op jit(solution)/shard_map/ppermute | solution.py:473
  16.0 2.5 %rotate_train.3.rtb_ref.rt_ref = bf16[16,256,512]{2,1,0:T(8,128)(2,1)S(1)} custom-call(f32[1,128]{1,0:T(1,128)S(1)} %add.38.after_ref, bf16[512,4096]{1,0:T(8,128)(2,1)S(1)} %get-tuple-element.47.x_ref, bf16[256,256]{1,0:T(8,128)(2,1)S(1)} %get-tuple-element.41.w3_ref, bf16[256,256]{1,0:T(8,128)(2,1)S(1)} %get-tuple-element.44.w4_ref), custom_call_target="tpu_custom_call" | custom-call | flops 2147483648 | tf_op jit(solution)/shard_map/rotate_train/pallas_call | solution.py:87
  18.5 0.0 collective-permute-done.3
  18.5 4.2 %scores_self.1 = (f32[520,256]{1,0:T(8,128)S(1)}, bf16[2,256,1024]{2,1,0:T(8,128)(2,1)S(1)}, f32[8,256]{1,0:T(8,128)S(1)}) custom-call(bf16[16,256,512]{2,1,0:T(8,128)(2,1)S(1)} %get-tuple-element.46.rta_ref.rt_ref, bf16[16,256,512]{2,1,0:T(8,128)(2,1)S(1)} %rotate_train.3.rtb_ref.rt_ref, f32[512,4096]{1,0:T(8,128)S(1)} %get-tuple-element.48.turned_ref, ...), custom_call_target="tpu_custom_call" | custom-call | tf_op jit(solution)/shard_map/scores_self/pallas_call | solution.py:87
  22.7 0.1 collective-permute-start.4
  22.8 1.4 %scores_first.1 = (bf16[256,4096]{1,0:T(8,128)(2,1)S(1)}, bf16[2,256,512]{2,1,0:T(8,128)(2,1)S(1)}) custom-call(f32[520,256]{1,0:T(8,128)S(1)} %get-tuple-element.51.refs_0_.after_ref, bf16[16,256,512]{2,1,0:T(8,128)(2,1)S(1)} %get-tuple-element.46.rta_ref.rt_ref, f32[512,4096]{1,0:T(8,128)S(1)} %get-tuple-element.48.turned_ref, ...), custom_call_target="tpu_custom_call" | custom-call | tf_op jit(solution)/shard_map/scores_first/pallas_call | solution.py:87
  24.2 0.5 keep_first.2
  24.6 0.0 collective-permute-done.4
  24.7 2.0 %scores_second.1 = (f32[512,256]{1,0:T(8,128)S(1)}, bf16[2,256,512]{2,1,0:T(8,128)(2,1)S(1)}) custom-call(f32[264,256]{1,0:T(8,128)S(1)} %slice_add_fusion.after_ref, bf16[16,256,512]{2,1,0:T(8,128)(2,1)S(1)} %rotate_train.3.rtb_ref.rt_ref, bf16[256,4096]{1,0:T(8,128)(2,1)S(1)} %get-tuple-element.54.d_ref, ...), custom_call_target="tpu_custom_call" | custom-call | tf_op jit(solution)/shard_map/scores_second/pallas_call | solution.py:87
  26.7 0.6 %collective-permute-start.5 = (f32[512,256]{1,0:T(8,128)S(1)}, f32[512,256]{1,0:T(8,128)S(1)}, u32[]{:S(2)}, u32[]{:S(2)}) collective-permute-start(f32[512,256]{1,0:T(8,128)S(1)} %get-tuple-element.56.refs_0_), channel_id=1, source_target_pairs={{0,1},{1,0},{2,3},{3,2},{4,5},{5,4},{6,7},{7,6},{8,9},{9,8},{10,11... | collective-permute-start | bytes 1572872 | tf_op jit(solution)/shard_map/ppermute | solution.py:469
  27.2 0.8 %collective-permute-start.9 = (f32[264,256]{1,0:T(8,128)S(1)}, f32[264,256]{1,0:T(8,128)S(1)}, u32[]{:S(2)}, u32[]{:S(2)}) collective-permute-start(f32[264,256]{1,0:T(8,128)S(1)} %slice_add_fusion.after_ref), channel_id=1, source_target_pairs={{0,2},{1,5},{2,0},{3,7},{4,6},{5,1},{6,4},{7,3},{8,10},{9,13},{10,... | collective-permute-start | bytes 811016 | tf_op jit(solution)/shard_map/ppermute | solution.py:469
  28.1 0.5 keep_first.3
  28.5 0.2 collective-permute-done.5
  28.8 1.0 %collective-permute-start.6 = (f32[256,256]{1,0:T(8,128)S(1)}, f32[256,256]{1,0:T(8,128)S(1)}, u32[]{:S(2)}, u32[]{:S(2)}) collective-permute-start(f32[256,256]{1,0:T(8,128)S(1)} %slice_add_fusion.2.refs_0_), channel_id=1, source_target_pairs={{0,2},{1,5},{2,0},{3,7},{4,6},{5,1},{6,4},{7,3},{8,10},{9,13},{10,... | collective-permute-start | bytes 786440 | tf_op jit(solution)/shard_map/ppermute | solution.py:469
  29.9 0.5 keep_later.3
  30.4 3.3 %collective-permute-done.9 = f32[264,256]{1,0:T(8,128)S(1)} collective-permute-done((f32[264,256]{1,0:T(8,128)S(1)}, f32[264,256]{1,0:T(8,128)S(1)}, u32[]{:S(2)}, u32[]{:S(2)}) %collective-permute-start.9) | collective-permute-done | bytes 270368 | tf_op jit(solution)/shard_map/ppermute | solution.py:469
  33.7 0.1 fusion
  33.8 0.5 keep_later.2
  34.3 0.8 %collective-permute-start.10 = (f32[136,256]{1,0:T(8,128)S(1)}, f32[136,256]{1,0:T(8,128)S(1)}, u32[]{:S(2)}, u32[]{:S(2)}) collective-permute-start(f32[136,256]{1,0:T(8,128)S(1)} %slice.71), channel_id=1, source_target_pairs={{0,4},{1,3},{2,6},{3,1},{4,0},{5,7},{6,2},{7,5},{8,12},{9,11},{10,... | collective-permute-start | bytes 417800 | tf_op jit(solution)/shard_map/ppermute | solution.py:469
  35.1 1.6 %collective-permute-done.6 = f32[256,256]{1,0:T(8,128)S(1)} collective-permute-done((f32[256,256]{1,0:T(8,128)S(1)}, f32[256,256]{1,0:T(8,128)S(1)}, u32[]{:S(2)}, u32[]{:S(2)}) %collective-permute-start.6) | collective-permute-done | bytes 262176 | tf_op jit(solution)/shard_map/ppermute | solution.py:469
  36.8 0.1 fusion.1
  36.9 0.8 %collective-permute-start.7 = (f32[128,256]{1,0:T(8,128)S(1)}, f32[128,256]{1,0:T(8,128)S(1)}, u32[]{:S(2)}, u32[]{:S(2)}) collective-permute-start(f32[128,256]{1,0:T(8,128)S(1)} %slice.64), channel_id=1, source_target_pairs={{0,4},{1,3},{2,6},{3,1},{4,0},{5,7},{6,2},{7,5},{8,12},{9,11},{10,... | collective-permute-start | bytes 393224 | tf_op jit(solution)/shard_map/ppermute | solution.py:469
  37.7 1.7 %collective-permute-done.10 = f32[136,256]{1,0:T(8,128)S(1)} collective-permute-done((f32[136,256]{1,0:T(8,128)S(1)}, f32[136,256]{1,0:T(8,128)S(1)}, u32[]{:S(2)}, u32[]{:S(2)}) %collective-permute-start.10) | collective-permute-done | bytes 139296 | tf_op jit(solution)/shard_map/ppermute | solution.py:469
  39.5 2.0 %collective-permute-start.11 = (f32[72,256]{1,0:T(8,128)S(1)}, f32[72,256]{1,0:T(8,128)S(1)}, u32[]{:S(2)}, u32[]{:S(2)}) collective-permute-start(f32[72,256]{1,0:T(8,128)S(1)} %slice.74), channel_id=1, source_target_pairs={{0,8},{1,9},{2,10},{3,11},{4,12},{5,13},{6,14},{7,15},{8,0},{9,1},... | collective-permute-start | bytes 221192 | tf_op jit(solution)/shard_map/ppermute | solution.py:469
  41.5 0.8 %collective-permute-done.7 = f32[128,256]{1,0:T(8,128)S(1)} collective-permute-done((f32[128,256]{1,0:T(8,128)S(1)}, f32[128,256]{1,0:T(8,128)S(1)}, u32[]{:S(2)}, u32[]{:S(2)}) %collective-permute-start.7) | collective-permute-done | bytes 131104 | tf_op jit(solution)/shard_map/ppermute | solution.py:469
  42.3 2.7 %collective-permute-start.8 = (f32[64,256]{1,0:T(8,128)S(1)}, f32[64,256]{1,0:T(8,128)S(1)}, u32[]{:S(2)}, u32[]{:S(2)}) collective-permute-start(f32[64,256]{1,0:T(8,128)S(1)} %get-tuple-element.61), channel_id=1, source_target_pairs={{0,8},{1,9},{2,10},{3,11},{4,12},{5,13},{6,14},{7,15},{8,0},{9,1},... | collective-permute-start | bytes 196616 | tf_op jit(solution)/shard_map/ppermute | solution.py:469
  45.0 1.5 %collective-permute-done.11.got_ref = f32[72,256]{1,0:T(8,128)S(1)} collective-permute-done((f32[72,256]{1,0:T(8,128)S(1)}, f32[72,256]{1,0:T(8,128)S(1)}, u32[]{:S(2)}, u32[]{:S(2)}) %collective-permute-start.11) | collective-permute-done | bytes 73760 | tf_op jit(solution)/shard_map/ppermute | solution.py:469
  46.5 0.3 finish_first.1
  46.8 1.3 %collective-permute-done.8.got_ref = f32[64,256]{1,0:T(8,128)S(1)} collective-permute-done((f32[64,256]{1,0:T(8,128)S(1)}, f32[64,256]{1,0:T(8,128)S(1)}, u32[]{:S(2)}, u32[]{:S(2)}) %collective-permute-start.8) | collective-permute-done | bytes 65568 | tf_op jit(solution)/shard_map/ppermute | solution.py:469
  48.1 0.9 %finish_second.1 = f32[64,512]{1,0:T(8,128)} custom-call(f32[64,256]{1,0:T(8,128)S(1)} %get-tuple-element.62.mine_ref, f32[64,256]{1,0:T(8,128)S(1)} %collective-permute-done.8.got_ref, f32[64,512]{1,0:T(8,128)S(1)} %get-tuple-element.59.first_ref, f32[64,128]{1,0:T(8,128)S(1)} %get-tuple-element.60.norm_ref, bf16[512,512]{1,0:T(8,128)(2,1)S(1)} %get-tuple-element.58.sel_q_ref), custom_call_target="tpu_custom_call" | custom-call | tf_op jit(solution)/shard_map/finish_second/pallas_call | solution.py:440
  (19 shorter events, 0.2 us)
Async XLA Ops:
  1.1 2.6 %collective-permute-start = (f32[1,128]{1,0:T(1,128)S(1)}, f32[1,128]{1,0:T(1,128)S(1)}, u32[]{:S(2)}, u32[]{:S(2)}) collective-permute-start(f32[1,128]{1,0:T(1,128)S(1)} %get-tuple-element.33.refs_0_), channel_id=1, source_target_pairs={{0,1},{1,0},{2,3},{3,2},{4,5},{5,4},{6,7},{7,6},{8,9},{9,8},{10,11... | collective-permute-start | bytes 1544 | tf_op jit(solution)/shard_map/ppermute | solution.py:473
  3.8 5.2 %collective-permute-start.1 = (f32[1,128]{1,0:T(1,128)S(1)}, f32[1,128]{1,0:T(1,128)S(1)}, u32[]{:S(2)}, u32[]{:S(2)}) collective-permute-start(f32[1,128]{1,0:T(1,128)S(1)} %add.36.after_ref), channel_id=1, source_target_pairs={{0,2},{1,3},{2,0},{3,1},{4,6},{5,7},{6,4},{7,5},{8,10},{9,11},{10,... | collective-permute-start | bytes 1544 | tf_op jit(solution)/shard_map/ppermute | solution.py:473
  9.0 4.3 %collective-permute-start.2 = (f32[1,128]{1,0:T(1,128)S(1)}, f32[1,128]{1,0:T(1,128)S(1)}, u32[]{:S(2)}, u32[]{:S(2)}) collective-permute-start(f32[1,128]{1,0:T(1,128)S(1)} %add.37.after_ref), channel_id=1, source_target_pairs={{0,4},{1,5},{2,6},{3,7},{4,0},{5,1},{6,2},{7,3},{8,12},{9,13},{10,... | collective-permute-start | bytes 1544 | tf_op jit(solution)/shard_map/ppermute | solution.py:473
  13.3 5.1 %collective-permute-start.3 = (f32[1,128]{1,0:T(1,128)S(1)}, f32[1,128]{1,0:T(1,128)S(1)}, u32[]{:S(2)}, u32[]{:S(2)}) collective-permute-start(f32[1,128]{1,0:T(1,128)S(1)} %add.38.after_ref), channel_id=1, source_target_pairs={{0,8},{1,9},{2,10},{3,11},{4,12},{5,13},{6,14},{7,15},{8,0},{9,1},... | collective-permute-start | bytes 1544 | tf_op jit(solution)/shard_map/ppermute | solution.py:473
  22.7 2.0 %collective-permute-start.4 = (f32[520,256]{1,0:T(8,128)S(1)}, f32[520,256]{1,0:T(8,128)S(1)}, u32[]{:S(2)}, u32[]{:S(2)}) collective-permute-start(f32[520,256]{1,0:T(8,128)S(1)} %get-tuple-element.51.refs_0_.after_ref), channel_id=1, source_target_pairs={{0,1},{1,0},{2,3},{3,2},{4,5},{5,4},{6,7},{7,6},{8,9},{9,8},{10,11... | collective-permute-start | bytes 1597448 | tf_op jit(solution)/shard_map/ppermute | solution.py:469
  26.7 2.1 %collective-permute-start.5 = (f32[512,256]{1,0:T(8,128)S(1)}, f32[512,256]{1,0:T(8,128)S(1)}, u32[]{:S(2)}, u32[]{:S(2)}) collective-permute-start(f32[512,256]{1,0:T(8,128)S(1)} %get-tuple-element.56.refs_0_), channel_id=1, source_target_pairs={{0,1},{1,0},{2,3},{3,2},{4,5},{5,4},{6,7},{7,6},{8,9},{9,8},{10,11... | collective-permute-start | bytes 1572872 | tf_op jit(solution)/shard_map/ppermute | solution.py:469
  27.2 6.5 %collective-permute-start.9 = (f32[264,256]{1,0:T(8,128)S(1)}, f32[264,256]{1,0:T(8,128)S(1)}, u32[]{:S(2)}, u32[]{:S(2)}) collective-permute-start(f32[264,256]{1,0:T(8,128)S(1)} %slice_add_fusion.after_ref), channel_id=1, source_target_pairs={{0,2},{1,5},{2,0},{3,7},{4,6},{5,1},{6,4},{7,3},{8,10},{9,13},{10,... | collective-permute-start | bytes 811016 | tf_op jit(solution)/shard_map/ppermute | solution.py:469
  28.8 8.0 %collective-permute-start.6 = (f32[256,256]{1,0:T(8,128)S(1)}, f32[256,256]{1,0:T(8,128)S(1)}, u32[]{:S(2)}, u32[]{:S(2)}) collective-permute-start(f32[256,256]{1,0:T(8,128)S(1)} %slice_add_fusion.2.refs_0_), channel_id=1, source_target_pairs={{0,2},{1,5},{2,0},{3,7},{4,6},{5,1},{6,4},{7,3},{8,10},{9,13},{10,... | collective-permute-start | bytes 786440 | tf_op jit(solution)/shard_map/ppermute | solution.py:469
  34.3 5.1 %collective-permute-start.10 = (f32[136,256]{1,0:T(8,128)S(1)}, f32[136,256]{1,0:T(8,128)S(1)}, u32[]{:S(2)}, u32[]{:S(2)}) collective-permute-start(f32[136,256]{1,0:T(8,128)S(1)} %slice.71), channel_id=1, source_target_pairs={{0,4},{1,3},{2,6},{3,1},{4,0},{5,7},{6,2},{7,5},{8,12},{9,11},{10,... | collective-permute-start | bytes 417800 | tf_op jit(solution)/shard_map/ppermute | solution.py:469
  36.9 5.4 %collective-permute-start.7 = (f32[128,256]{1,0:T(8,128)S(1)}, f32[128,256]{1,0:T(8,128)S(1)}, u32[]{:S(2)}, u32[]{:S(2)}) collective-permute-start(f32[128,256]{1,0:T(8,128)S(1)} %slice.64), channel_id=1, source_target_pairs={{0,4},{1,3},{2,6},{3,1},{4,0},{5,7},{6,2},{7,5},{8,12},{9,11},{10,... | collective-permute-start | bytes 393224 | tf_op jit(solution)/shard_map/ppermute | solution.py:469
  39.5 7.0 %collective-permute-start.11 = (f32[72,256]{1,0:T(8,128)S(1)}, f32[72,256]{1,0:T(8,128)S(1)}, u32[]{:S(2)}, u32[]{:S(2)}) collective-permute-start(f32[72,256]{1,0:T(8,128)S(1)} %slice.74), channel_id=1, source_target_pairs={{0,8},{1,9},{2,10},{3,11},{4,12},{5,13},{6,14},{7,15},{8,0},{9,1},... | collective-permute-start | bytes 221192 | tf_op jit(solution)/shard_map/ppermute | solution.py:469
  42.3 5.8 %collective-permute-start.8 = (f32[64,256]{1,0:T(8,128)S(1)}, f32[64,256]{1,0:T(8,128)S(1)}, u32[]{:S(2)}, u32[]{:S(2)}) collective-permute-start(f32[64,256]{1,0:T(8,128)S(1)} %get-tuple-element.61), channel_id=1, source_target_pairs={{0,8},{1,9},{2,10},{3,11},{4,12},{5,13},{6,14},{7,15},{8,0},{9,1},... | collective-permute-start | bytes 196616 | tf_op jit(solution)/shard_map/ppermute | solution.py:469
